TPU v7x, 128 devices: a whole 4x4x4 slice. The times are simulated.
128 devices in a mesh: outer: 8 (over y, core), inner: 16 (over z, x).
Axes of the slice: x: 4, y: 4, z: 4, core: 2. Of those that a mesh axis runs over, the one named last changes fastest.
Arguments:
- points: bfloat16 [262144, 2048], P(('outer', 'inner')), may hold values from -6 to 6
- leaf_order: int32 [128, 2048], P(('outer', 'inner')), may hold values from 0 to 2047, each once within a row
- diag_blocks: bfloat16 [128, 2048, 2048], P(('outer', 'inner')), may hold values from -0.125 to 0.125
- leaf_basis: bfloat16 [128, 2048, 256], P(('outer', 'inner')), may hold values from -0.125 to 0.125
- leaf_nodes: bfloat16 [128, 2, 256, 256], P(('outer', 'inner')), may hold values from -1.5 to 1.5
- inner_nodes: bfloat16 [8, 15, 2, 256, 256], P('outer'), may hold values from -1.5 to 1.5
- outer_nodes: bfloat16 [6, 2, 256, 256], replicated, may hold values from -1.5 to 1.5
- root_coupling: bfloat16 [256, 256], replicated, may hold values from -1.5 to 1.5
- node_ranks: int32 [255], replicated, may hold values from 64 to 256
Outputs:
- product: bfloat16 [262144, 2048], P(('outer', 'inner'))
Inputs may be any that keep to these rules, and one draw needn't show every extreme that they name: `leaf_order`: each row is a permutation of the positions 0 to 2047 within the leaf's block.
All inputs are finite; a program needn't handle non-finite values.
Results may differ from a plain program's by a relative error of at most 0.017.
Values may be sent and summed in bfloat16 or wider, within the bound.
No kernel may reach another device: no remote copies, remote signals or barrier semaphores. Data moves between devices by JAX's collectives and lax.ppermute only.
A program may use at most 256 MiB of HBM per device.

v0:
```python
import jax
import jax.numpy as jnp
from jax import lax
from jax.sharding import PartitionSpec as P


def swapped(block, axis, apart):
    count = lax.axis_size(axis)
    route = []
    for low in range(count):
        high = low | 1 << apart
        if high != low and high < count:
            route += [(low, high), (high, low)]
    return lax.ppermute(block, axis, route)


def column_mask(node_ranks, heap_id, rank_width):
    limit = node_ranks[heap_id]
    return (jnp.arange(rank_width, dtype=jnp.int32)[:, None] < limit).astype(jnp.float32)


def body(
    points,
    leaf_order,
    diag_blocks,
    leaf_basis,
    leaf_nodes,
    inner_nodes,
    outer_nodes,
    root_coupling,
    node_ranks,
):
    count_inner = lax.axis_size("inner")
    count_outer = lax.axis_size("outer")
    depth_inner = count_inner.bit_length() - 1
    depth_outer = count_outer.bit_length() - 1
    depth_total = depth_inner + depth_outer
    leaf_count = count_inner * count_outer
    inner_pos = lax.axis_index("inner")
    outer_pos = lax.axis_index("outer")
    leaf_id = outer_pos * count_inner + inner_pos
    rank_width = leaf_basis.shape[2]

    def own_mask(height):
        heap_id = (leaf_count >> height) - 1 + (leaf_id >> height)
        return column_mask(node_ranks, heap_id, rank_width)

    def inner_node(height, position):
        first_node = count_inner - (count_inner >> height - 1)
        return lax.dynamic_index_in_dim(inner_nodes[0], first_node + position, 0, keepdims=False)

    def outer_node(segment, position):
        first_node = count_outer - (count_outer >> segment - 1)
        return lax.dynamic_index_in_dim(outer_nodes, first_node + position, 0, keepdims=False)

    def own_pair(height):
        if height == 0:
            return leaf_nodes[0]
        if height <= depth_inner:
            return inner_node(height, inner_pos >> height)
        segment = height - depth_inner
        return outer_node(segment, outer_pos >> segment)

    positions = leaf_order[0]
    ordered = points[positions]
    near = jnp.dot(diag_blocks[0], ordered, preferred_element_type=jnp.float32)
    basis = leaf_basis[0]
    base = jnp.dot(basis.T, ordered, preferred_element_type=jnp.float32)
    coef = (base * own_mask(0)).astype(jnp.bfloat16)
    leaf_transfer = leaf_nodes[0, 0]
    sibling_coefs = []
    peer_coef, peer_transfer = swapped((coef, leaf_transfer), "inner", 0)
    sibling_coefs.append(peer_coef)
    upward = jnp.dot(leaf_transfer.T, coef, preferred_element_type=jnp.float32)
    upward = upward + jnp.dot(peer_transfer.T, peer_coef, preferred_element_type=jnp.float32)
    coef = (upward * own_mask(1)).astype(jnp.bfloat16)
    for height in range(1, depth_inner):
        peer_coef = swapped(coef, "inner", height)
        sibling_coefs.append(peer_coef)
        own_transfer = inner_node(height, inner_pos >> height)[0]
        peer_transfer = inner_node(height, inner_pos >> height ^ 1)[0]
        upward = jnp.dot(own_transfer.T, coef, preferred_element_type=jnp.float32)
        upward = upward + jnp.dot(peer_transfer.T, peer_coef, preferred_element_type=jnp.float32)
        coef = (upward * own_mask(height + 1)).astype(jnp.bfloat16)
    group_transfer = inner_nodes[0, count_inner - 2, 0]
    peer_coef, peer_transfer = swapped((coef, group_transfer), "outer", 0)
    sibling_coefs.append(peer_coef)
    upward = jnp.dot(group_transfer.T, coef, preferred_element_type=jnp.float32)
    upward = upward + jnp.dot(peer_transfer.T, peer_coef, preferred_element_type=jnp.float32)
    coef = (upward * own_mask(depth_inner + 1)).astype(jnp.bfloat16)
    for segment in range(1, depth_outer):
        peer_coef = swapped(coef, "outer", segment)
        sibling_coefs.append(peer_coef)
        own_transfer = outer_node(segment, outer_pos >> segment)[0]
        peer_transfer = outer_node(segment, outer_pos >> segment ^ 1)[0]
        upward = jnp.dot(own_transfer.T, coef, preferred_element_type=jnp.float32)
        upward = upward + jnp.dot(peer_transfer.T, peer_coef, preferred_element_type=jnp.float32)
        coef = (upward * own_mask(depth_inner + segment + 1)).astype(jnp.bfloat16)
    top = jnp.dot(root_coupling, coef, preferred_element_type=jnp.float32)
    far_coef = (top * own_mask(depth_total)).astype(jnp.bfloat16)
    for height in reversed(range(depth_total)):
        node_pair = own_pair(height)
        summed = jnp.dot(node_pair[1], sibling_coefs[height], preferred_element_type=jnp.float32)
        summed = summed + jnp.dot(node_pair[0], far_coef, preferred_element_type=jnp.float32)
        far_coef = (summed * own_mask(height)).astype(jnp.bfloat16)
    values = (near + jnp.dot(basis, far_coef, preferred_element_type=jnp.float32)).astype(
        jnp.bfloat16
    )
    return jnp.zeros_like(values).at[positions].set(values)


def solution(mesh):
    in_specs = (
        P(("outer", "inner"), None),
        P(("outer", "inner"), None),
        P(("outer", "inner"), None, None),
        P(("outer", "inner"), None, None),
        P(("outer", "inner"), None, None, None),
        P("outer", None, None, None, None),
        P(),
        P(),
        P(),
    )
    out_specs = P(("outer", "inner"), None)
    return jax.shard_map(body, mesh=mesh, in_specs=in_specs, out_specs=out_specs, check_vma=False)
```

profile of v0, /device:TPU:0, one launch (start us, length us, event | category | flops | bytes accessed | tf_op | source)
XLA Modules:
  0.0 275.8 jit_solution(11047795217686066261)
XLA Ops:
  0.0 1.7 fusion.86
  1.7 0.7 compare_convert_fusion.7
  2.3 0.7 compare_select_fusion
  3.1 20.9 %gather_fusion = bf16[2048,2048]{1,0:T(8,128)(2,1)} fusion(bf16[2048,2048]{1,0:T(8,128)(2,1)} %param.9, s32[2048]{0:T(1024)S(1)} %broadcast_clamp_fusion), kind=kCustom, calls=%fused_computation | custom fusion | bytes 16785408 | tf_op jit(solution)/shard_map/gather | solution.py:65
  23.9 5.9 %fusion.33 = bf16[2048,256]{1,0:T(8,128)(2,1)S(1)} fusion(bf16[2048,2048]{1,0:T(8,128)(2,1)} %gather_fusion, bf16[1,2048,256]{2,1,0:T(8,128)(2,1)S(1)} %copy-done.3, f32[256]{0:T(256)S(1)} %compare_convert_fusion.7), kind=kOutput, calls=%fused_computation.52 | convolution fusion | flops 2148532224 | bytes 10486784 | tf_op jit(solution)/shard_map/dot_general | solution.py:68
  29.9 1.7 collective-permute-start
  32.5 0.6 compare_convert_fusion.6
  33.1 24.4 %collective-permute-done.1 = bf16[256,256]{1,0:T(8,128)(2,1)S(1)} collective-permute-done((bf16[256,256]{1,0:T(8,128)(2,1)S(1)}, bf16[256,256]{1,0:T(8,128)(2,1)S(1)}, u32[]{:S(2)}, u32[]{:S(2)}) %collective-permute-start.1) | collective-permute-done | bytes 131104 | tf_op jit(solution)/shard_map/ppermute | solution.py:14
  57.5 1.4 fusion.20
  58.9 3.3 %collective-permute-start.2 = (bf16[256,2048]{0,1:T(8,128)(2,1)}, bf16[256,2048]{0,1:T(8,128)(2,1)}, u32[]{:S(2)}, u32[]{:S(2)}) collective-permute-start(bf16[256,2048]{0,1:T(8,128)(2,1)} %bitcast.10), channel_id=1, source_target_pairs={{0,2},{2,0},{1,3},{3,1},{4,6},{6,4},{5,7},{7,5},{8,10},{10,8},{9,1... | collective-permute-start | bytes 3145736 | tf_op jit(solution)/shard_map/ppermute | solution.py:14
  62.2 0.7 compare_convert_fusion.5
  62.9 1.8 fusion.56
  64.7 20.1 %collective-permute-done.2 = bf16[256,2048]{0,1:T(8,128)(2,1)} collective-permute-done((bf16[256,2048]{0,1:T(8,128)(2,1)}, bf16[256,2048]{0,1:T(8,128)(2,1)}, u32[]{:S(2)}, u32[]{:S(2)}) %collective-permute-start.2) | collective-permute-done | bytes 1048608 | tf_op jit(solution)/shard_map/ppermute | solution.py:14
  84.8 2.9 %fusion.22 = bf16[256,2048]{1,0:T(8,128)(2,1)} fusion(f32[256,2048]{1,0:T(8,128)S(1)} %fusion.56, bf16[256,2048]{0,1:T(8,128)(2,1)} %collective-permute-done.2, f32[256]{0:T(256)S(1)} %compare_convert_fusion.5, bf16[1,15,2,256,256]{4,3,2,1,0:T(8,128)(2,1)} %param.14, s32[]{:T(128)S(6)} %select_n.88), kind=kOutput, calls=%fused_computation.41 | convolution fusion | flops 270008320 | bytes 4326404 | tf_op jit(solution)/shard_map/dot_general | solution.py:83
  87.7 2.2 collective-permute-start.3
  90.4 1.8 fusion.57
  92.2 19.4 %collective-permute-done.3 = bf16[256,2048]{1,0:T(8,128)(2,1)} collective-permute-done((bf16[256,2048]{1,0:T(8,128)(2,1)}, bf16[256,2048]{1,0:T(8,128)(2,1)}, u32[]{:S(2)}, u32[]{:S(2)}) %collective-permute-start.3) | collective-permute-done | bytes 1048608 | tf_op jit(solution)/shard_map/ppermute | solution.py:14
  111.6 2.8 fusion.24
  114.3 3.7 %collective-permute-start.4 = (bf16[256,2048]{1,0:T(8,128)(2,1)}, bf16[256,2048]{1,0:T(8,128)(2,1)}, u32[]{:S(2)}, u32[]{:S(2)}) collective-permute-start(bf16[256,2048]{1,0:T(8,128)(2,1)} %fusion.24), channel_id=1, source_target_pairs={{0,8},{8,0},{1,9},{9,1},{2,10},{10,2},{3,11},{11,3},{4,12},{12,4},... | collective-permute-start | bytes 3145736 | tf_op jit(solution)/shard_map/ppermute | solution.py:14
  118.0 0.6 compare_convert_fusion.3
  118.6 1.8 fusion.58
  120.4 18.3 %collective-permute-done.4 = bf16[256,2048]{1,0:T(8,128)(2,1)} collective-permute-done((bf16[256,2048]{1,0:T(8,128)(2,1)}, bf16[256,2048]{1,0:T(8,128)(2,1)}, u32[]{:S(2)}, u32[]{:S(2)}) %collective-permute-start.4) | collective-permute-done | bytes 1048608 | tf_op jit(solution)/shard_map/ppermute | solution.py:14
  138.7 1.8 fusion.26
  140.6 0.9 slice_bitcast_fusion
  141.5 0.6 collective-permute-start.6
  142.1 0.6 compare_convert_fusion.2
  142.7 1.4 fusion.84
  144.2 1.5 fusion.28
  145.6 1.6 collective-permute-start.7
  147.2 0.6 compare_convert_fusion.1
  147.8 1.7 fusion.59
  149.5 21.5 %collective-permute-done.7 = bf16[256,2048]{0,1:T(8,128)(2,1)} collective-permute-done((bf16[256,2048]{0,1:T(8,128)(2,1)}, bf16[256,2048]{0,1:T(8,128)(2,1)}, u32[]{:S(2)}, u32[]{:S(2)}) %collective-permute-start.7) | collective-permute-done | bytes 1048608 | tf_op jit(solution)/shard_map/ppermute | solution.py:14
  171.0 2.8 %fusion.30 = bf16[256,2048]{1,0:T(8,128)(2,1)} fusion(f32[256,2048]{1,0:T(8,128)S(1)} %fusion.59, bf16[256,2048]{0,1:T(8,128)(2,1)} %collective-permute-done.7, f32[256]{0:T(256)S(1)} %compare_convert_fusion.1, bf16[6,2,256,256]{3,2,1,0:T(8,128)(2,1)S(1)} %copy-done, s32[]{:T(128)S(6)} %select_n.99), kind=kOutput, calls=%fused_computation.49 | convolution fusion | flops 270008320 | bytes 4326404 | tf_op jit(solution)/shard_map/dot_general | solution.py:97
  173.9 3.2 %collective-permute-start.8 = (bf16[256,2048]{1,0:T(8,128)(2,1)}, bf16[256,2048]{1,0:T(8,128)(2,1)}, u32[]{:S(2)}, u32[]{:S(2)}) collective-permute-start(bf16[256,2048]{1,0:T(8,128)(2,1)} %fusion.30), channel_id=1, source_target_pairs={{0,64},{64,0},{16,80},{80,16},{32,96},{96,32},{48,112},{112,48},{1... | collective-permute-start | bytes 3145736 | tf_op jit(solution)/shard_map/ppermute | solution.py:14
  177.1 24.4 %fusion = f32[2048,2048]{1,0:T(8,128)} fusion(bf16[2048,2048]{1,0:T(8,128)(2,1)} %gather_fusion, bf16[1,2048,2048]{2,1,0:T(8,128)(2,1)} %param.11), kind=kOutput, calls=%fused_computation.3 | convolution fusion | flops 17179869184 | bytes 33554432 | tf_op jit(solution)/shard_map/dot_general | solution.py:66
  201.5 0.7 compare_convert_fusion
  202.2 1.7 fusion.60
  203.9 2.7 fusion.32
  206.6 3.5 %fusion.41 = f32[256,2048]{1,0:T(8,128)} fusion(bf16[256,2048]{1,0:T(8,128)(2,1)} %fusion.32, bf16[256,256]{1,0:T(8,128)(2,1)S(1)} %copy-done.4, f32[256]{0:T(256)S(1)} %compare_convert_fusion, bf16[6,2,256,256]{3,2,1,0:T(8,128)(2,1)S(1)} %copy-done, s32[]{:T(128)S(6)} %select_n.98), kind=kOutput, calls=%fused_computation.60 | convolution fusion | flops 537919488 | bytes 3408900 | tf_op jit(solution)/shard_map/dot_general | solution.py:104
  210.1 4.0 %fusion.35 = f32[256,2048]{1,0:T(8,128)} fusion(f32[256,2048]{1,0:T(8,128)} %fusion.41, bf16[256,2048]{1,0:T(8,128)(2,1)} %collective-permute-done.8, f32[256]{0:T(256)S(1)} %compare_convert_fusion.1, bf16[6,2,256,256]{3,2,1,0:T(8,128)(2,1)S(1)} %copy-done, s32[]{:T(128)S(6)} %select_n.98, s32[]{:T(128)S(6)} %add.261, s32[]{:T(128)S(6)} %select_n.96), kind=kOutput, calls=%fused_computation.54 | convolution fusion | flops 538443776 | bytes 5506060 | tf_op jit(solution)/shard_map/dot_general | solution.py:104
  214.1 4.0 %fusion.36 = f32[256,2048]{1,0:T(8,128)} fusion(f32[256,2048]{1,0:T(8,128)} %fusion.35, bf16[256,2048]{0,1:T(8,128)(2,1)} %collective-permute-done.7, f32[256]{0:T(256)S(1)} %compare_convert_fusion.2, bf16[6,2,256,256]{3,2,1,0:T(8,128)(2,1)S(1)} %copy-done, s32[]{:T(128)S(6)} %select_n.96, s32[]{:T(128)S(6)} %add.261, ...), kind=kOutput, calls=%fused_computation.55 | convolution fusion | flops 538443776 | bytes 5506060 | tf_op jit(solution)/shard_map/dot_general | solution.py:104
  218.1 4.1 %fusion.37 = f32[256,2048]{1,0:T(8,128)} fusion(f32[256,2048]{1,0:T(8,128)} %fusion.36, bf16[256,2048]{1,0:T(8,128)(2,1)} %copy-done.1, f32[256]{0:T(256)S(1)} %compare_convert_fusion.3, bf16[1,15,2,256,256]{4,3,2,1,0:T(8,128)(2,1)} %param.14, s32[]{:T(128)S(6)} %select_n.93, s32[]{:T(128)S(6)} %add.261, s32[]{:T(128)S(6)} %select_n.90), kind=kOutput, calls=%fused_computation.56 | convolution fusion | flops 538443776 | bytes 5506060 | tf_op jit(solution)/shard_map/dot_general | solution.py:104
  222.2 4.1 %fusion.38 = f32[256,2048]{1,0:T(8,128)} fusion(f32[256,2048]{1,0:T(8,128)} %fusion.37, bf16[256,2048]{1,0:T(8,128)(2,1)} %collective-permute-done.4, f32[256]{0:T(256)S(1)} %compare_convert_fusion.4, bf16[1,15,2,256,256]{4,3,2,1,0:T(8,128)(2,1)} %param.14, s32[]{:T(128)S(6)} %select_n.90, s32[]{:T(128)S(6)} %add.261, s32[]{:T(128)S(6)} %select_n.87), kind=kOutput, calls=%fused_computation.57 | convolution fusion | flops 538443776 | bytes 5506060 | tf_op jit(solution)/shard_map/dot_general | solution.py:104
  226.3 4.1 %fusion.39 = f32[256,2048]{1,0:T(8,128)} fusion(f32[256,2048]{1,0:T(8,128)} %fusion.38, bf16[256,2048]{1,0:T(8,128)(2,1)} %collective-permute-done.3, f32[256]{0:T(256)S(1)} %compare_convert_fusion.5, bf16[1,15,2,256,256]{4,3,2,1,0:T(8,128)(2,1)} %param.14, s32[]{:T(128)S(6)} %select_n.87, s32[]{:T(128)S(6)} %add.261, s32[]{:T(128)S(6)} %select_n.85), kind=kOutput, calls=%fused_computation.58 | convolution fusion | flops 538443776 | bytes 5506060 | tf_op jit(solution)/shard_map/dot_general | solution.py:104
  230.5 4.1 %fusion.40 = f32[2048,256]{1,0:T(8,128)} fusion(f32[256,2048]{1,0:T(8,128)} %fusion.39, bf16[256,2048]{0,1:T(8,128)(2,1)} %collective-permute-done.2, f32[256]{0:T(256)S(1)} %compare_convert_fusion.6, bf16[1,15,2,256,256]{4,3,2,1,0:T(8,128)(2,1)} %param.14, s32[]{:T(128)S(6)} %select_n.85, s32[]{:T(128)S(6)} %add.261, bf16[1,2,256,256]{3,2,1,0:T(8,128)(2,1)S(1)} %copy-done.2), kind=kOutput, calls=%fused_computation.59 | convolution fusion | flops 538443776 | bytes 5506056 | tf_op jit(solution)/shard_map/dot_general | solution.py:104
  234.6 10.9 %fusion.2 = bf16[2048,2048]{0,1:T(8,128)(2,1)} fusion(f32[2048,2048]{1,0:T(8,128)} %fusion, f32[2048,256]{1,0:T(8,128)} %fusion.40, bf16[256,2048]{0,1:T(8,128)(2,1)S(1)} %collective-permute-done, bf16[1,2048,256]{2,1,0:T(8,128)(2,1)} %param.12, f32[256]{0:T(256)S(1)} %compare_convert_fusion.7, bf16[1,2,256,256]{3,2,1,0:T(8,128)(2,1)S(1)} %copy-done.2), kind=kOutput, calls=%fused_computation.5 | convolution fusion | flops 2425880576 | bytes 29492224 | tf_op jit(solution)/shard_map/dot_general | solution.py:106
  245.5 12.3 %copy.11 = bf16[2048,2048]{1,0:T(8,128)(2,1)} copy(bf16[2048,2048]{0,1:T(8,128)(2,1)} %fusion.2) | data formatting | bytes 16777216 | tf_op jit(solution)/shard_map/convert_element_type | solution.py:106
  257.8 18.0 %scatter_custom_fusion = bf16[2048,2048]{1,0:T(8,128)(2,1)} fusion(s32[2048]{0:T(1024)S(1)} %bitcast.127, bf16[2048,2048]{1,0:T(8,128)(2,1)} %copy.11, bf16[]{:T(256)} %constant.83.clone.1), kind=kCustom, calls=%fused_computation.6 | custom fusion | bytes 8389120 | tf_op jit(solution)/shard_map/scatter | solution.py:109
  (20 shorter events, 1.6 us)
Async XLA Ops:
  0.0 147.8 %copy-start = (bf16[6,2,256,256]{3,2,1,0:T(8,128)(2,1)S(1)}, bf16[6,2,256,256]{3,2,1,0:T(8,128)(2,1)}, u32[]{:S(2)}) copy-start(bf16[6,2,256,256]{3,2,1,0:T(8,128)(2,1)} %param.15) | copy-start | bytes 4718596
  3.0 20.9 %copy-start.3 = (bf16[1,2048,256]{2,1,0:T(8,128)(2,1)S(1)}, bf16[1,2048,256]{2,1,0:T(8,128)(2,1)}, u32[]{:S(2)}) copy-start(bf16[1,2048,256]{2,1,0:T(8,128)(2,1)} %param.12) | copy-start | bytes 3145732
  23.9 7.6 %copy-start.2 = (bf16[1,2,256,256]{3,2,1,0:T(8,128)(2,1)S(1)}, bf16[1,2,256,256]{3,2,1,0:T(8,128)(2,1)}, u32[]{:S(2)}) copy-start(bf16[1,2,256,256]{3,2,1,0:T(8,128)(2,1)} %param.13) | copy-start | bytes 786436
  29.9 27.6 %collective-permute-start = (bf16[256,2048]{0,1:T(8,128)(2,1)S(1)}, bf16[256,2048]{0,1:T(8,128)(2,1)S(1)}, u32[]{:S(2)}, u32[]{:S(2)}) collective-permute-start(bf16[256,2048]{0,1:T(8,128)(2,1)S(1)} %bitcast.125), channel_id=1, source_target_pairs={{0,1},{1,0},{2,3},{3,2},{4,5},{5,4},{6,7},{7,6},{8,9},{9,8},{10,11... | collective-permute-start | bytes 3145736 | tf_op jit(solution)/shard_map/ppermute | solution.py:14
  31.5 26.0 %collective-permute-start.1 = (bf16[256,256]{1,0:T(8,128)(2,1)S(1)}, bf16[256,256]{1,0:T(8,128)(2,1)S(1)}, u32[]{:S(2)}, u32[]{:S(2)}) collective-permute-start(bf16[256,256]{1,0:T(8,128)(2,1)S(1)} %slice_bitcast_fusion.1), channel_id=1, source_target_pairs={{0,1},{1,0},{2,3},{3,2},{4,5},{5,4},{6,7},{7,6},{8,9},{9,8},{10,11... | collective-permute-start | bytes 393224 | tf_op jit(solution)/shard_map/ppermute | solution.py:14
  58.9 25.9 %collective-permute-start.2 = (bf16[256,2048]{0,1:T(8,128)(2,1)}, bf16[256,2048]{0,1:T(8,128)(2,1)}, u32[]{:S(2)}, u32[]{:S(2)}) collective-permute-start(bf16[256,2048]{0,1:T(8,128)(2,1)} %bitcast.10), channel_id=1, source_target_pairs={{0,2},{2,0},{1,3},{3,1},{4,6},{6,4},{5,7},{7,5},{8,10},{10,8},{9,1... | collective-permute-start | bytes 3145736 | tf_op jit(solution)/shard_map/ppermute | solution.py:14
  87.7 23.8 %collective-permute-start.3 = (bf16[256,2048]{1,0:T(8,128)(2,1)}, bf16[256,2048]{1,0:T(8,128)(2,1)}, u32[]{:S(2)}, u32[]{:S(2)}) collective-permute-start(bf16[256,2048]{1,0:T(8,128)(2,1)} %fusion.22), channel_id=1, source_target_pairs={{0,4},{4,0},{1,5},{5,1},{2,6},{6,2},{3,7},{7,3},{8,12},{12,8},{9,1... | collective-permute-start | bytes 3145736 | tf_op jit(solution)/shard_map/ppermute | solution.py:14
  114.3 24.4 %collective-permute-start.4 = (bf16[256,2048]{1,0:T(8,128)(2,1)}, bf16[256,2048]{1,0:T(8,128)(2,1)}, u32[]{:S(2)}, u32[]{:S(2)}) collective-permute-start(bf16[256,2048]{1,0:T(8,128)(2,1)} %fusion.24), channel_id=1, source_target_pairs={{0,8},{8,0},{1,9},{9,1},{2,10},{10,2},{3,11},{11,3},{4,12},{12,4},... | collective-permute-start | bytes 3145736 | tf_op jit(solution)/shard_map/ppermute | solution.py:14
  140.5 3.6 %collective-permute-start.5 = (bf16[256,2048]{1,0:T(8,128)(2,1)S(1)}, bf16[256,2048]{1,0:T(8,128)(2,1)S(1)}, u32[]{:S(2)}, u32[]{:S(2)}) collective-permute-start(bf16[256,2048]{1,0:T(8,128)(2,1)S(1)} %fusion.26), channel_id=1, source_target_pairs={{0,16},{16,0},{32,48},{48,32},{64,80},{80,64},{96,112},{112,96},{1... | collective-permute-start | bytes 3145736 | tf_op jit(solution)/shard_map/ppermute | solution.py:14
  141.5 2.6 collective-permute-start.6
  144.2 1.5 copy-start.1
  145.6 25.4 %collective-permute-start.7 = (bf16[256,2048]{0,1:T(8,128)(2,1)}, bf16[256,2048]{0,1:T(8,128)(2,1)}, u32[]{:S(2)}, u32[]{:S(2)}) collective-permute-start(bf16[256,2048]{0,1:T(8,128)(2,1)} %bitcast.27), channel_id=1, source_target_pairs={{0,32},{32,0},{16,48},{48,16},{64,96},{96,64},{80,112},{112,80},{1... | collective-permute-start | bytes 3145736 | tf_op jit(solution)/shard_map/ppermute | solution.py:14
  173.9 30.0 %collective-permute-start.8 = (bf16[256,2048]{1,0:T(8,128)(2,1)}, bf16[256,2048]{1,0:T(8,128)(2,1)}, u32[]{:S(2)}, u32[]{:S(2)}) collective-permute-start(bf16[256,2048]{1,0:T(8,128)(2,1)} %fusion.30), channel_id=1, source_target_pairs={{0,64},{64,0},{16,80},{80,16},{32,96},{96,32},{48,112},{112,48},{1... | collective-permute-start | bytes 3145736 | tf_op jit(solution)/shard_map/ppermute | solution.py:14
  203.9 2.7 copy-start.4
where the time goes:
time: 277 us; the launch traced here: 276 us
  waiting for transfers between devices  104 us (38%)
  matrix products  95.7 us (35%)
  local copies, waits for them, and re-layouts  53.8 us (19%)
  starting transfers between devices  16.7 us (6%)
  other arithmetic  5.65 us (2%)
    ppermute x9, waiting for transfers between devices, swapped(): return lax.ppermute(block, axis, route)  104 us
    dot_general x7, matrix products, body(): jnp.dot(node_pair[0], far_coef, preferred_element_type=jnp.float32)  27.9 us
    dot_general x1, matrix products, body(): near = jnp.dot(diag_blocks[0], ordered, preferred_element_type=jnp.float32)  24.4 us
    gather x1, local copies, waits for them, and re-layouts, body(): ordered = points[positions]  20.9 us
    scatter x1, local copies, waits for them, and re-layouts, body(): return jnp.zeros_like(values).at[positions].set(values)  18 us
    ppermute x9, starting transfers between devices, swapped(): return lax.ppermute(block, axis, route)  16.7 us
    dot_general x7, matrix products, body(): jnp.dot(peer_transfer.T, peer_coef, preferred_element_type=jnp.float32)  15.9 us
    convert_element_type x1, local copies, waits for them, and re-layouts, body(): (near + jnp.dot(basis, far_coef, preferred_element_type=jnp.float32)).ast...  12.3 us
  transfers between devices with their start and end apart: 9, of which 5 were waited for; matrix products, arithmetic and copies ran while one was open for 15% of the time, Pallas kernels for 0%

commit v1 on v0

v1 whole, which is shorter than its diff:
```python
import functools

import jax
import jax.numpy as jnp
from jax import lax
from jax.experimental import pallas as pl
from jax.experimental.pallas import tpu as pltpu
from jax.sharding import PartitionSpec as P

BF = jnp.bfloat16
F32 = jnp.float32
RING = 4
SMALL = 24 * 2**20


def nn(a, b):
    return jnp.dot(a, b, preferred_element_type=F32)


def nt(a, b):
    return lax.dot_general(a, b, (((1,), (1,)), ((), ())), preferred_element_type=F32)


def masked(value, rank):
    lane = lax.broadcasted_iota(jnp.int32, value.shape, 1)
    return jnp.where(lane < rank, value, 0.0).astype(BF)


def params(limit):
    return pltpu.CompilerParams(vmem_limit_bytes=limit)


def cost(flops, moved):
    return pl.CostEstimate(flops=flops, bytes_accessed=moved, transcendentals=0)


def sds(*shape):
    return jax.ShapeDtypeStruct(shape, BF)


def held(*shape):
    return pltpu.VMEM(shape, BF)


def pin(x, space=pltpu.VMEM):
    return pltpu.with_memory_space_constraint(x, space)


SMEM = pl.BlockSpec(memory_space=pltpu.SMEM)
VMEM = pl.BlockSpec(memory_space=pltpu.VMEM)
HBM = pl.BlockSpec(memory_space=pltpu.HBM)


def place():
    inner = lax.axis_index("inner")
    return inner & 3, inner >> 2, lax.axis_index("outer")


def call(kernel, name, out_shapes, args, flops=2**28, limit=8, scratch=(), specs=None):
    many = isinstance(out_shapes, tuple)
    return pl.pallas_call(
        kernel,
        out_shape=out_shapes,
        in_specs=specs or [SMEM] + [VMEM] * (len(args) - 1),
        out_specs=(VMEM,) * len(out_shapes) if many else VMEM,
        scratch_shapes=list(scratch),
        compiler_params=params(limit * 2**20),
        cost_estimate=cost(flops, 2**20),
        name=name,
    )(*args)


def shuffle_basis(order, basis, out, out_t, src, dst):
    rows = basis.shape[0]

    @pl.loop(0, rows // 64)
    def _(b):
        for r in range(4):
            for t in range(2):
                start = pl.multiple_of(b * 64 + r * 16, 16)
                x = basis[pl.ds(start, 16), t * 128 : (t + 1) * 128].astype(F32)
                base = (b * 64 + r * 16) * 3 + t
                src[pl.ds(base, 8, stride=3), :] = x[:8]
                src[pl.ds(base + 24, 8, stride=3), :] = x[8:]

    @pl.loop(0, rows // 64)
    def _(i):
        for j in range(64):
            to = order[0, i * 64 + j] * 3
            dst[pl.ds(to, 2), :] = src[pl.ds(i * 192 + j * 3, 2), :]

    @pl.loop(0, rows // 256)
    def _(b):
        for t in range(2):
            parts = []
            for r in range(32):
                base = (b * 256 + r * 8) * 3 + t
                parts.append(dst[pl.ds(base, 8, stride=3), :])
            x = jnp.concatenate(parts, axis=0)
            start = pl.multiple_of(b * 256, 256)
            out[pl.ds(start, 256), t * 128 : (t + 1) * 128] = x.astype(BF)
            out_t[t * 128 : (t + 1) * 128, pl.ds(start, 256)] = x.T.astype(BF)


def coef_block(shift, ranks, basis_t, x, transfer, coef, piece):
    ring, z, outer = place()
    cols = piece.shape[0]
    start = pl.multiple_of(lax.rem(ring + shift, RING) * cols, cols)
    rank = ranks[127 + outer * 16 + z * RING + ring]
    for j in range(0, cols, 256):
        c = masked(nn(basis_t[...], x[:, pl.ds(start + j, 256)]).T, rank)
        coef[pl.ds(start + j, 256), :] = c
        piece[j : j + 256] = nn(c, transfer[...]).astype(BF)


def front_kernel(
    order_hbm, ranks_hbm, basis_hbm, x_hbm, node_hbm,
    out, x, coef, p0, p1, p2, p3,
    order, ranks, basis, out_t, transfer, src, dst, sem,
):
    cols = p0.shape[0]
    ring = place()[0]

    def fetch(k):
        start = pl.multiple_of(lax.rem(ring + (2, 1, 3, 0)[k], RING) * cols, cols)
        part = pl.ds(start, cols)
        return pltpu.make_async_copy(x_hbm.at[:, part], x.at[:, part], sem.at[k])

    loads = [
        pltpu.make_async_copy(basis_hbm, basis, sem.at[4]),
        pltpu.make_async_copy(order_hbm, order, sem.at[5]),
        pltpu.make_async_copy(ranks_hbm, ranks, sem.at[6]),
        pltpu.make_async_copy(node_hbm.at[0], transfer, sem.at[7]),
    ]
    for load in loads:
        load.start()
    for k in range(RING):
        fetch(k).start()
    for load in loads:
        load.wait()
    shuffle_basis(order, basis, out, out_t, src, dst)
    for k, ref in enumerate((p2, p1, p3, p0)):
        fetch(k).wait()
        coef_block((2, 1, 3, 0)[k], ranks, out_t, x, transfer, coef, ref)


def front(order, ranks, basis, points, nodes):
    rows, width = basis.shape
    cols = points.shape[1]
    piece = held(cols // RING, width)
    return call(
        front_kernel,
        "front",
        (held(rows, width), held(rows, cols), held(cols, width)) + (piece,) * 4,
        [pin(a, pltpu.HBM) for a in (order, ranks, basis, points, nodes)],
        flops=2**31,
        limit=16,
        scratch=[
            pltpu.SMEM(order.shape, jnp.int32),
            pltpu.SMEM(ranks.shape, jnp.int32),
            pltpu.VMEM((rows, width), BF),
            pltpu.VMEM((width, rows), BF),
            pltpu.VMEM((width, width), BF),
            pltpu.VMEM((rows * 3, 128), F32),
            pltpu.VMEM((rows * 3, 128), F32),
            pltpu.SemaphoreType.DMA((8,)),
        ],
        specs=[HBM] * 5,
    )


PITCH = 9


def move_kernel(scatter, order, x, o, src, dst):
    rows = x.shape[0]

    for half in range(x.shape[1] // 1024):

        @pl.loop(0, rows // 32)
        def _(b):
            for r in range(2):
                base = (b * 32 + r * 16) * PITCH
                start = pl.multiple_of(b * 32 + r * 16, 16)
                for t in range(8):
                    at = half * 1024 + t * 128
                    v = x[pl.ds(start, 16), at : at + 128].astype(F32)
                    src[pl.ds(base + t, 8, stride=PITCH), :] = v[:8]
                    src[pl.ds(base + 8 * PITCH + t, 8, stride=PITCH), :] = v[8:]

        @pl.loop(0, rows // 64)
        def _(i):
            for j in range(64):
                far_at = order[0, i * 64 + j] * PITCH
                near_at = i * (64 * PITCH) + j * PITCH
                s, d = (near_at, far_at) if scatter else (far_at, near_at)
                dst[pl.ds(d, 8), :] = src[pl.ds(s, 8), :]

        @pl.loop(0, rows // 32)
        def _(b):
            for r in range(2):
                base = (b * 32 + r * 16) * PITCH
                start = pl.multiple_of(b * 32 + r * 16, 16)
                for t in range(8):
                    lo = dst[pl.ds(base + t, 8, stride=PITCH), :]
                    hi = dst[pl.ds(base + 8 * PITCH + t, 8, stride=PITCH), :]
                    at = half * 1024 + t * 128
                    v = jnp.concatenate([lo, hi], axis=0).astype(BF)
                    o[pl.ds(start, 16), at : at + 128] = v


def move_rows(scatter, order, x):
    rows, cols = x.shape
    return pl.pallas_call(
        functools.partial(move_kernel, scatter),
        out_shape=held(rows, cols),
        in_specs=[SMEM, VMEM],
        out_specs=VMEM,
        scratch_shapes=[pltpu.VMEM((rows * PITCH, 128), F32)] * 2,
        compiler_params=params(22 * 2**20),
        cost_estimate=cost(0, 18 * 2**20),
        name=f"move_{int(scatter)}",
    )(order, pin(x))


def near_kernel(first, d, x, out):
    size = out.shape[0]

    for j in range(0, x.shape[1], 256):
        out[:, j : j + 256] = nn(d[first : first + size], x[:, j : j + 256]).astype(BF)


def near_rows(piece, pieces, diag, ordered):
    rows, depth = diag.shape
    cols = ordered.shape[1]
    size = rows // pieces
    return pl.pallas_call(
        functools.partial(near_kernel, piece * size),
        out_shape=held(size, cols),
        in_specs=[VMEM] * 2,
        out_specs=VMEM,
        compiler_params=params(8 * 2**20),
        cost_estimate=cost(2 * size * depth * cols, 2**20),
        name=f"near_{piece}",
    )(pin(diag), pin(ordered))


def quad_up_kernel(ranks, u0, u1, u2, u3, inner, mid, p0, p1, p2, p3, leaf, top):
    x, z, outer = place()
    quad = outer * RING + z
    size = p0.shape[0]
    for s, ref in enumerate((u0, u1, u2, u3)):
        leaf[(x - s) & 3] = ref[...]
    for k in range(2):
        up = leaf[2 * k].astype(F32) + leaf[2 * k + 1].astype(F32)
        mid[k] = masked(up, ranks[63 + 2 * quad + k])
    up = nn(mid[0], inner[2 * z, 0]) + nn(mid[1], inner[2 * z + 1, 0])
    top[...] = masked(up, ranks[31 + quad])
    for t, ref in enumerate((p0, p1, p2, p3)):
        ref[...] = top[pl.ds(pl.multiple_of(((z + t) & 3) * size, size), size), :]


def quad_up(ranks, pieces, inner):
    cols, width = pieces[0].shape
    return call(
        quad_up_kernel,
        "quad_up",
        (held(2, cols, width),) + (held(cols // RING, width),) * 4,
        (ranks, *map(pin, pieces), pin(inner)),
        scratch=[pltpu.VMEM((4, cols, width), BF), pltpu.VMEM((cols, width), BF)],
    )


def group_up_kernel(ranks, q0, q1, q2, q3, inner, out2, out3, out4, lift):
    x, z, group = place()
    for t, ref in enumerate((q0, q1, q2, q3)):
        out2[(z - t) & 3] = ref[...]
    for k in range(2):
        up = nn(out2[2 * k], inner[8 + 2 * k, 0]) + nn(out2[2 * k + 1], inner[9 + 2 * k, 0])
        out3[k] = masked(up, ranks[15 + 2 * group + k])
    up = nn(out3[0], inner[12, 0]) + nn(out3[1], inner[13, 0])
    out4[...] = masked(up, ranks[7 + group])
    lift[...] = nn(out4[...], inner[14, 0])


def group_up(ranks, pieces, inner):
    part, width = pieces[0].shape
    return call(
        group_up_kernel,
        "group_up",
        (
            held(4, part, width),
            held(2, part, width),
            held(part, width),
            pltpu.VMEM((part, width), F32),
        ),
        (ranks, *map(pin, pieces), pin(inner)),
    )


def five_kernel(ranks, own, peer, out):
    out[...] = masked(own[...] + peer[...], ranks[3 + (place()[2] >> 1)])


def five_up(ranks, own, peer):
    return call(five_kernel, "five", held(*own.shape), (ranks, pin(own), pin(peer)))


def top_kernel(
    ranks, y0, y1, y2, y3, peer4, c2, c3, inner, outer, root, p0, p1, p2, p3, five, far2
):
    x, z, group = place()
    y = group >> 1
    half = y >> 1
    for s, ref in enumerate((y0, y1, y2, y3)):
        five[y ^ s] = ref[...]
    six = []
    for k in range(2):
        up = nn(five[2 * k], outer[2 * k, 0]) + nn(five[2 * k + 1], outer[2 * k + 1, 0])
        six.append(masked(up, ranks[1 + k]))
    up = nn(six[0], outer[4, 0]) + nn(six[1], outer[5, 0])
    seven = masked(up, ranks[0])
    far = masked(nt(seven, root[...]), ranks[0])
    sib = jnp.where(half == 0, six[1].astype(F32), six[0].astype(F32)).astype(BF)
    far = masked(nt(sib, outer[4 + half, 1]) + nt(far, outer[4 + half, 0]), ranks[1 + half])
    far = masked(nt(five[y ^ 1], outer[y, 1]) + nt(far, outer[y, 0]), ranks[3 + y])
    far = masked(nt(peer4[...], inner[14, 1]) + nt(far, inner[14, 0]), ranks[7 + group])
    for k in range(2):
        down = nt(c3[1 - k], inner[12 + k, 1]) + nt(far, inner[12 + k, 0])
        far3 = masked(down, ranks[15 + 2 * group + k])
        for i in (2 * k, 2 * k + 1):
            down = nt(c2[i ^ 1], inner[8 + i, 1]) + nt(far3, inner[8 + i, 0])
            far2[i] = masked(down, ranks[31 + 4 * group + i])
    for t, ref in enumerate((p0, p1, p2, p3)):
        ref[...] = far2[(z + t) & 3]


def top_sweep(ranks, fives, peer4, c2, c3, inner, outer, root):
    part, width = fives[0].shape
    return call(
        top_kernel,
        "top",
        (held(part, width),) * 4,
        (ranks, *map(pin, (*fives, peer4, c2, c3, inner, outer, root))),
        scratch=[pltpu.VMEM((4, part, width), BF)] * 2,
    )


def quad_down_kernel(ranks, f0, f1, f2, f3, mid, inner, p0, p1, p2, p3, far2, far1):
    x, z, outer = place()
    quad = outer * RING + z
    size = f0.shape[0]
    for t, ref in enumerate((f0, f1, f2, f3)):
        far2[pl.ds(pl.multiple_of(((z - t) & 3) * size, size), size), :] = ref[...]
    for k in range(2):
        down = nt(mid[1 - k], inner[2 * z + k, 1]) + nt(far2[...], inner[2 * z + k, 0])
        far1[k] = masked(down, ranks[63 + 2 * quad + k])
    for s, ref in enumerate((p0, p1, p2, p3)):
        ref[...] = far1[((x + s) & 3) >> 1]


def quad_down(ranks, fars, mid, inner):
    part, width = fars[0].shape
    cols = part * RING
    return call(
        quad_down_kernel,
        "quad_down",
        (held(cols, width),) * 4,
        (ranks, *map(pin, (*fars, mid, inner))),
        scratch=[pltpu.VMEM((cols, width), BF), pltpu.VMEM((2, cols, width), BF)],
    )


def tail_kernel(shift, ranks, basis, sibling, node, far1, *refs):
    nears = refs[:4]
    o_hbm, buf, sem = refs[-3:]
    x, z, outer = place()
    cols = far1.shape[0]
    size = nears[0].shape[0]
    at = pl.ds(pl.multiple_of(((x - shift) & 3) * cols, cols), cols)

    def put(k):
        return pltpu.make_async_copy(buf.at[k], o_hbm.at[pl.ds(k * size, size), at], sem.at[k])

    down = nt(sibling[at, :], node[1]) + nt(far1[...], node[0])
    far = masked(down, ranks[127 + outer * 16 + z * RING + x])
    for k, near in enumerate(nears):
        add = nt(basis[k * size : (k + 1) * size], far)
        buf[k] = (near[:, at].astype(F32) + add).astype(BF)
        put(k).start()
    for k in range(len(nears)):
        put(k).wait()


def add_far(shift, ranks, basis, sibling, node, far1, nears, sofar):
    rows, width = basis.shape
    cols = far1.shape[0]
    count = len(nears)
    args = [ranks] + [pin(a) for a in (basis, sibling, node, far1, *nears)]
    specs = [SMEM] + [VMEM] * (4 + count)
    alias = {}
    if sofar is not None:
        alias = {len(args): 0}
        args.append(sofar)
        specs.append(HBM)
    return pl.pallas_call(
        functools.partial(tail_kernel, shift),
        out_shape=sds(rows, nears[0].shape[1]),
        in_specs=specs,
        out_specs=HBM,
        input_output_aliases=alias,
        scratch_shapes=[
            pltpu.VMEM((count, rows // count, cols), BF),
            pltpu.SemaphoreType.DMA((count,)),
        ],
        compiler_params=params(8 * 2**20),
        cost_estimate=cost(2 * rows * width * cols, 3 * 2**20),
        name=f"tail_{shift}",
    )(*args)


def ring_x(block, shift):
    route = [(z * RING + x, z * RING + (x + shift) % RING) for z in range(RING) for x in range(RING)]
    return lax.ppermute(block, "inner", route)


def ring_z(block, shift):
    route = [(z * RING + x, (z + shift) % RING * RING + x) for z in range(RING) for x in range(RING)]
    return lax.ppermute(block, "inner", route)


def swap_inner(block, bits):
    return lax.ppermute(block, "inner", [(i, i ^ bits) for i in range(RING * RING)])


def swap_outer(block, bits):
    return lax.ppermute(block, "outer", [(o, o ^ bits) for o in range(2 * RING)])


def exchange(move, pieces, order=(2, 1, 3)):
    got = {0: pieces[0]}
    for s in order:
        got[s] = move(pieces[s], s)
    return [got[s] for s in range(RING)]


def body(
    points,
    leaf_order,
    diag_blocks,
    leaf_basis,
    leaf_nodes,
    inner_nodes,
    outer_nodes,
    root_coupling,
    node_ranks,
):
    ranks = node_ranks
    inner = inner_nodes[0]
    node = leaf_nodes[0]

    basis, x, coef, *pieces = front(leaf_order, ranks, leaf_basis[0], points, node)
    pieces = exchange(ring_x, pieces)
    ordered = move_rows(False, leaf_order, x)
    diag = move_rows(True, leaf_order, diag_blocks[0])
    *pieces, ordered, diag, coef = lax.optimization_barrier((*pieces, ordered, diag, coef))

    mid, *parts = quad_up(ranks, pieces, inner)
    coef, *parts = lax.optimization_barrier((coef, *parts))
    parts = exchange(ring_z, parts)
    sibling = swap_inner(coef, 1)
    nears = [near_rows(0, 4, diag, ordered)]
    *parts, nears[0] = lax.optimization_barrier((*parts, nears[0]))
    c2, c3, c4, lift = group_up(ranks, parts, inner)
    peer4 = swap_outer(c4, 1)
    five = five_up(ranks, lift, swap_outer(lift, 1))
    fives = [five] + [swap_outer(five, 2 * s) for s in (1, 2, 3)]
    nears.append(near_rows(1, 4, diag, ordered))
    *fives, nears[1] = lax.optimization_barrier((*fives, nears[1]))
    parts = top_sweep(ranks, fives, peer4, c2, c3, inner, outer_nodes, root_coupling)
    parts = exchange(ring_z, parts)
    nears.append(near_rows(2, 4, diag, ordered))
    *parts, nears[2] = lax.optimization_barrier((*parts, nears[2]))
    fars = quad_down(ranks, parts, mid, inner)
    fars = exchange(ring_x, fars)
    nears.append(near_rows(3, 4, diag, ordered))
    out = None
    for s in (0, 1, 3, 2):
        out = add_far(s, ranks, basis, sibling, node, fars[s], nears, out)
    return out


def solution(mesh):
    in_specs = (
        P(("outer", "inner"), None),
        P(("outer", "inner"), None),
        P(("outer", "inner"), None, None),
        P(("outer", "inner"), None, None),
        P(("outer", "inner"), None, None, None),
        P("outer", None, None, None, None),
        P(),
        P(),
        P(),
    )
    out_specs = P(("outer", "inner"), None)
    return jax.shard_map(body, mesh=mesh, in_specs=in_specs, out_specs=out_specs, check_vma=False)
```

time: 277 us -> 94.3 us (0.34)
  waiting for transfers between devices: 104 us -> 3.76 us
  matrix products: 95.7 us -> 0 us
  Pallas kernels: 0 us -> 64.8 us
  local copies, waits for them, and re-layouts: 53.8 us -> 0.04 us
  starting transfers between devices: 16.7 us -> 25.2 us
  other arithmetic: 5.65 us -> 0 us
    ppermute x9 -> x18, waiting for transfers between devices: 104 us -> 3.76 us  [the longest x6 2.74 us: ring_x(): return lax.ppermute(block, 'inner', route)]
    dot_general x24 -> x0, matrix products: 95.7 us -> none  [the longest x7 27.9 us: body(): jnp.dot(node_pair[0], far_coef, preferred_element_type=jnp.float32)]
    pallas_call x0 -> x16, Pallas kernels: none -> 64.8 us  [the longest x2 18.1 us: move_rows(): pl.pallas_call(functools.partial(move_kernel, scatter), out_shape=held(ro...]
    gather x1 -> x0, local copies, waits for them, and re-layouts: 20.9 us -> none  [body(): ordered = points[positions]]
    scatter x1 -> x0, local copies, waits for them, and re-layouts: 18 us -> none  [body(): return jnp.zeros_like(values).at[positions].set(values)]
    convert_element_type x1 -> x0, local copies, waits for them, and re-layouts: 12.3 us -> none  [body(): (near + jnp.dot(basis, far_coef, preferred_element_type=jnp.float32)).ast...]
    ppermute x9 -> x18, starting transfers between devices: 16.7 us -> 25.2 us  [the longest x6 10.4 us: ring_z(): return lax.ppermute(block, 'inner', route)]
    convert_element_type x8 -> x0, other arithmetic: 4.94 us -> none  [column_mask(): (jnp.arange(rank_width, dtype=jnp.int32)[:, None] < limit).astype(jnp.flo...]
  transfers between devices with their start and end apart: 9 -> 18, of which waited for: 5 -> 3; matrix products, arithmetic and copies ran while one was open for 15% -> 0% of each run, Pallas kernels for 0% -> 51%
where the time goes in v1:
time: 94.3 us; the launch traced here: 94.2 us
  Pallas kernels  64.8 us (69%)
  starting transfers between devices  25.2 us (27%)
  waiting for transfers between devices  3.76 us (4%)
    pallas_call x2, Pallas kernels, move_rows(): pl.pallas_call(functools.partial(move_kernel, scatter), out_shape=held(ro...  18.1 us
    pallas_call x4, Pallas kernels, near_rows(): pl.pallas_call(functools.partial(near_kernel, piece * size), out_shape=he...  18 us
    pallas_call x6, Pallas kernels, call(): pl.pallas_call(kernel, out_shape=out_shapes, in_specs=specs or [SMEM] + [...  17.9 us
    pallas_call x4, Pallas kernels, add_far(): pl.pallas_call(functools.partial(tail_kernel, shift), out_shape=sds(rows,...  10.8 us
    ppermute x6, starting transfers between devices, ring_z(): return lax.ppermute(block, 'inner', route)  10.4 us
    ppermute x6, starting transfers between devices, ring_x(): return lax.ppermute(block, 'inner', route)  9.7 us
    ppermute x5, starting transfers between devices, swap_outer(): lax.ppermute(block, 'outer', [(o, o ^ bits) for o in range(2 * RING)])  4.41 us
    ppermute x6, waiting for transfers between devices, ring_x(): return lax.ppermute(block, 'inner', route)  2.74 us
  transfers between devices with their start and end apart: 18, of which 3 were waited for; matrix products, arithmetic and copies ran while one was open for 0% of the time, Pallas kernels for 51%

profile of v1, /device:TPU:0, one launch (start us, length us, event | category | flops | bytes accessed | tf_op | source)
XLA Modules:
  0.0 94.2 jit_solution(5147332198414696573)
XLA Ops:
  0.0 11.7 %front.1 = (bf16[2048,256]{1,0:T(8,128)(2,1)S(1)}, bf16[2048,2048]{1,0:T(8,128)(2,1)S(1)}, bf16[2048,256]{1,0:T(8,128)(2,1)S(1)}, bf16[512,256]{1,0:T(8,128)(2,1...) custom-call(s32[1,2048]{1,0:T(1,128)} %order.3, s32[255]{0:T(256)} %ranks.17, ...), custom_call_target="tpu_custom_call" | custom-call | flops 2147483648 | bytes 1048576 | tf_op jit(solution)/shard_map/front/pallas_call | solution.py:61
  11.7 1.6 %collective-permute-start = (bf16[512,256]{1,0:T(8,128)(2,1)S(1)}, bf16[512,256]{1,0:T(8,128)(2,1)S(1)}, u32[]{:S(2)}, u32[]{:S(2)}) collective-permute-start(bf16[512,256]{1,0:T(8,128)(2,1)S(1)} %get-tuple-element.58), channel_id=1, source_target_pairs={{0,1},{1,2},{2,3},{3,0},{4,5},{5,6},{6,7},{7,4},{8,9},{9,10},{10,1... | collective-permute-start | bytes 786440 | tf_op jit(solution)/shard_map/ppermute | solution.py:424
  13.3 2.7 %collective-permute-start.1 = (bf16[512,256]{1,0:T(8,128)(2,1)S(1)}, bf16[512,256]{1,0:T(8,128)(2,1)S(1)}, u32[]{:S(2)}, u32[]{:S(2)}) collective-permute-start(bf16[512,256]{1,0:T(8,128)(2,1)S(1)} %get-tuple-element.59), channel_id=1, source_target_pairs={{0,2},{1,3},{2,0},{3,1},{4,6},{5,7},{6,4},{7,5},{8,10},{9,11},{10,... | collective-permute-start | bytes 786440 | tf_op jit(solution)/shard_map/ppermute | solution.py:424
  16.1 1.4 %collective-permute-start.2 = (bf16[512,256]{1,0:T(8,128)(2,1)S(1)}, bf16[512,256]{1,0:T(8,128)(2,1)S(1)}, u32[]{:S(2)}, u32[]{:S(2)}) collective-permute-start(bf16[512,256]{1,0:T(8,128)(2,1)S(1)} %get-tuple-element.60), channel_id=1, source_target_pairs={{0,3},{1,0},{2,1},{3,2},{4,7},{5,4},{6,5},{7,6},{8,11},{9,8},{10,9... | collective-permute-start | bytes 786440 | tf_op jit(solution)/shard_map/ppermute | solution.py:424
  17.5 9.1 %move_1.1.d = bf16[2048,2048]{1,0:T(8,128)(2,1)S(1)} custom-call(s32[1,2048]{1,0:T(1,128)S(1)} %copy-done.6, bf16[2048,2048]{1,0:T(8,128)(2,1)S(1)} %bitcast.8), custom_call_target="tpu_custom_call" | custom-call | bytes 18874368 | tf_op jit(solution)/shard_map/move_1/pallas_call | solution.py:214
  26.6 0.0 copy-start
  26.6 0.0 copy-start.5
  26.6 9.1 %move_0.1.x = bf16[2048,2048]{1,0:T(8,128)(2,1)S(1)} custom-call(s32[1,2048]{1,0:T(1,128)S(1)} %copy-done.6, bf16[2048,2048]{1,0:T(8,128)(2,1)S(1)} %get-tuple-element.61.x), custom_call_target="tpu_custom_call" | custom-call | bytes 18874368 | tf_op jit(solution)/shard_map/move_0/pallas_call | solution.py:214
  35.6 0.0 collective-permute-done.u1
  35.7 1.1 %quad_up.1 = (bf16[2,512,256]{2,1,0:T(8,128)(2,1)S(1)}, bf16[128,256]{1,0:T(8,128)(2,1)S(1)}, bf16[128,256]{1,0:T(8,128)(2,1)S(1)}, bf16[128,256]{1,0:T(8,128)(2,1)S(1)}, bf16[128,256]{1,0:T(8,128)(2,1)S(1)}) custom-call(s32[255]{0:T(256)S(1)} %copy-done.5, bf16[512,256]{1,0:T(8,128)(2,1)S(1)} %get-tuple-element.64.u0, ...), custom_call_target="tpu_custom_call" | custom-call | flops 268435456 | bytes 1048576 | tf_op jit(solution)/shard_map/quad_up/pallas_call | solution.py:61
  36.8 2.0 %collective-permute-start.4 = (bf16[128,256]{1,0:T(8,128)(2,1)S(1)}, bf16[128,256]{1,0:T(8,128)(2,1)S(1)}, u32[]{:S(2)}, u32[]{:S(2)}) collective-permute-start(bf16[128,256]{1,0:T(8,128)(2,1)S(1)} %get-tuple-element.74), channel_id=1, source_target_pairs={{0,4},{1,5},{2,6},{3,7},{4,8},{5,9},{6,10},{7,11},{8,12},{9,13},{1... | collective-permute-start | bytes 196616 | tf_op jit(solution)/shard_map/ppermute | solution.py:429
  38.8 3.6 %collective-permute-start.5 = (bf16[128,256]{1,0:T(8,128)(2,1)S(1)}, bf16[128,256]{1,0:T(8,128)(2,1)S(1)}, u32[]{:S(2)}, u32[]{:S(2)}) collective-permute-start(bf16[128,256]{1,0:T(8,128)(2,1)S(1)} %get-tuple-element.75), channel_id=1, source_target_pairs={{0,8},{1,9},{2,10},{3,11},{4,12},{5,13},{6,14},{7,15},{8,0},{9,1},... | collective-permute-start | bytes 196616 | tf_op jit(solution)/shard_map/ppermute | solution.py:429
  42.4 1.0 %collective-permute-start.6 = (bf16[128,256]{1,0:T(8,128)(2,1)S(1)}, bf16[128,256]{1,0:T(8,128)(2,1)S(1)}, u32[]{:S(2)}, u32[]{:S(2)}) collective-permute-start(bf16[128,256]{1,0:T(8,128)(2,1)S(1)} %get-tuple-element.76), channel_id=1, source_target_pairs={{0,12},{1,13},{2,14},{3,15},{4,0},{5,1},{6,2},{7,3},{8,4},{9,5},{1... | collective-permute-start | bytes 196616 | tf_op jit(solution)/shard_map/ppermute | solution.py:429
  43.4 4.5 %near_0.1.refs_0_ = bf16[512,2048]{1,0:T(8,128)(2,1)S(1)} custom-call(bf16[2048,2048]{1,0:T(8,128)(2,1)S(1)} %move_1.1.d, bf16[2048,2048]{1,0:T(8,128)(2,1)S(1)} %move_0.1.x), custom_call_target="tpu_custom_call" | custom-call | flops 4294967296 | bytes 1048576 | tf_op jit(solution)/shard_map/near_0/pallas_call | solution.py:237
  47.9 0.0 collective-permute-done.4.q1
  47.9 0.0 collective-permute-done.5.q2
  47.9 1.1 %group_up.1 = (bf16[4,128,256]{2,1,0:T(8,128)(2,1)S(1)}, bf16[2,128,256]{2,1,0:T(8,128)(2,1)S(1)}, bf16[128,256]{1,0:T(8,128)(2,1)S(1)}, f32[128,256]{1,0:T(8,128)S(1)}) custom-call(s32[255]{0:T(256)S(1)} %copy-done.5, bf16[128,256]{1,0:T(8,128)(2,1)S(1)} %get-tuple-element.79.q0, bf16[128,256]{1,0:T(8,128)(2,1)S(1)} %collective-permute-done.4.q1, ...), custom_call_target="tpu_custom_call" | custom-call | flops 268435456 | bytes 1048576 | tf_op jit(solution)/shard_map/group_up/pallas_call | solution.py:61
  49.0 0.1 collective-permute-start.7
  49.1 0.7 collective-permute-start.3
  49.7 0.2 collective-permute-start.11
  49.9 0.5 collective-permute-done.7.peer
  50.4 0.6 five.1.y0
  51.0 0.0 copy-start.3
  51.0 0.0 copy-start.4
  51.0 3.1 %collective-permute-start.10 = (bf16[128,256]{1,0:T(8,128)(2,1)S(1)}, bf16[128,256]{1,0:T(8,128)(2,1)S(1)}, u32[]{:S(2)}, u32[]{:S(2)}) collective-permute-start(bf16[128,256]{1,0:T(8,128)(2,1)S(1)} %five.1.y0), channel_id=1, source_target_pairs={{0,96},{16,112},{32,64},{48,80},{64,32},{80,48},{96,0},{112,16},{1... | collective-permute-start | bytes 196616 | tf_op jit(solution)/shard_map/ppermute | solution.py:437
  54.1 0.6 collective-permute-start.9
  54.7 0.5 collective-permute-start.8
  55.2 4.5 %near_1.1.refs_1_ = bf16[512,2048]{1,0:T(8,128)(2,1)S(1)} custom-call(bf16[2048,2048]{1,0:T(8,128)(2,1)S(1)} %move_1.1.d, bf16[2048,2048]{1,0:T(8,128)(2,1)S(1)} %move_0.1.x), custom_call_target="tpu_custom_call" | custom-call | flops 4294967296 | bytes 1048576 | tf_op jit(solution)/shard_map/near_1/pallas_call | solution.py:237
  59.7 0.5 collective-permute-done.9.y2
  60.2 0.0 collective-permute-done.8.y1
  60.2 0.0 collective-permute-done.11.peer4
  60.2 2.3 %top.1 = (bf16[128,256]{1,0:T(8,128)(2,1)S(1)}, bf16[128,256]{1,0:T(8,128)(2,1)S(1)}, bf16[128,256]{1,0:T(8,128)(2,1)S(1)}, bf16[128,256]{1,0:T(8,128)(2,1)S(1)}) custom-call(s32[255]{0:T(256)S(1)} %copy-done.5, bf16[128,256]{1,0:T(8,128)(2,1)S(1)} %five.1.y0, bf16[128,256]{1,0:T(8,128)(2,1)S(1)} %collective-permute-done.8.y1, ...), custom_call_target="tpu_custom_call" | custom-call | flops 268435456 | bytes 1048576 | tf_op jit(solution)/shard_map/top/pallas_call | solution.py:61
  62.5 1.1 %collective-permute-start.12 = (bf16[128,256]{1,0:T(8,128)(2,1)S(1)}, bf16[128,256]{1,0:T(8,128)(2,1)S(1)}, u32[]{:S(2)}, u32[]{:S(2)}) collective-permute-start(bf16[128,256]{1,0:T(8,128)(2,1)S(1)} %get-tuple-element.92), channel_id=1, source_target_pairs={{0,4},{1,5},{2,6},{3,7},{4,8},{5,9},{6,10},{7,11},{8,12},{9,13},{1... | collective-permute-start | bytes 196616 | tf_op jit(solution)/shard_map/ppermute | solution.py:429
  63.6 1.4 %collective-permute-start.13 = (bf16[128,256]{1,0:T(8,128)(2,1)S(1)}, bf16[128,256]{1,0:T(8,128)(2,1)S(1)}, u32[]{:S(2)}, u32[]{:S(2)}) collective-permute-start(bf16[128,256]{1,0:T(8,128)(2,1)S(1)} %get-tuple-element.93), channel_id=1, source_target_pairs={{0,8},{1,9},{2,10},{3,11},{4,12},{5,13},{6,14},{7,15},{8,0},{9,1},... | collective-permute-start | bytes 196616 | tf_op jit(solution)/shard_map/ppermute | solution.py:429
  65.0 1.4 %collective-permute-start.14 = (bf16[128,256]{1,0:T(8,128)(2,1)S(1)}, bf16[128,256]{1,0:T(8,128)(2,1)S(1)}, u32[]{:S(2)}, u32[]{:S(2)}) collective-permute-start(bf16[128,256]{1,0:T(8,128)(2,1)S(1)} %get-tuple-element.94), channel_id=1, source_target_pairs={{0,12},{1,13},{2,14},{3,15},{4,0},{5,1},{6,2},{7,3},{8,4},{9,5},{1... | collective-permute-start | bytes 196616 | tf_op jit(solution)/shard_map/ppermute | solution.py:429
  66.4 4.5 %near_2.1.refs_2_ = bf16[512,2048]{1,0:T(8,128)(2,1)S(1)} custom-call(bf16[2048,2048]{1,0:T(8,128)(2,1)S(1)} %move_1.1.d, bf16[2048,2048]{1,0:T(8,128)(2,1)S(1)} %move_0.1.x), custom_call_target="tpu_custom_call" | custom-call | flops 4294967296 | bytes 1048576 | tf_op jit(solution)/shard_map/near_2/pallas_call | solution.py:237
  70.9 0.0 collective-permute-done.12.f1
  70.9 0.0 collective-permute-done.14.f3
  70.9 1.1 %quad_down.1 = (bf16[512,256]{1,0:T(8,128)(2,1)S(1)}, bf16[512,256]{1,0:T(8,128)(2,1)S(1)}, bf16[512,256]{1,0:T(8,128)(2,1)S(1)}, bf16[512,256]{1,0:T(8,128)(2,1)S(1)}) custom-call(s32[255]{0:T(256)S(1)} %copy-done.5, bf16[128,256]{1,0:T(8,128)(2,1)S(1)} %get-tuple-element.95.f0, bf16[128,256]{1,0:T(8,128)(2,1)S(1)} %collective-permute-done.12.f1, ...), custom_call_target="tpu_custom_call" | custom-call | flops 268435456 | bytes 1048576 | tf_op jit(solution)/shard_map/quad_down/pallas_call | solution.py:61
  72.1 0.7 collective-permute-start.15
  72.7 3.2 %collective-permute-start.16 = (bf16[512,256]{1,0:T(8,128)(2,1)S(1)}, bf16[512,256]{1,0:T(8,128)(2,1)S(1)}, u32[]{:S(2)}, u32[]{:S(2)}) collective-permute-start(bf16[512,256]{1,0:T(8,128)(2,1)S(1)} %get-tuple-element.104), channel_id=1, source_target_pairs={{0,3},{1,0},{2,1},{3,2},{4,7},{5,4},{6,5},{7,6},{8,11},{9,8},{10,9... | collective-permute-start | bytes 786440 | tf_op jit(solution)/shard_map/ppermute | solution.py:424
  76.0 0.0 collective-permute-start.17
  76.0 4.5 %near_3.1.refs_3_ = bf16[512,2048]{1,0:T(8,128)(2,1)S(1)} custom-call(bf16[2048,2048]{1,0:T(8,128)(2,1)S(1)} %move_1.1.d, bf16[2048,2048]{1,0:T(8,128)(2,1)S(1)} %move_0.1.x), custom_call_target="tpu_custom_call" | custom-call | flops 4294967296 | bytes 1048576 | tf_op jit(solution)/shard_map/near_3/pallas_call | solution.py:237
  80.5 2.7 %tail_0.1.refs_4_ = bf16[2048,2048]{1,0:T(8,128)(2,1)} custom-call(s32[255]{0:T(256)S(1)} %copy-done.5, bf16[2048,256]{1,0:T(8,128)(2,1)S(1)} %get-tuple-element.56.basis, bf16[2048,256]{1,0:T(8,128)(2,1)S(1)} %collective-permute-done.3.sibling, bf16[2,256,256]{2,1,0:T(8,128)(2,1)S(1)} %bitcast.10, bf16[512,256]{1,0:T(8,128)(2,1)S(1)} %get-tuple-element.106.far1, ...), custom_call_target="tpu_custom_call" | custom-call | flops 536870912 | bytes 3145728 | tf_op jit(solution)/shard_map/tail_0/pallas_call | solution.py:406
  83.2 2.7 %collective-permute-done.17.far1 = bf16[512,256]{1,0:T(8,128)(2,1)S(1)} collective-permute-done((bf16[512,256]{1,0:T(8,128)(2,1)S(1)}, bf16[512,256]{1,0:T(8,128)(2,1)S(1)}, u32[]{:S(2)}, u32[]{:S(2)}) %collective-permute-start.17) | collective-permute-done | bytes 262176 | tf_op jit(solution)/shard_map/ppermute | solution.py:424
  85.9 2.7 %tail_1.1.refs_4_ = bf16[2048,2048]{1,0:T(8,128)(2,1)} custom-call(s32[255]{0:T(256)S(1)} %copy-done.5, bf16[2048,256]{1,0:T(8,128)(2,1)S(1)} %get-tuple-element.56.basis, bf16[2048,256]{1,0:T(8,128)(2,1)S(1)} %collective-permute-done.3.sibling, bf16[2,256,256]{2,1,0:T(8,128)(2,1)S(1)} %bitcast.11, ...), custom_call_target="tpu_custom_call", output_to_operand_aliasing={{}: (9, {})} | custom-call | flops 536870912 | bytes 3145728 | tf_op jit(solution)/shard_map/tail_1/pallas_call | solution.py:406
  88.6 2.7 %tail_3.1.refs_4_ = bf16[2048,2048]{1,0:T(8,128)(2,1)} custom-call(s32[255]{0:T(256)S(1)} %copy-done.5, bf16[2048,256]{1,0:T(8,128)(2,1)S(1)} %get-tuple-element.56.basis, bf16[2048,256]{1,0:T(8,128)(2,1)S(1)} %collective-permute-done.3.sibling, bf16[2,256,256]{2,1,0:T(8,128)(2,1)S(1)} %bitcast.12, ...), custom_call_target="tpu_custom_call", output_to_operand_aliasing={{}: (9, {})} | custom-call | flops 536870912 | bytes 3145728 | tf_op jit(solution)/shard_map/tail_3/pallas_call | solution.py:406
  91.4 2.7 %tail_2.1 = bf16[2048,2048]{1,0:T(8,128)(2,1)} custom-call(s32[255]{0:T(256)S(1)} %copy-done.5, bf16[2048,256]{1,0:T(8,128)(2,1)S(1)} %get-tuple-element.56.basis, bf16[2048,256]{1,0:T(8,128)(2,1)S(1)} %collective-permute-done.3.sibling, bf16[2,256,256]{2,1,0:T(8,128)(2,1)S(1)} %bitcast.13, ...), custom_call_target="tpu_custom_call", output_to_operand_aliasing={{}: (9, {})} | custom-call | flops 536870912 | bytes 3145728 | tf_op jit(solution)/shard_map/tail_2/pallas_call | solution.py:406
  (18 shorter events, 0.0 us)
Async XLA Ops:
  0.0 17.5 %copy-start.6 = (s32[1,2048]{1,0:T(1,128)S(1)}, s32[1,2048]{1,0:T(1,128)}, u32[]{:S(2)}) copy-start(s32[1,2048]{1,0:T(1,128)} %order.3) | copy-start | bytes 24580
  0.0 17.5 %copy-start.1 = (bf16[1,2048,2048]{2,1,0:T(8,128)(2,1)S(1)}, bf16[1,2048,2048]{2,1,0:T(8,128)(2,1)}, u32[]{:S(2)}) copy-start(bf16[1,2048,2048]{2,1,0:T(8,128)(2,1)} %param.11) | copy-start | bytes 25165828
  11.7 24.0 %collective-permute-start = (bf16[512,256]{1,0:T(8,128)(2,1)S(1)}, bf16[512,256]{1,0:T(8,128)(2,1)S(1)}, u32[]{:S(2)}, u32[]{:S(2)}) collective-permute-start(bf16[512,256]{1,0:T(8,128)(2,1)S(1)} %get-tuple-element.58), channel_id=1, source_target_pairs={{0,1},{1,2},{2,3},{3,0},{4,5},{5,6},{6,7},{7,4},{8,9},{9,10},{10,1... | collective-permute-start | bytes 786440 | tf_op jit(solution)/shard_map/ppermute | solution.py:424
  13.3 22.3 %collective-permute-start.1 = (bf16[512,256]{1,0:T(8,128)(2,1)S(1)}, bf16[512,256]{1,0:T(8,128)(2,1)S(1)}, u32[]{:S(2)}, u32[]{:S(2)}) collective-permute-start(bf16[512,256]{1,0:T(8,128)(2,1)S(1)} %get-tuple-element.59), channel_id=1, source_target_pairs={{0,2},{1,3},{2,0},{3,1},{4,6},{5,7},{6,4},{7,5},{8,10},{9,11},{10,... | collective-permute-start | bytes 786440 | tf_op jit(solution)/shard_map/ppermute | solution.py:424
  16.1 19.6 %collective-permute-start.2 = (bf16[512,256]{1,0:T(8,128)(2,1)S(1)}, bf16[512,256]{1,0:T(8,128)(2,1)S(1)}, u32[]{:S(2)}, u32[]{:S(2)}) collective-permute-start(bf16[512,256]{1,0:T(8,128)(2,1)S(1)} %get-tuple-element.60), channel_id=1, source_target_pairs={{0,3},{1,0},{2,1},{3,2},{4,7},{5,4},{6,5},{7,6},{8,11},{9,8},{10,9... | collective-permute-start | bytes 786440 | tf_op jit(solution)/shard_map/ppermute | solution.py:424
  26.6 9.1 %copy-start = (bf16[1,15,2,256,256]{4,3,2,1,0:T(8,128)(2,1)S(1)}, bf16[1,15,2,256,256]{4,3,2,1,0:T(8,128)(2,1)}, u32[]{:S(2)}) copy-start(bf16[1,15,2,256,256]{4,3,2,1,0:T(8,128)(2,1)} %param.14) | copy-start | bytes 11796484
  26.6 9.1 %copy-start.5 = (s32[255]{0:T(256)S(1)}, s32[255]{0:T(256)}, u32[]{:S(2)}) copy-start(s32[255]{0:T(256)} %ranks.17) | copy-start | bytes 3064
  36.8 11.1 %collective-permute-start.4 = (bf16[128,256]{1,0:T(8,128)(2,1)S(1)}, bf16[128,256]{1,0:T(8,128)(2,1)S(1)}, u32[]{:S(2)}, u32[]{:S(2)}) collective-permute-start(bf16[128,256]{1,0:T(8,128)(2,1)S(1)} %get-tuple-element.74), channel_id=1, source_target_pairs={{0,4},{1,5},{2,6},{3,7},{4,8},{5,9},{6,10},{7,11},{8,12},{9,13},{1... | collective-permute-start | bytes 196616 | tf_op jit(solution)/shard_map/ppermute | solution.py:429
  38.8 9.1 %collective-permute-start.5 = (bf16[128,256]{1,0:T(8,128)(2,1)S(1)}, bf16[128,256]{1,0:T(8,128)(2,1)S(1)}, u32[]{:S(2)}, u32[]{:S(2)}) collective-permute-start(bf16[128,256]{1,0:T(8,128)(2,1)S(1)} %get-tuple-element.75), channel_id=1, source_target_pairs={{0,8},{1,9},{2,10},{3,11},{4,12},{5,13},{6,14},{7,15},{8,0},{9,1},... | collective-permute-start | bytes 196616 | tf_op jit(solution)/shard_map/ppermute | solution.py:429
  42.4 5.5 %collective-permute-start.6 = (bf16[128,256]{1,0:T(8,128)(2,1)S(1)}, bf16[128,256]{1,0:T(8,128)(2,1)S(1)}, u32[]{:S(2)}, u32[]{:S(2)}) collective-permute-start(bf16[128,256]{1,0:T(8,128)(2,1)S(1)} %get-tuple-element.76), channel_id=1, source_target_pairs={{0,12},{1,13},{2,14},{3,15},{4,0},{5,1},{6,2},{7,3},{8,4},{9,5},{1... | collective-permute-start | bytes 196616 | tf_op jit(solution)/shard_map/ppermute | solution.py:429
  49.0 1.4 %collective-permute-start.7 = (f32[128,256]{1,0:T(8,128)S(1)}, f32[128,256]{1,0:T(8,128)S(1)}, u32[]{:S(2)}, u32[]{:S(2)}) collective-permute-start(f32[128,256]{1,0:T(8,128)S(1)} %get-tuple-element.83.own), channel_id=1, source_target_pairs={{0,16},{16,0},{32,48},{48,32},{64,80},{80,64},{96,112},{112,96},{1... | collective-permute-start | bytes 393224 | tf_op jit(solution)/shard_map/ppermute | solution.py:437
  49.1 31.4 %collective-permute-start.3 = (bf16[2048,256]{1,0:T(8,128)(2,1)S(1)}, bf16[2048,256]{1,0:T(8,128)(2,1)S(1)}, u32[]{:S(2)}, u32[]{:S(2)}) collective-permute-start(bf16[2048,256]{1,0:T(8,128)(2,1)S(1)} %get-tuple-element.72), channel_id=1, source_target_pairs={{0,1},{1,0},{2,3},{3,2},{4,5},{5,4},{6,7},{7,6},{8,9},{9,8},{10,11... | collective-permute-start | bytes 3145736 | tf_op jit(solution)/shard_map/ppermute | solution.py:433
  49.7 10.4 %collective-permute-start.11 = (bf16[128,256]{1,0:T(8,128)(2,1)S(1)}, bf16[128,256]{1,0:T(8,128)(2,1)S(1)}, u32[]{:S(2)}, u32[]{:S(2)}) collective-permute-start(bf16[128,256]{1,0:T(8,128)(2,1)S(1)} %get-tuple-element.88), channel_id=1, source_target_pairs={{0,16},{16,0},{32,48},{48,32},{64,80},{80,64},{96,112},{112,96},{1... | collective-permute-start | bytes 196616 | tf_op jit(solution)/shard_map/ppermute | solution.py:437
  51.0 9.2 %copy-start.3 = (bf16[6,2,256,256]{3,2,1,0:T(8,128)(2,1)S(1)}, bf16[6,2,256,256]{3,2,1,0:T(8,128)(2,1)}, u32[]{:S(2)}) copy-start(bf16[6,2,256,256]{3,2,1,0:T(8,128)(2,1)} %outer.1) | copy-start | bytes 4718596
  51.0 9.2 %copy-start.4 = (bf16[256,256]{1,0:T(8,128)(2,1)S(1)}, bf16[256,256]{1,0:T(8,128)(2,1)}, u32[]{:S(2)}) copy-start(bf16[256,256]{1,0:T(8,128)(2,1)} %root.1) | copy-start | bytes 393220
  51.0 8.7 %collective-permute-start.10 = (bf16[128,256]{1,0:T(8,128)(2,1)S(1)}, bf16[128,256]{1,0:T(8,128)(2,1)S(1)}, u32[]{:S(2)}, u32[]{:S(2)}) collective-permute-start(bf16[128,256]{1,0:T(8,128)(2,1)S(1)} %five.1.y0), channel_id=1, source_target_pairs={{0,96},{16,112},{32,64},{48,80},{64,32},{80,48},{96,0},{112,16},{1... | collective-permute-start | bytes 196616 | tf_op jit(solution)/shard_map/ppermute | solution.py:437
  54.1 6.1 %collective-permute-start.9 = (bf16[128,256]{1,0:T(8,128)(2,1)S(1)}, bf16[128,256]{1,0:T(8,128)(2,1)S(1)}, u32[]{:S(2)}, u32[]{:S(2)}) collective-permute-start(bf16[128,256]{1,0:T(8,128)(2,1)S(1)} %five.1.y0), channel_id=1, source_target_pairs={{0,64},{16,80},{32,96},{48,112},{64,0},{80,16},{96,32},{112,48},{1... | collective-permute-start | bytes 196616 | tf_op jit(solution)/shard_map/ppermute | solution.py:437
  54.7 5.4 %collective-permute-start.8 = (bf16[128,256]{1,0:T(8,128)(2,1)S(1)}, bf16[128,256]{1,0:T(8,128)(2,1)S(1)}, u32[]{:S(2)}, u32[]{:S(2)}) collective-permute-start(bf16[128,256]{1,0:T(8,128)(2,1)S(1)} %five.1.y0), channel_id=1, source_target_pairs={{0,32},{16,48},{32,0},{48,16},{64,96},{80,112},{96,64},{112,80},{1... | collective-permute-start | bytes 196616 | tf_op jit(solution)/shard_map/ppermute | solution.py:437
  62.5 8.3 %collective-permute-start.12 = (bf16[128,256]{1,0:T(8,128)(2,1)S(1)}, bf16[128,256]{1,0:T(8,128)(2,1)S(1)}, u32[]{:S(2)}, u32[]{:S(2)}) collective-permute-start(bf16[128,256]{1,0:T(8,128)(2,1)S(1)} %get-tuple-element.92), channel_id=1, source_target_pairs={{0,4},{1,5},{2,6},{3,7},{4,8},{5,9},{6,10},{7,11},{8,12},{9,13},{1... | collective-permute-start | bytes 196616 | tf_op jit(solution)/shard_map/ppermute | solution.py:429
  63.6 7.3 %collective-permute-start.13 = (bf16[128,256]{1,0:T(8,128)(2,1)S(1)}, bf16[128,256]{1,0:T(8,128)(2,1)S(1)}, u32[]{:S(2)}, u32[]{:S(2)}) collective-permute-start(bf16[128,256]{1,0:T(8,128)(2,1)S(1)} %get-tuple-element.93), channel_id=1, source_target_pairs={{0,8},{1,9},{2,10},{3,11},{4,12},{5,13},{6,14},{7,15},{8,0},{9,1},... | collective-permute-start | bytes 196616 | tf_op jit(solution)/shard_map/ppermute | solution.py:429
  65.0 5.9 %collective-permute-start.14 = (bf16[128,256]{1,0:T(8,128)(2,1)S(1)}, bf16[128,256]{1,0:T(8,128)(2,1)S(1)}, u32[]{:S(2)}, u32[]{:S(2)}) collective-permute-start(bf16[128,256]{1,0:T(8,128)(2,1)S(1)} %get-tuple-element.94), channel_id=1, source_target_pairs={{0,12},{1,13},{2,14},{3,15},{4,0},{5,1},{6,2},{7,3},{8,4},{9,5},{1... | collective-permute-start | bytes 196616 | tf_op jit(solution)/shard_map/ppermute | solution.py:429
  72.1 19.3 %collective-permute-start.15 = (bf16[512,256]{1,0:T(8,128)(2,1)S(1)}, bf16[512,256]{1,0:T(8,128)(2,1)S(1)}, u32[]{:S(2)}, u32[]{:S(2)}) collective-permute-start(bf16[512,256]{1,0:T(8,128)(2,1)S(1)} %get-tuple-element.100), channel_id=1, source_target_pairs={{0,2},{1,3},{2,0},{3,1},{4,6},{5,7},{6,4},{7,5},{8,10},{9,11},{10,... | collective-permute-start | bytes 786440 | tf_op jit(solution)/shard_map/ppermute | solution.py:424
  72.7 15.9 %collective-permute-start.16 = (bf16[512,256]{1,0:T(8,128)(2,1)S(1)}, bf16[512,256]{1,0:T(8,128)(2,1)S(1)}, u32[]{:S(2)}, u32[]{:S(2)}) collective-permute-start(bf16[512,256]{1,0:T(8,128)(2,1)S(1)} %get-tuple-element.104), channel_id=1, source_target_pairs={{0,3},{1,0},{2,1},{3,2},{4,7},{5,4},{6,5},{7,6},{8,11},{9,8},{10,9... | collective-permute-start | bytes 786440 | tf_op jit(solution)/shard_map/ppermute | solution.py:424
  76.0 4.5 %copy-start.2 = (bf16[1,2,256,256]{3,2,1,0:T(8,128)(2,1)S(1)}, bf16[1,2,256,256]{3,2,1,0:T(8,128)(2,1)}, u32[]{:S(2)}) copy-start(bf16[1,2,256,256]{3,2,1,0:T(8,128)(2,1)} %param.13) | copy-start | bytes 786436
  76.0 10.0 %collective-permute-start.17 = (bf16[512,256]{1,0:T(8,128)(2,1)S(1)}, bf16[512,256]{1,0:T(8,128)(2,1)S(1)}, u32[]{:S(2)}, u32[]{:S(2)}) collective-permute-start(bf16[512,256]{1,0:T(8,128)(2,1)S(1)} %get-tuple-element.105), channel_id=1, source_target_pairs={{0,1},{1,2},{2,3},{3,0},{4,5},{5,6},{6,7},{7,4},{8,9},{9,10},{10,1... | collective-permute-start | bytes 786440 | tf_op jit(solution)/shard_map/ppermute | solution.py:424

commit v2 on v1

--- a/solution.py
+++ b/solution.py
@@ -107,10 +107,9 @@
     cols = piece.shape[0]
     start = pl.multiple_of(lax.rem(ring + shift, RING) * cols, cols)
     rank = ranks[127 + outer * 16 + z * RING + ring]
-    for j in range(0, cols, 256):
-        c = masked(nn(basis_t[...], x[:, pl.ds(start + j, 256)]).T, rank)
-        coef[pl.ds(start + j, 256), :] = c
-        piece[j : j + 256] = nn(c, transfer[...]).astype(BF)
+    c = masked(nn(basis_t[...], x[:, pl.ds(start, cols)]).T, rank)
+    coef[pl.ds(start, cols), :] = c
+    piece[...] = nn(c, transfer[...]).astype(BF)
 
 
 def front_kernel(
@@ -169,58 +168,79 @@
     )
 
 
-PITCH = 9
-
-
-def move_kernel(scatter, order, x, o, src, dst):
+PITCH = 17
+
+
+def move_rows(scatter, order, x, src, dst):
     rows = x.shape[0]
-
-    for half in range(x.shape[1] // 1024):
-
-        @pl.loop(0, rows // 32)
-        def _(b):
-            for r in range(2):
-                base = (b * 32 + r * 16) * PITCH
-                start = pl.multiple_of(b * 32 + r * 16, 16)
-                for t in range(8):
-                    at = half * 1024 + t * 128
-                    v = x[pl.ds(start, 16), at : at + 128].astype(F32)
-                    src[pl.ds(base + t, 8, stride=PITCH), :] = v[:8]
-                    src[pl.ds(base + 8 * PITCH + t, 8, stride=PITCH), :] = v[8:]
-
-        @pl.loop(0, rows // 64)
-        def _(i):
-            for j in range(64):
-                far_at = order[0, i * 64 + j] * PITCH
-                near_at = i * (64 * PITCH) + j * PITCH
-                s, d = (near_at, far_at) if scatter else (far_at, near_at)
-                dst[pl.ds(d, 8), :] = src[pl.ds(s, 8), :]
-
-        @pl.loop(0, rows // 32)
-        def _(b):
-            for r in range(2):
-                base = (b * 32 + r * 16) * PITCH
-                start = pl.multiple_of(b * 32 + r * 16, 16)
-                for t in range(8):
-                    lo = dst[pl.ds(base + t, 8, stride=PITCH), :]
-                    hi = dst[pl.ds(base + 8 * PITCH + t, 8, stride=PITCH), :]
-                    at = half * 1024 + t * 128
-                    v = jnp.concatenate([lo, hi], axis=0).astype(BF)
-                    o[pl.ds(start, 16), at : at + 128] = v
-
-
-def move_rows(scatter, order, x):
+    tiles = x.shape[1] // 128
+
+    @pl.loop(0, rows // 32)
+    def _(b):
+        for r in range(2):
+            base = (b * 32 + r * 16) * PITCH
+            start = pl.multiple_of(b * 32 + r * 16, 16)
+            for t in range(tiles):
+                v = x[pl.ds(start, 16), t * 128 : (t + 1) * 128].astype(F32)
+                src[pl.ds(base + t, 8, stride=PITCH), :] = v[:8]
+                src[pl.ds(base + 8 * PITCH + t, 8, stride=PITCH), :] = v[8:]
+
+    @pl.loop(0, rows // 64)
+    def _(i):
+        for j in range(64):
+            far_at = order[0, i * 64 + j]
+            near_at = i * (64 * PITCH) + j * PITCH
+            s, d = (near_at, far_at) if scatter else (far_at, near_at)
+            for h in range(0, tiles, 8):
+                dst[pl.ds(d + h, 8), :] = src[pl.ds(s + h, 8), :]
+
+    @pl.loop(0, rows // 32)
+    def _(b):
+        for r in range(2):
+            base = (b * 32 + r * 16) * PITCH
+            start = pl.multiple_of(b * 32 + r * 16, 16)
+            for t in range(tiles):
+                lo = dst[pl.ds(base + t, 8, stride=PITCH), :]
+                hi = dst[pl.ds(base + 8 * PITCH + t, 8, stride=PITCH), :]
+                v = jnp.concatenate([lo, hi], axis=0).astype(BF)
+                x[pl.ds(start, 16), t * 128 : (t + 1) * 128] = v
+
+
+def move_kernel(order, x_in, diag_hbm, x, diag, src, dst, scaled, row_at, sem):
+    size = diag.shape[0] // 4
+    loads = []
+    for k in range(4):
+        part = pl.ds(k * size, size)
+        loads.append(pltpu.make_async_copy(diag_hbm.at[part], diag.at[part], sem.at[k]))
+        loads[k].start()
+    scaled[...] = order[...] * PITCH
+    load = pltpu.make_async_copy(scaled, row_at, sem.at[4])
+    load.start()
+    load.wait()
+    move_rows(False, row_at, x, src, dst)
+    for load in loads:
+        load.wait()
+    move_rows(True, row_at, diag, src, dst)
+
+
+def move_both(order, x, diag):
     rows, cols = x.shape
     return pl.pallas_call(
-        functools.partial(move_kernel, scatter),
-        out_shape=held(rows, cols),
-        in_specs=[SMEM, VMEM],
-        out_specs=VMEM,
-        scratch_shapes=[pltpu.VMEM((rows * PITCH, 128), F32)] * 2,
-        compiler_params=params(22 * 2**20),
-        cost_estimate=cost(0, 18 * 2**20),
-        name=f"move_{int(scatter)}",
-    )(order, pin(x))
+        move_kernel,
+        out_shape=(held(rows, cols), held(rows, cols)),
+        in_specs=[VMEM, VMEM, HBM],
+        out_specs=(VMEM, VMEM),
+        input_output_aliases={1: 0},
+        scratch_shapes=[pltpu.VMEM((rows * PITCH, 128), F32)] * 2
+        + [
+            pltpu.VMEM(order.shape, jnp.int32),
+            pltpu.SMEM(order.shape, jnp.int32),
+            pltpu.SemaphoreType.DMA((5,)),
+        ],
+        compiler_params=params(37 * 2**20),
+        cost_estimate=cost(0, 40 * 2**20),
+        name="move",
+    )(pin(order), pin(x), pin(diag, pltpu.HBM))
 
 
 def near_kernel(first, d, x, out):
@@ -230,18 +250,17 @@
         out[:, j : j + 256] = nn(d[first : first + size], x[:, j : j + 256]).astype(BF)
 
 
-def near_rows(piece, pieces, diag, ordered):
+def near_rows(first, size, diag, ordered):
     rows, depth = diag.shape
     cols = ordered.shape[1]
-    size = rows // pieces
     return pl.pallas_call(
-        functools.partial(near_kernel, piece * size),
+        functools.partial(near_kernel, first),
         out_shape=held(size, cols),
         in_specs=[VMEM] * 2,
         out_specs=VMEM,
         compiler_params=params(8 * 2**20),
         cost_estimate=cost(2 * size * depth * cols, 2**20),
-        name=f"near_{piece}",
+        name=f"near_{first}",
     )(pin(diag), pin(ordered))
 
 
@@ -271,7 +290,7 @@
     )
 
 
-def group_up_kernel(ranks, q0, q1, q2, q3, inner, out2, out3, out4, lift):
+def group_up_kernel(ranks, q0, q1, q2, q3, inner, out2, out3, lift):
     x, z, group = place()
     for t, ref in enumerate((q0, q1, q2, q3)):
         out2[(z - t) & 3] = ref[...]
@@ -279,8 +298,9 @@
         up = nn(out2[2 * k], inner[8 + 2 * k, 0]) + nn(out2[2 * k + 1], inner[9 + 2 * k, 0])
         out3[k] = masked(up, ranks[15 + 2 * group + k])
     up = nn(out3[0], inner[12, 0]) + nn(out3[1], inner[13, 0])
-    out4[...] = masked(up, ranks[7 + group])
-    lift[...] = nn(out4[...], inner[14, 0])
+    four = masked(up, ranks[7 + group])
+    lift[0] = four.astype(F32)
+    lift[1] = nn(four, inner[14, 0])
 
 
 def group_up(ranks, pieces, inner):
@@ -291,19 +311,18 @@
         (
             held(4, part, width),
             held(2, part, width),
-            held(part, width),
-            pltpu.VMEM((part, width), F32),
+            pltpu.VMEM((2, part, width), F32),
         ),
         (ranks, *map(pin, pieces), pin(inner)),
     )
 
 
 def five_kernel(ranks, own, peer, out):
-    out[...] = masked(own[...] + peer[...], ranks[3 + (place()[2] >> 1)])
+    out[...] = masked(own[1] + peer[1], ranks[3 + (place()[2] >> 1)])
 
 
 def five_up(ranks, own, peer):
-    return call(five_kernel, "five", held(*own.shape), (ranks, pin(own), pin(peer)))
+    return call(five_kernel, "five", held(*own.shape[1:]), (ranks, pin(own), pin(peer)))
 
 
 def top_kernel(
@@ -324,7 +343,7 @@
     sib = jnp.where(half == 0, six[1].astype(F32), six[0].astype(F32)).astype(BF)
     far = masked(nt(sib, outer[4 + half, 1]) + nt(far, outer[4 + half, 0]), ranks[1 + half])
     far = masked(nt(five[y ^ 1], outer[y, 1]) + nt(far, outer[y, 0]), ranks[3 + y])
-    far = masked(nt(peer4[...], inner[14, 1]) + nt(far, inner[14, 0]), ranks[7 + group])
+    far = masked(nt(peer4[0].astype(BF), inner[14, 1]) + nt(far, inner[14, 0]), ranks[7 + group])
     for k in range(2):
         down = nt(c3[1 - k], inner[12 + k, 1]) + nt(far, inner[12 + k, 0])
         far3 = masked(down, ranks[15 + 2 * group + k])
@@ -371,51 +390,58 @@
     )
 
 
-def tail_kernel(shift, ranks, basis, sibling, node, far1, *refs):
-    nears = refs[:4]
+TAIL = 256
+
+
+def tail_kernel(shifts, starts, ranks, basis, sibling, node, *refs):
+    fars = refs[: len(shifts)]
+    nears = refs[len(shifts) : len(shifts) + len(starts)]
     o_hbm, buf, sem = refs[-3:]
     x, z, outer = place()
-    cols = far1.shape[0]
-    size = nears[0].shape[0]
-    at = pl.ds(pl.multiple_of(((x - shift) & 3) * cols, cols), cols)
-
-    def put(k):
-        return pltpu.make_async_copy(buf.at[k], o_hbm.at[pl.ds(k * size, size), at], sem.at[k])
-
-    down = nt(sibling[at, :], node[1]) + nt(far1[...], node[0])
-    far = masked(down, ranks[127 + outer * 16 + z * RING + x])
-    for k, near in enumerate(nears):
-        add = nt(basis[k * size : (k + 1) * size], far)
-        buf[k] = (near[:, at].astype(F32) + add).astype(BF)
-        put(k).start()
-    for k in range(len(nears)):
-        put(k).wait()
-
-
-def add_far(shift, ranks, basis, sibling, node, far1, nears, sofar):
+    cols = fars[0].shape[0]
+    rank = ranks[127 + outer * 16 + z * RING + x]
+    copies = []
+    for i, (shift, far1) in enumerate(zip(shifts, fars)):
+        at = pl.ds(pl.multiple_of(((x - shift) & 3) * cols, cols), cols)
+        down = nt(sibling[at, :], node[1]) + nt(far1[...], node[0])
+        far = masked(down, rank)
+        for first, near in zip(starts, nears):
+            for r in range(0, near.shape[0], TAIL):
+                row = first + r
+                add = nt(basis[row : row + TAIL], far)
+                buf[i, row : row + TAIL] = (near[r : r + TAIL, at].astype(F32) + add).astype(BF)
+                copy = pltpu.make_async_copy(
+                    buf.at[i, pl.ds(row, TAIL)], o_hbm.at[pl.ds(row, TAIL), at], sem.at[len(copies)]
+                )
+                copy.start()
+                copies.append(copy)
+    for copy in copies:
+        copy.wait()
+
+
+def add_far(shifts, starts, ranks, basis, sibling, node, fars, nears, sofar):
     rows, width = basis.shape
-    cols = far1.shape[0]
-    count = len(nears)
-    args = [ranks] + [pin(a) for a in (basis, sibling, node, far1, *nears)]
-    specs = [SMEM] + [VMEM] * (4 + count)
+    cols = fars[0].shape[0]
+    args = [ranks] + [pin(a) for a in (basis, sibling, node, *fars, *nears)]
+    specs = [SMEM] + [VMEM] * (len(args) - 1)
     alias = {}
     if sofar is not None:
         alias = {len(args): 0}
         args.append(sofar)
         specs.append(HBM)
     return pl.pallas_call(
-        functools.partial(tail_kernel, shift),
+        functools.partial(tail_kernel, shifts, starts),
         out_shape=sds(rows, nears[0].shape[1]),
         in_specs=specs,
         out_specs=HBM,
         input_output_aliases=alias,
         scratch_shapes=[
-            pltpu.VMEM((count, rows // count, cols), BF),
-            pltpu.SemaphoreType.DMA((count,)),
+            pltpu.VMEM((len(shifts), rows, cols), BF),
+            pltpu.SemaphoreType.DMA((len(shifts) * rows // TAIL,)),
         ],
-        compiler_params=params(8 * 2**20),
+        compiler_params=params(12 * 2**20),
         cost_estimate=cost(2 * rows * width * cols, 3 * 2**20),
-        name=f"tail_{shift}",
+        name="tail_" + "".join(map(str, shifts)),
     )(*args)
 
 
@@ -461,33 +487,32 @@
 
     basis, x, coef, *pieces = front(leaf_order, ranks, leaf_basis[0], points, node)
     pieces = exchange(ring_x, pieces)
-    ordered = move_rows(False, leaf_order, x)
-    diag = move_rows(True, leaf_order, diag_blocks[0])
+    ordered, diag = move_both(leaf_order, x, diag_blocks[0])
     *pieces, ordered, diag, coef = lax.optimization_barrier((*pieces, ordered, diag, coef))
 
     mid, *parts = quad_up(ranks, pieces, inner)
     coef, *parts = lax.optimization_barrier((coef, *parts))
     parts = exchange(ring_z, parts)
     sibling = swap_inner(coef, 1)
-    nears = [near_rows(0, 4, diag, ordered)]
+    starts = (0, 256, 768, 1024)
+    nears = [near_rows(0, 256, diag, ordered)]
     *parts, nears[0] = lax.optimization_barrier((*parts, nears[0]))
-    c2, c3, c4, lift = group_up(ranks, parts, inner)
-    peer4 = swap_outer(c4, 1)
-    five = five_up(ranks, lift, swap_outer(lift, 1))
+    c2, c3, lift = group_up(ranks, parts, inner)
+    peer = swap_outer(lift, 1)
+    five = five_up(ranks, lift, peer)
     fives = [five] + [swap_outer(five, 2 * s) for s in (1, 2, 3)]
-    nears.append(near_rows(1, 4, diag, ordered))
+    nears.append(near_rows(256, 512, diag, ordered))
     *fives, nears[1] = lax.optimization_barrier((*fives, nears[1]))
-    parts = top_sweep(ranks, fives, peer4, c2, c3, inner, outer_nodes, root_coupling)
+    parts = top_sweep(ranks, fives, peer, c2, c3, inner, outer_nodes, root_coupling)
     parts = exchange(ring_z, parts)
-    nears.append(near_rows(2, 4, diag, ordered))
-    *parts, nears[2] = lax.optimization_barrier((*parts, nears[2]))
+    nears.append(near_rows(768, 256, diag, ordered))
+    *parts, nears[2], sibling = lax.optimization_barrier((*parts, nears[2], sibling))
     fars = quad_down(ranks, parts, mid, inner)
     fars = exchange(ring_x, fars)
-    nears.append(near_rows(3, 4, diag, ordered))
-    out = None
-    for s in (0, 1, 3, 2):
-        out = add_far(s, ranks, basis, sibling, node, fars[s], nears, out)
-    return out
+    nears.append(near_rows(1024, 1024, diag, ordered))
+    add = functools.partial(add_far, starts=starts, ranks=ranks, basis=basis, sibling=sibling, node=node)
+    out = add((0, 1, 3), fars=[fars[s] for s in (0, 1, 3)], nears=nears, sofar=None)
+    return add((2,), fars=[fars[2]], nears=nears, sofar=out)
 
 
 def solution(mesh):

time: 94.3 us -> 81.7 us (0.87)
  Pallas kernels: 64.8 us -> 50.6 us
  starting transfers between devices: 25.2 us -> 26.9 us
    pallas_call x10 -> x7, Pallas kernels: 46.9 us -> 35.5 us  [the longest x4 17.9 us: near_rows(): pl.pallas_call(functools.partial(near_kernel, first), out_shape=held(size...]
    pallas_call x6, Pallas kernels: 17.9 us -> 15.1 us  [call(): pl.pallas_call(kernel, out_shape=out_shapes, in_specs=specs or [SMEM] + [...]
    ppermute x6, waiting for transfers between devices: 2.74 us -> 0.02 us  [ring_x(): return lax.ppermute(block, 'inner', route)]
    ppermute x6, waiting for transfers between devices: 0.02 us -> 1.47 us  [ring_z(): return lax.ppermute(block, 'inner', route)]
    ppermute x5 -> x4, waiting for transfers between devices: 1 us -> 2.26 us  [swap_outer(): lax.ppermute(block, 'outer', [(o, o ^ bits) for o in range(2 * RING)])]
    ppermute x5 -> x4, starting transfers between devices: 4.41 us -> 4.86 us  [swap_outer(): lax.ppermute(block, 'outer', [(o, o ^ bits) for o in range(2 * RING)])]
  transfers between devices with their start and end apart: 18 -> 17, of which waited for: 3 -> 4; matrix products, arithmetic and copies ran while one was open for 0% -> 0% of each run, Pallas kernels for 51% -> 45%
where the time goes in v2:
time: 81.7 us; the launch traced here: 81.6 us
  Pallas kernels  50.6 us (62%)
  starting transfers between devices  26.9 us (33%)
  waiting for transfers between devices  3.75 us (5%)
    pallas_call x4, Pallas kernels, near_rows(): pl.pallas_call(functools.partial(near_kernel, first), out_shape=held(size...  17.9 us
    pallas_call x6, Pallas kernels, call(): pl.pallas_call(kernel, out_shape=out_shapes, in_specs=specs or [SMEM] + [...  15.1 us
    ppermute x6, starting transfers between devices, ring_z(): return lax.ppermute(block, 'inner', route)  10.6 us
    pallas_call x1, Pallas kernels, move_both(): pl.pallas_call(move_kernel, out_shape=(held(rows, cols), held(rows, cols)...  10.4 us
    ppermute x6, starting transfers between devices, ring_x(): return lax.ppermute(block, 'inner', route)  10.3 us
    pallas_call x2, Pallas kernels, add_far(): pl.pallas_call(functools.partial(tail_kernel, shifts, starts), out_shape=...  7.19 us
    ppermute x4, starting transfers between devices, swap_outer(): lax.ppermute(block, 'outer', [(o, o ^ bits) for o in range(2 * RING)])  4.86 us
    ppermute x4, waiting for transfers between devices, swap_outer(): lax.ppermute(block, 'outer', [(o, o ^ bits) for o in range(2 * RING)])  2.26 us
  transfers between devices with their start and end apart: 17, of which 4 were waited for; matrix products, arithmetic and copies ran while one was open for 0% of the time, Pallas kernels for 45%

profile of v2, /device:TPU:0, one launch (start us, length us, event | category | flops | bytes accessed | tf_op | source)
XLA Modules:
  0.0 81.6 jit_solution(1096027137754222875)
XLA Ops:
  0.0 8.8 %front.1 = (bf16[2048,256]{1,0:T(8,128)(2,1)S(1)}, bf16[2048,2048]{1,0:T(8,128)(2,1)S(1)}, bf16[2048,256]{1,0:T(8,128)(2,1)S(1)}, bf16[512,256]{1,0:T(8,128)(2,1...) custom-call(s32[1,2048]{1,0:T(1,128)} %order.1, s32[255]{0:T(256)} %ranks.13, ...), custom_call_target="tpu_custom_call" | custom-call | flops 2147483648 | bytes 1048576 | tf_op jit(solution)/shard_map/front/pallas_call | solution.py:61
  8.8 1.6 %collective-permute-start = (bf16[512,256]{1,0:T(8,128)(2,1)S(1)}, bf16[512,256]{1,0:T(8,128)(2,1)S(1)}, u32[]{:S(2)}, u32[]{:S(2)}) collective-permute-start(bf16[512,256]{1,0:T(8,128)(2,1)S(1)} %get-tuple-element.60), channel_id=1, source_target_pairs={{0,1},{1,2},{2,3},{3,0},{4,5},{5,6},{6,7},{7,4},{8,9},{9,10},{10,1... | collective-permute-start | bytes 786440 | tf_op jit(solution)/shard_map/ppermute | solution.py:450
  10.5 2.7 %collective-permute-start.1 = (bf16[512,256]{1,0:T(8,128)(2,1)S(1)}, bf16[512,256]{1,0:T(8,128)(2,1)S(1)}, u32[]{:S(2)}, u32[]{:S(2)}) collective-permute-start(bf16[512,256]{1,0:T(8,128)(2,1)S(1)} %get-tuple-element.61), channel_id=1, source_target_pairs={{0,2},{1,3},{2,0},{3,1},{4,6},{5,7},{6,4},{7,5},{8,10},{9,11},{10,... | collective-permute-start | bytes 786440 | tf_op jit(solution)/shard_map/ppermute | solution.py:450
  13.2 1.4 %collective-permute-start.2 = (bf16[512,256]{1,0:T(8,128)(2,1)S(1)}, bf16[512,256]{1,0:T(8,128)(2,1)S(1)}, u32[]{:S(2)}, u32[]{:S(2)}) collective-permute-start(bf16[512,256]{1,0:T(8,128)(2,1)S(1)} %get-tuple-element.62), channel_id=1, source_target_pairs={{0,3},{1,0},{2,1},{3,2},{4,7},{5,4},{6,5},{7,6},{8,11},{9,8},{10,9... | collective-permute-start | bytes 786440 | tf_op jit(solution)/shard_map/ppermute | solution.py:450
  14.7 10.4 %move.1 = (bf16[2048,2048]{1,0:T(8,128)(2,1)S(1)}, bf16[2048,2048]{1,0:T(8,128)(2,1)S(1)}) custom-call(s32[1,2048]{1,0:T(1,128)S(1)} %copy-done.5, bf16[2048,2048]{1,0:T(8,128)(2,1)S(1)} %get-tuple-element.63.x_in, bf16[2048,2048]{1,0:T(8,128)(2,1)} %bitcast.11), custom_call_target="tpu_custom_call", output_to_operand_aliasing={{0}: (1, {})} | custom-call | bytes 41943040 | tf_op jit(solution)/shard_map/move/pallas_call | solution.py:228
  25.1 0.0 collective-permute-done.u1
  25.1 0.0 collective-permute-done.1.u2
  25.1 0.0 collective-permute-done.2.u3
  25.1 1.1 %quad_up.1 = (bf16[2,512,256]{2,1,0:T(8,128)(2,1)S(1)}, bf16[128,256]{1,0:T(8,128)(2,1)S(1)}, bf16[128,256]{1,0:T(8,128)(2,1)S(1)}, bf16[128,256]{1,0:T(8,128)(2,1)S(1)}, bf16[128,256]{1,0:T(8,128)(2,1)S(1)}) custom-call(s32[255]{0:T(256)S(1)} %copy-done.4, bf16[512,256]{1,0:T(8,128)(2,1)S(1)} %get-tuple-element.68.u0, ...), custom_call_target="tpu_custom_call" | custom-call | flops 268435456 | bytes 1048576 | tf_op jit(solution)/shard_map/quad_up/pallas_call | solution.py:61
  26.2 2.0 %collective-permute-start.3 = (bf16[128,256]{1,0:T(8,128)(2,1)S(1)}, bf16[128,256]{1,0:T(8,128)(2,1)S(1)}, u32[]{:S(2)}, u32[]{:S(2)}) collective-permute-start(bf16[128,256]{1,0:T(8,128)(2,1)S(1)} %get-tuple-element.77), channel_id=1, source_target_pairs={{0,4},{1,5},{2,6},{3,7},{4,8},{5,9},{6,10},{7,11},{8,12},{9,13},{1... | collective-permute-start | bytes 196616 | tf_op jit(solution)/shard_map/ppermute | solution.py:455
  28.2 3.6 %collective-permute-start.4 = (bf16[128,256]{1,0:T(8,128)(2,1)S(1)}, bf16[128,256]{1,0:T(8,128)(2,1)S(1)}, u32[]{:S(2)}, u32[]{:S(2)}) collective-permute-start(bf16[128,256]{1,0:T(8,128)(2,1)S(1)} %get-tuple-element.78), channel_id=1, source_target_pairs={{0,8},{1,9},{2,10},{3,11},{4,12},{5,13},{6,14},{7,15},{8,0},{9,1},... | collective-permute-start | bytes 196616 | tf_op jit(solution)/shard_map/ppermute | solution.py:455
  31.8 1.0 %collective-permute-start.5 = (bf16[128,256]{1,0:T(8,128)(2,1)S(1)}, bf16[128,256]{1,0:T(8,128)(2,1)S(1)}, u32[]{:S(2)}, u32[]{:S(2)}) collective-permute-start(bf16[128,256]{1,0:T(8,128)(2,1)S(1)} %get-tuple-element.79), channel_id=1, source_target_pairs={{0,12},{1,13},{2,14},{3,15},{4,0},{5,1},{6,2},{7,3},{8,4},{9,5},{1... | collective-permute-start | bytes 196616 | tf_op jit(solution)/shard_map/ppermute | solution.py:455
  32.8 1.1 %collective-permute-start.13 = (bf16[2048,256]{1,0:T(8,128)(2,1)S(1)}, bf16[2048,256]{1,0:T(8,128)(2,1)S(1)}, u32[]{:S(2)}, u32[]{:S(2)}) collective-permute-start(bf16[2048,256]{1,0:T(8,128)(2,1)S(1)} %get-tuple-element.97), channel_id=1, source_target_pairs={{0,1},{1,0},{2,3},{3,2},{4,5},{5,4},{6,7},{7,6},{8,9},{9,8},{10,11... | collective-permute-start | bytes 3145736 | tf_op jit(solution)/shard_map/ppermute | solution.py:459
  33.9 2.3 %near_0.1.refs_3_.refs_1_ = bf16[256,2048]{1,0:T(8,128)(2,1)S(1)} custom-call(bf16[2048,2048]{1,0:T(8,128)(2,1)S(1)} %get-tuple-element.80.d, bf16[2048,2048]{1,0:T(8,128)(2,1)S(1)} %get-tuple-element.81.x), custom_call_target="tpu_custom_call" | custom-call | flops 2147483648 | bytes 1048576 | tf_op jit(solution)/shard_map/near_0/pallas_call | solution.py:256
  36.2 0.0 collective-permute-done.3.q1
  36.2 0.0 collective-permute-done.4.q2
  36.2 0.0 collective-permute-done.5.q3
  36.2 1.1 %group_up.1 = (bf16[4,128,256]{2,1,0:T(8,128)(2,1)S(1)}, bf16[2,128,256]{2,1,0:T(8,128)(2,1)S(1)}, f32[2,128,256]{2,1,0:T(8,128)S(1)}) custom-call(s32[255]{0:T(256)S(1)} %copy-done.4, bf16[128,256]{1,0:T(8,128)(2,1)S(1)} %get-tuple-element.82.q0, bf16[128,256]{1,0:T(8,128)(2,1)S(1)} %collective-permute-done.3.q1, ...), custom_call_target="tpu_custom_call" | custom-call | flops 268435456 | bytes 1048576 | tf_op jit(solution)/shard_map/group_up/pallas_call | solution.py:61
  37.3 0.1 collective-permute-start.6
  37.4 1.5 %collective-permute-done.6.peer.peer4 = f32[2,128,256]{2,1,0:T(8,128)S(1)} collective-permute-done((f32[2,128,256]{2,1,0:T(8,128)S(1)}, f32[2,128,256]{2,1,0:T(8,128)S(1)}, u32[]{:S(2)}, u32[]{:S(2)}) %collective-permute-start.6) | collective-permute-done | bytes 262176 | tf_op jit(solution)/shard_map/ppermute | solution.py:463
  38.9 0.6 five.1.y0
  39.5 0.0 copy-start.2
  39.5 0.0 copy-start.3
  39.5 1.7 %collective-permute-start.7 = (bf16[128,256]{1,0:T(8,128)(2,1)S(1)}, bf16[128,256]{1,0:T(8,128)(2,1)S(1)}, u32[]{:S(2)}, u32[]{:S(2)}) collective-permute-start(bf16[128,256]{1,0:T(8,128)(2,1)S(1)} %five.1.y0), channel_id=1, source_target_pairs={{0,32},{16,48},{32,0},{48,16},{64,96},{80,112},{96,64},{112,80},{1... | collective-permute-start | bytes 196616 | tf_op jit(solution)/shard_map/ppermute | solution.py:463
  41.2 2.9 %collective-permute-start.8 = (bf16[128,256]{1,0:T(8,128)(2,1)S(1)}, bf16[128,256]{1,0:T(8,128)(2,1)S(1)}, u32[]{:S(2)}, u32[]{:S(2)}) collective-permute-start(bf16[128,256]{1,0:T(8,128)(2,1)S(1)} %five.1.y0), channel_id=1, source_target_pairs={{0,64},{16,80},{32,96},{48,112},{64,0},{80,16},{96,32},{112,48},{1... | collective-permute-start | bytes 196616 | tf_op jit(solution)/shard_map/ppermute | solution.py:463
  44.1 0.2 collective-permute-start.9
  44.3 4.5 %near_256.1.refs_4_.refs_2_ = bf16[512,2048]{1,0:T(8,128)(2,1)S(1)} custom-call(bf16[2048,2048]{1,0:T(8,128)(2,1)S(1)} %get-tuple-element.80.d, bf16[2048,2048]{1,0:T(8,128)(2,1)S(1)} %get-tuple-element.81.x), custom_call_target="tpu_custom_call" | custom-call | flops 4294967296 | bytes 1048576 | tf_op jit(solution)/shard_map/near_256/pallas_call | solution.py:256
  48.8 0.0 collective-permute-done.7.y1
  48.8 0.0 collective-permute-done.8.y2
  48.8 0.7 collective-permute-done.9.y3
  49.6 2.3 %top.1 = (bf16[128,256]{1,0:T(8,128)(2,1)S(1)}, bf16[128,256]{1,0:T(8,128)(2,1)S(1)}, bf16[128,256]{1,0:T(8,128)(2,1)S(1)}, bf16[128,256]{1,0:T(8,128)(2,1)S(1)}) custom-call(s32[255]{0:T(256)S(1)} %copy-done.4, bf16[128,256]{1,0:T(8,128)(2,1)S(1)} %five.1.y0, bf16[128,256]{1,0:T(8,128)(2,1)S(1)} %collective-permute-done.7.y1, ...), custom_call_target="tpu_custom_call" | custom-call | flops 268435456 | bytes 1048576 | tf_op jit(solution)/shard_map/top/pallas_call | solution.py:61
  51.9 1.1 %collective-permute-start.10 = (bf16[128,256]{1,0:T(8,128)(2,1)S(1)}, bf16[128,256]{1,0:T(8,128)(2,1)S(1)}, u32[]{:S(2)}, u32[]{:S(2)}) collective-permute-start(bf16[128,256]{1,0:T(8,128)(2,1)S(1)} %get-tuple-element.94), channel_id=1, source_target_pairs={{0,4},{1,5},{2,6},{3,7},{4,8},{5,9},{6,10},{7,11},{8,12},{9,13},{1... | collective-permute-start | bytes 196616 | tf_op jit(solution)/shard_map/ppermute | solution.py:455
  53.0 2.5 %collective-permute-start.11 = (bf16[128,256]{1,0:T(8,128)(2,1)S(1)}, bf16[128,256]{1,0:T(8,128)(2,1)S(1)}, u32[]{:S(2)}, u32[]{:S(2)}) collective-permute-start(bf16[128,256]{1,0:T(8,128)(2,1)S(1)} %get-tuple-element.95), channel_id=1, source_target_pairs={{0,8},{1,9},{2,10},{3,11},{4,12},{5,13},{6,14},{7,15},{8,0},{9,1},... | collective-permute-start | bytes 196616 | tf_op jit(solution)/shard_map/ppermute | solution.py:455
  55.5 0.5 collective-permute-start.12
  56.0 2.3 %near_768.1.refs_5_.refs_3_ = bf16[256,2048]{1,0:T(8,128)(2,1)S(1)} custom-call(bf16[2048,2048]{1,0:T(8,128)(2,1)S(1)} %get-tuple-element.80.d, bf16[2048,2048]{1,0:T(8,128)(2,1)S(1)} %get-tuple-element.81.x), custom_call_target="tpu_custom_call" | custom-call | flops 2147483648 | bytes 1048576 | tf_op jit(solution)/shard_map/near_768/pallas_call | solution.py:256
  58.3 0.0 collective-permute-done.10.f1
  58.3 0.5 collective-permute-done.11.f2
  58.8 1.0 %collective-permute-done.12.f3 = bf16[128,256]{1,0:T(8,128)(2,1)S(1)} collective-permute-done((bf16[128,256]{1,0:T(8,128)(2,1)S(1)}, bf16[128,256]{1,0:T(8,128)(2,1)S(1)}, u32[]{:S(2)}, u32[]{:S(2)}) %collective-permute-start.12) | collective-permute-done | bytes 65568 | tf_op jit(solution)/shard_map/ppermute | solution.py:455
  59.8 0.0 collective-permute-done.13.sibling
  59.8 1.1 %quad_down.1 = (bf16[512,256]{1,0:T(8,128)(2,1)S(1)}, bf16[512,256]{1,0:T(8,128)(2,1)S(1)}, bf16[512,256]{1,0:T(8,128)(2,1)S(1)}, bf16[512,256]{1,0:T(8,128)(2,1)S(1)}) custom-call(s32[255]{0:T(256)S(1)} %copy-done.4, bf16[128,256]{1,0:T(8,128)(2,1)S(1)} %get-tuple-element.99.f0, bf16[128,256]{1,0:T(8,128)(2,1)S(1)} %collective-permute-done.10.f1, ...), custom_call_target="tpu_custom_call" | custom-call | flops 268435456 | bytes 1048576 | tf_op jit(solution)/shard_map/quad_down/pallas_call | solution.py:61
  60.9 1.1 %collective-permute-start.15 = (bf16[512,256]{1,0:T(8,128)(2,1)S(1)}, bf16[512,256]{1,0:T(8,128)(2,1)S(1)}, u32[]{:S(2)}, u32[]{:S(2)}) collective-permute-start(bf16[512,256]{1,0:T(8,128)(2,1)S(1)} %get-tuple-element.109), channel_id=1, source_target_pairs={{0,1},{1,2},{2,3},{3,0},{4,5},{5,6},{6,7},{7,4},{8,9},{9,10},{10,1... | collective-permute-start | bytes 786440 | tf_op jit(solution)/shard_map/ppermute | solution.py:450
  62.0 2.2 %collective-permute-start.16 = (bf16[512,256]{1,0:T(8,128)(2,1)S(1)}, bf16[512,256]{1,0:T(8,128)(2,1)S(1)}, u32[]{:S(2)}, u32[]{:S(2)}) collective-permute-start(bf16[512,256]{1,0:T(8,128)(2,1)S(1)} %get-tuple-element.110), channel_id=1, source_target_pairs={{0,3},{1,0},{2,1},{3,2},{4,7},{5,4},{6,5},{7,6},{8,11},{9,8},{10,9... | collective-permute-start | bytes 786440 | tf_op jit(solution)/shard_map/ppermute | solution.py:450
  64.2 1.2 %collective-permute-start.14 = (bf16[512,256]{1,0:T(8,128)(2,1)S(1)}, bf16[512,256]{1,0:T(8,128)(2,1)S(1)}, u32[]{:S(2)}, u32[]{:S(2)}) collective-permute-start(bf16[512,256]{1,0:T(8,128)(2,1)S(1)} %get-tuple-element.104), channel_id=1, source_target_pairs={{0,2},{1,3},{2,0},{3,1},{4,6},{5,7},{6,4},{7,5},{8,10},{9,11},{10,... | collective-permute-start | bytes 786440 | tf_op jit(solution)/shard_map/ppermute | solution.py:450
  65.4 8.8 %near_1024.1.refs_6_.refs_4_ = bf16[1024,2048]{1,0:T(8,128)(2,1)S(1)} custom-call(bf16[2048,2048]{1,0:T(8,128)(2,1)S(1)} %get-tuple-element.80.d, bf16[2048,2048]{1,0:T(8,128)(2,1)S(1)} %get-tuple-element.81.x), custom_call_target="tpu_custom_call" | custom-call | flops 8589934592 | bytes 1048576 | tf_op jit(solution)/shard_map/near_1024/pallas_call | solution.py:256
  74.2 0.0 collective-permute-done.15.refs_1_
  74.2 0.0 collective-permute-done.16.refs_2_
  74.3 4.5 %tail_013.1.refs_5_ = bf16[2048,2048]{1,0:T(8,128)(2,1)} custom-call(s32[255]{0:T(256)S(1)} %copy-done.4, bf16[2048,256]{1,0:T(8,128)(2,1)S(1)} %get-tuple-element.58.basis, bf16[2048,256]{1,0:T(8,128)(2,1)S(1)} %collective-permute-done.13.sibling, bf16[2,256,256]{2,1,0:T(8,128)(2,1)S(1)} %bitcast.9, bf16[512,256]{1,0:T(8,128)(2,1)S(1)} %get-tuple-element.108.refs_0_, ...), custom_call_target="tpu_custom_call" | custom-call | flops 536870912 | bytes 3145728 | tf_op jit(solution)/shard_map/tail_013/pallas_call | solution.py:432
  78.8 2.7 %tail_2.1 = bf16[2048,2048]{1,0:T(8,128)(2,1)} custom-call(s32[255]{0:T(256)S(1)} %copy-done.4, bf16[2048,256]{1,0:T(8,128)(2,1)S(1)} %get-tuple-element.58.basis, bf16[2048,256]{1,0:T(8,128)(2,1)S(1)} %collective-permute-done.13.sibling, bf16[2,256,256]{2,1,0:T(8,128)(2,1)S(1)} %bitcast.10, ...), custom_call_target="tpu_custom_call", output_to_operand_aliasing={{}: (9, {})} | custom-call | flops 536870912 | bytes 3145728 | tf_op jit(solution)/shard_map/tail_2/pallas_call | solution.py:432
  (11 shorter events, 0.0 us)
Async XLA Ops:
  0.0 14.7 %copy-start.5 = (s32[1,2048]{1,0:T(1,128)S(1)}, s32[1,2048]{1,0:T(1,128)}, u32[]{:S(2)}) copy-start(s32[1,2048]{1,0:T(1,128)} %order.1) | copy-start | bytes 24580
  8.8 16.2 %collective-permute-start = (bf16[512,256]{1,0:T(8,128)(2,1)S(1)}, bf16[512,256]{1,0:T(8,128)(2,1)S(1)}, u32[]{:S(2)}, u32[]{:S(2)}) collective-permute-start(bf16[512,256]{1,0:T(8,128)(2,1)S(1)} %get-tuple-element.60), channel_id=1, source_target_pairs={{0,1},{1,2},{2,3},{3,0},{4,5},{5,6},{6,7},{7,4},{8,9},{9,10},{10,1... | collective-permute-start | bytes 786440 | tf_op jit(solution)/shard_map/ppermute | solution.py:450
  10.5 14.6 %collective-permute-start.1 = (bf16[512,256]{1,0:T(8,128)(2,1)S(1)}, bf16[512,256]{1,0:T(8,128)(2,1)S(1)}, u32[]{:S(2)}, u32[]{:S(2)}) collective-permute-start(bf16[512,256]{1,0:T(8,128)(2,1)S(1)} %get-tuple-element.61), channel_id=1, source_target_pairs={{0,2},{1,3},{2,0},{3,1},{4,6},{5,7},{6,4},{7,5},{8,10},{9,11},{10,... | collective-permute-start | bytes 786440 | tf_op jit(solution)/shard_map/ppermute | solution.py:450
  13.2 11.9 %collective-permute-start.2 = (bf16[512,256]{1,0:T(8,128)(2,1)S(1)}, bf16[512,256]{1,0:T(8,128)(2,1)S(1)}, u32[]{:S(2)}, u32[]{:S(2)}) collective-permute-start(bf16[512,256]{1,0:T(8,128)(2,1)S(1)} %get-tuple-element.62), channel_id=1, source_target_pairs={{0,3},{1,0},{2,1},{3,2},{4,7},{5,4},{6,5},{7,6},{8,11},{9,8},{10,9... | collective-permute-start | bytes 786440 | tf_op jit(solution)/shard_map/ppermute | solution.py:450
  14.7 10.5 %copy-start = (bf16[1,15,2,256,256]{4,3,2,1,0:T(8,128)(2,1)S(1)}, bf16[1,15,2,256,256]{4,3,2,1,0:T(8,128)(2,1)}, u32[]{:S(2)}) copy-start(bf16[1,15,2,256,256]{4,3,2,1,0:T(8,128)(2,1)} %param.14) | copy-start | bytes 11796484
  14.7 10.5 %copy-start.4 = (s32[255]{0:T(256)S(1)}, s32[255]{0:T(256)}, u32[]{:S(2)}) copy-start(s32[255]{0:T(256)} %ranks.13) | copy-start | bytes 3064
  26.2 10.0 %collective-permute-start.3 = (bf16[128,256]{1,0:T(8,128)(2,1)S(1)}, bf16[128,256]{1,0:T(8,128)(2,1)S(1)}, u32[]{:S(2)}, u32[]{:S(2)}) collective-permute-start(bf16[128,256]{1,0:T(8,128)(2,1)S(1)} %get-tuple-element.77), channel_id=1, source_target_pairs={{0,4},{1,5},{2,6},{3,7},{4,8},{5,9},{6,10},{7,11},{8,12},{9,13},{1... | collective-permute-start | bytes 196616 | tf_op jit(solution)/shard_map/ppermute | solution.py:455
  28.2 8.0 %collective-permute-start.4 = (bf16[128,256]{1,0:T(8,128)(2,1)S(1)}, bf16[128,256]{1,0:T(8,128)(2,1)S(1)}, u32[]{:S(2)}, u32[]{:S(2)}) collective-permute-start(bf16[128,256]{1,0:T(8,128)(2,1)S(1)} %get-tuple-element.78), channel_id=1, source_target_pairs={{0,8},{1,9},{2,10},{3,11},{4,12},{5,13},{6,14},{7,15},{8,0},{9,1},... | collective-permute-start | bytes 196616 | tf_op jit(solution)/shard_map/ppermute | solution.py:455
  31.8 4.4 %collective-permute-start.5 = (bf16[128,256]{1,0:T(8,128)(2,1)S(1)}, bf16[128,256]{1,0:T(8,128)(2,1)S(1)}, u32[]{:S(2)}, u32[]{:S(2)}) collective-permute-start(bf16[128,256]{1,0:T(8,128)(2,1)S(1)} %get-tuple-element.79), channel_id=1, source_target_pairs={{0,12},{1,13},{2,14},{3,15},{4,0},{5,1},{6,2},{7,3},{8,4},{9,5},{1... | collective-permute-start | bytes 196616 | tf_op jit(solution)/shard_map/ppermute | solution.py:455
  32.8 27.0 %collective-permute-start.13 = (bf16[2048,256]{1,0:T(8,128)(2,1)S(1)}, bf16[2048,256]{1,0:T(8,128)(2,1)S(1)}, u32[]{:S(2)}, u32[]{:S(2)}) collective-permute-start(bf16[2048,256]{1,0:T(8,128)(2,1)S(1)} %get-tuple-element.97), channel_id=1, source_target_pairs={{0,1},{1,0},{2,3},{3,2},{4,5},{5,4},{6,7},{7,6},{8,9},{9,8},{10,11... | collective-permute-start | bytes 3145736 | tf_op jit(solution)/shard_map/ppermute | solution.py:459
  37.3 1.6 %collective-permute-start.6 = (f32[2,128,256]{2,1,0:T(8,128)S(1)}, f32[2,128,256]{2,1,0:T(8,128)S(1)}, u32[]{:S(2)}, u32[]{:S(2)}) collective-permute-start(f32[2,128,256]{2,1,0:T(8,128)S(1)} %get-tuple-element.86.own), channel_id=1, source_target_pairs={{0,16},{16,0},{32,48},{48,32},{64,80},{80,64},{96,112},{112,96},{1... | collective-permute-start | bytes 786440 | tf_op jit(solution)/shard_map/ppermute | solution.py:463
  39.5 10.1 %copy-start.2 = (bf16[6,2,256,256]{3,2,1,0:T(8,128)(2,1)S(1)}, bf16[6,2,256,256]{3,2,1,0:T(8,128)(2,1)}, u32[]{:S(2)}) copy-start(bf16[6,2,256,256]{3,2,1,0:T(8,128)(2,1)} %outer.1) | copy-start | bytes 4718596
  39.5 10.0 %copy-start.3 = (bf16[256,256]{1,0:T(8,128)(2,1)S(1)}, bf16[256,256]{1,0:T(8,128)(2,1)}, u32[]{:S(2)}) copy-start(bf16[256,256]{1,0:T(8,128)(2,1)} %root.1) | copy-start | bytes 393220
  39.5 9.3 %collective-permute-start.7 = (bf16[128,256]{1,0:T(8,128)(2,1)S(1)}, bf16[128,256]{1,0:T(8,128)(2,1)S(1)}, u32[]{:S(2)}, u32[]{:S(2)}) collective-permute-start(bf16[128,256]{1,0:T(8,128)(2,1)S(1)} %five.1.y0), channel_id=1, source_target_pairs={{0,32},{16,48},{32,0},{48,16},{64,96},{80,112},{96,64},{112,80},{1... | collective-permute-start | bytes 196616 | tf_op jit(solution)/shard_map/ppermute | solution.py:463
  41.2 7.6 %collective-permute-start.8 = (bf16[128,256]{1,0:T(8,128)(2,1)S(1)}, bf16[128,256]{1,0:T(8,128)(2,1)S(1)}, u32[]{:S(2)}, u32[]{:S(2)}) collective-permute-start(bf16[128,256]{1,0:T(8,128)(2,1)S(1)} %five.1.y0), channel_id=1, source_target_pairs={{0,64},{16,80},{32,96},{48,112},{64,0},{80,16},{96,32},{112,48},{1... | collective-permute-start | bytes 196616 | tf_op jit(solution)/shard_map/ppermute | solution.py:463
  44.1 5.5 %collective-permute-start.9 = (bf16[128,256]{1,0:T(8,128)(2,1)S(1)}, bf16[128,256]{1,0:T(8,128)(2,1)S(1)}, u32[]{:S(2)}, u32[]{:S(2)}) collective-permute-start(bf16[128,256]{1,0:T(8,128)(2,1)S(1)} %five.1.y0), channel_id=1, source_target_pairs={{0,96},{16,112},{32,64},{48,80},{64,32},{80,48},{96,0},{112,16},{1... | collective-permute-start | bytes 196616 | tf_op jit(solution)/shard_map/ppermute | solution.py:463
  51.9 6.4 %collective-permute-start.10 = (bf16[128,256]{1,0:T(8,128)(2,1)S(1)}, bf16[128,256]{1,0:T(8,128)(2,1)S(1)}, u32[]{:S(2)}, u32[]{:S(2)}) collective-permute-start(bf16[128,256]{1,0:T(8,128)(2,1)S(1)} %get-tuple-element.94), channel_id=1, source_target_pairs={{0,4},{1,5},{2,6},{3,7},{4,8},{5,9},{6,10},{7,11},{8,12},{9,13},{1... | collective-permute-start | bytes 196616 | tf_op jit(solution)/shard_map/ppermute | solution.py:455
  53.0 5.8 %collective-permute-start.11 = (bf16[128,256]{1,0:T(8,128)(2,1)S(1)}, bf16[128,256]{1,0:T(8,128)(2,1)S(1)}, u32[]{:S(2)}, u32[]{:S(2)}) collective-permute-start(bf16[128,256]{1,0:T(8,128)(2,1)S(1)} %get-tuple-element.95), channel_id=1, source_target_pairs={{0,8},{1,9},{2,10},{3,11},{4,12},{5,13},{6,14},{7,15},{8,0},{9,1},... | collective-permute-start | bytes 196616 | tf_op jit(solution)/shard_map/ppermute | solution.py:455
  55.5 4.3 %collective-permute-start.12 = (bf16[128,256]{1,0:T(8,128)(2,1)S(1)}, bf16[128,256]{1,0:T(8,128)(2,1)S(1)}, u32[]{:S(2)}, u32[]{:S(2)}) collective-permute-start(bf16[128,256]{1,0:T(8,128)(2,1)S(1)} %get-tuple-element.96), channel_id=1, source_target_pairs={{0,12},{1,13},{2,14},{3,15},{4,0},{5,1},{6,2},{7,3},{8,4},{9,5},{1... | collective-permute-start | bytes 196616 | tf_op jit(solution)/shard_map/ppermute | solution.py:455
  60.9 13.3 %collective-permute-start.15 = (bf16[512,256]{1,0:T(8,128)(2,1)S(1)}, bf16[512,256]{1,0:T(8,128)(2,1)S(1)}, u32[]{:S(2)}, u32[]{:S(2)}) collective-permute-start(bf16[512,256]{1,0:T(8,128)(2,1)S(1)} %get-tuple-element.109), channel_id=1, source_target_pairs={{0,1},{1,2},{2,3},{3,0},{4,5},{5,6},{6,7},{7,4},{8,9},{9,10},{10,1... | collective-permute-start | bytes 786440 | tf_op jit(solution)/shard_map/ppermute | solution.py:450
  62.0 12.2 %collective-permute-start.16 = (bf16[512,256]{1,0:T(8,128)(2,1)S(1)}, bf16[512,256]{1,0:T(8,128)(2,1)S(1)}, u32[]{:S(2)}, u32[]{:S(2)}) collective-permute-start(bf16[512,256]{1,0:T(8,128)(2,1)S(1)} %get-tuple-element.110), channel_id=1, source_target_pairs={{0,3},{1,0},{2,1},{3,2},{4,7},{5,4},{6,5},{7,6},{8,11},{9,8},{10,9... | collective-permute-start | bytes 786440 | tf_op jit(solution)/shard_map/ppermute | solution.py:450
  64.2 10.0 %copy-start.1 = (bf16[1,2,256,256]{3,2,1,0:T(8,128)(2,1)S(1)}, bf16[1,2,256,256]{3,2,1,0:T(8,128)(2,1)}, u32[]{:S(2)}) copy-start(bf16[1,2,256,256]{3,2,1,0:T(8,128)(2,1)} %param.13) | copy-start | bytes 786436
  64.2 14.6 %collective-permute-start.14 = (bf16[512,256]{1,0:T(8,128)(2,1)S(1)}, bf16[512,256]{1,0:T(8,128)(2,1)S(1)}, u32[]{:S(2)}, u32[]{:S(2)}) collective-permute-start(bf16[512,256]{1,0:T(8,128)(2,1)S(1)} %get-tuple-element.104), channel_id=1, source_target_pairs={{0,2},{1,3},{2,0},{3,1},{4,6},{5,7},{6,4},{7,5},{8,10},{9,11},{10,... | collective-permute-start | bytes 786440 | tf_op jit(solution)/shard_map/ppermute | solution.py:450

commit v3 on v2

--- a/solution.py
+++ b/solution.py
@@ -56,13 +56,14 @@
     return inner & 3, inner >> 2, lax.axis_index("outer")
 
 
-def call(kernel, name, out_shapes, args, flops=2**28, limit=8, scratch=(), specs=None):
+def call(kernel, name, out_shapes, args, flops=2**28, limit=5, scratch=(), specs=None, alias={}):
     many = isinstance(out_shapes, tuple)
     return pl.pallas_call(
         kernel,
         out_shape=out_shapes,
         in_specs=specs or [SMEM] + [VMEM] * (len(args) - 1),
         out_specs=(VMEM,) * len(out_shapes) if many else VMEM,
+        input_output_aliases=alias,
         scratch_shapes=list(scratch),
         compiler_params=params(limit * 2**20),
         cost_estimate=cost(flops, 2**20),
@@ -102,22 +103,25 @@
             out_t[t * 128 : (t + 1) * 128, pl.ds(start, 256)] = x.T.astype(BF)
 
 
-def coef_block(shift, ranks, basis_t, x, transfer, coef, piece):
+def coef_product(shift, basis_t, x):
+    cols = x.shape[1] // RING
+    start = pl.multiple_of(((place()[0] + shift) & 3) * cols, cols)
+    return nn(basis_t[...], x[:, pl.ds(start, cols)])
+
+
+def coef_finish(product, ranks, transfer, coef, piece):
     ring, z, outer = place()
-    cols = piece.shape[0]
-    start = pl.multiple_of(lax.rem(ring + shift, RING) * cols, cols)
-    rank = ranks[127 + outer * 16 + z * RING + ring]
-    c = masked(nn(basis_t[...], x[:, pl.ds(start, cols)]).T, rank)
-    coef[pl.ds(start, cols), :] = c
+    c = masked(product.T, ranks[127 + outer * 16 + z * RING + ring])
+    coef[...] = c
     piece[...] = nn(c, transfer[...]).astype(BF)
 
 
 def front_kernel(
     order_hbm, ranks_hbm, basis_hbm, x_hbm, node_hbm,
-    out, x, coef, p0, p1, p2, p3,
-    order, ranks, basis, out_t, transfer, src, dst, sem,
+    out, out_t, x, coef, piece,
+    order, ranks, basis, transfer, src, dst, sem,
 ):
-    cols = p0.shape[0]
+    cols = piece.shape[0]
     ring = place()[0]
 
     def fetch(k):
@@ -133,32 +137,37 @@
     ]
     for load in loads:
         load.start()
+    for load in loads:
+        load.wait()
     for k in range(RING):
         fetch(k).start()
-    for load in loads:
-        load.wait()
     shuffle_basis(order, basis, out, out_t, src, dst)
-    for k, ref in enumerate((p2, p1, p3, p0)):
+    fetch(0).wait()
+    coef_finish(coef_product(2, out_t, x), ranks, transfer, coef, piece)
+    for k in range(1, RING):
         fetch(k).wait()
-        coef_block((2, 1, 3, 0)[k], ranks, out_t, x, transfer, coef, ref)
 
 
 def front(order, ranks, basis, points, nodes):
     rows, width = basis.shape
     cols = points.shape[1]
-    piece = held(cols // RING, width)
     return call(
         front_kernel,
         "front",
-        (held(rows, width), held(rows, cols), held(cols, width)) + (piece,) * 4,
+        (
+            held(rows, width),
+            held(width, rows),
+            held(rows, cols),
+            held(cols // RING, width),
+            held(cols // RING, width),
+        ),
         [pin(a, pltpu.HBM) for a in (order, ranks, basis, points, nodes)],
         flops=2**31,
-        limit=16,
+        limit=13,
         scratch=[
             pltpu.SMEM(order.shape, jnp.int32),
             pltpu.SMEM(ranks.shape, jnp.int32),
             pltpu.VMEM((rows, width), BF),
-            pltpu.VMEM((width, rows), BF),
             pltpu.VMEM((width, width), BF),
             pltpu.VMEM((rows * 3, 128), F32),
             pltpu.VMEM((rows * 3, 128), F32),
@@ -168,45 +177,77 @@
     )
 
 
+def coef_kernel(ranks, basis_t, x, node, c1, c3, p1, p3):
+    product1 = coef_product(1, basis_t, x)
+    product3 = coef_product(3, basis_t, x)
+    coef_finish(product1, ranks, node.at[0], c1, p1)
+    coef_finish(product3, ranks, node.at[0], c3, p3)
+
+
+def coef_rest(ranks, basis_t, x, node):
+    return call(
+        coef_kernel,
+        "coef",
+        (held(x.shape[1] // RING, basis_t.shape[0]),) * 4,
+        (ranks, *map(pin, (basis_t, x, node))),
+        flops=2**30,
+    )
+
+
 PITCH = 17
-
-
-def move_rows(scatter, order, x, src, dst):
+GROUP = 64
+
+
+def spread(value, first_row, first_tile, to):
+    for r in range(0, value.shape[0], 8):
+        for t in range(value.shape[1] // 128):
+            at = (first_row + r) * PITCH + first_tile + t
+            to[pl.ds(at, 8, stride=PITCH), :] = value[r : r + 8, t * 128 : (t + 1) * 128]
+
+
+def gathered(first_row, rows, first_tile, tiles, of):
+    columns = []
+    for t in range(tiles):
+        parts = []
+        for r in range(0, rows, 8):
+            at = (first_row + r) * PITCH + first_tile + t
+            parts.append(of[pl.ds(at, 8, stride=PITCH), :])
+        columns.append(jnp.concatenate(parts, axis=0))
+    return jnp.concatenate(columns, axis=1)
+
+
+def move_rows(row_at, x, src, dst):
     rows = x.shape[0]
     tiles = x.shape[1] // 128
 
     @pl.loop(0, rows // 32)
     def _(b):
-        for r in range(2):
-            base = (b * 32 + r * 16) * PITCH
-            start = pl.multiple_of(b * 32 + r * 16, 16)
+        for r in range(0, 32, 16):
+            start = pl.multiple_of(b * 32 + r, 16)
             for t in range(tiles):
                 v = x[pl.ds(start, 16), t * 128 : (t + 1) * 128].astype(F32)
-                src[pl.ds(base + t, 8, stride=PITCH), :] = v[:8]
-                src[pl.ds(base + 8 * PITCH + t, 8, stride=PITCH), :] = v[8:]
-
-    @pl.loop(0, rows // 64)
+                spread(v, b * 32 + r, t, src)
+
+    @pl.loop(0, rows // (2 * GROUP))
     def _(i):
-        for j in range(64):
-            far_at = order[0, i * 64 + j]
-            near_at = i * (64 * PITCH) + j * PITCH
-            s, d = (near_at, far_at) if scatter else (far_at, near_at)
-            for h in range(0, tiles, 8):
-                dst[pl.ds(d + h, 8), :] = src[pl.ds(s + h, 8), :]
-
-    @pl.loop(0, rows // 32)
-    def _(b):
-        for r in range(2):
-            base = (b * 32 + r * 16) * PITCH
-            start = pl.multiple_of(b * 32 + r * 16, 16)
-            for t in range(tiles):
-                lo = dst[pl.ds(base + t, 8, stride=PITCH), :]
-                hi = dst[pl.ds(base + 8 * PITCH + t, 8, stride=PITCH), :]
-                v = jnp.concatenate([lo, hi], axis=0).astype(BF)
-                x[pl.ds(start, 16), t * 128 : (t + 1) * 128] = v
-
-
-def move_kernel(order, x_in, diag_hbm, x, diag, src, dst, scaled, row_at, sem):
+        first = pl.multiple_of(i * (2 * GROUP), 2 * GROUP)
+        for g in range(2):
+            for j in range(GROUP):
+                s = row_at[0, first + g * GROUP + j]
+                for h in range(0, tiles, 8):
+                    dst[g][pl.ds(j * PITCH + h, 8), :] = src[pl.ds(s + h, 8), :]
+        for g in range(2):
+            for r in range(0, GROUP, 16):
+                for t in range(tiles):
+                    v = gathered(r, 16, t, 1, dst[g]).astype(BF)
+                    x[pl.ds(first + g * GROUP + r, 16), t * 128 : (t + 1) * 128] = v
+
+
+def move_kernel(
+    ranks, order, basis_t, node, c1, c2, c3, x_in, diag_hbm,
+    coef, x, diag, piece, src,
+    even, odd, scaled, row_at, sem,
+):
     size = diag.shape[0] // 4
     loads = []
     for k in range(4):
@@ -216,52 +257,90 @@
     scaled[...] = order[...] * PITCH
     load = pltpu.make_async_copy(scaled, row_at, sem.at[4])
     load.start()
+    cols = piece.shape[0]
+    ring = place()[0]
+
+    def rows_of(shift):
+        return coef.at[pl.ds(pl.multiple_of(((ring + shift) & 3) * cols, cols), cols)]
+
+    coef_finish(coef_product(0, basis_t, x), ranks, node.at[0], rows_of(0), piece)
+    for shift, ref in ((1, c1), (2, c2), (3, c3)):
+        rows_of(shift)[...] = ref[...]
     load.wait()
-    move_rows(False, row_at, x, src, dst)
+    move_rows(row_at, x, src, (even, odd))
     for load in loads:
         load.wait()
-    move_rows(True, row_at, diag, src, dst)
-
-
-def move_both(order, x, diag):
+
+
+def move(ranks, order, basis_t, node, coefs, x, diag):
     rows, cols = x.shape
-    return pl.pallas_call(
+    width = basis_t.shape[0]
+    return call(
         move_kernel,
-        out_shape=(held(rows, cols), held(rows, cols)),
-        in_specs=[VMEM, VMEM, HBM],
-        out_specs=(VMEM, VMEM),
-        input_output_aliases={1: 0},
-        scratch_shapes=[pltpu.VMEM((rows * PITCH, 128), F32)] * 2
-        + [
+        "move",
+        (
+            held(cols, width),
+            held(rows, cols),
+            held(rows, cols),
+            held(cols // RING, width),
+            pltpu.VMEM((rows * PITCH, 128), F32),
+        ),
+        (ranks, *map(pin, (order, basis_t, node, *coefs, x)), pin(diag, pltpu.HBM)),
+        flops=2**33,
+        limit=6,
+        scratch=[
+            pltpu.VMEM((GROUP * PITCH, 128), F32),
+            pltpu.VMEM((GROUP * PITCH, 128), F32),
             pltpu.VMEM(order.shape, jnp.int32),
             pltpu.SMEM(order.shape, jnp.int32),
             pltpu.SemaphoreType.DMA((5,)),
         ],
-        compiler_params=params(37 * 2**20),
-        cost_estimate=cost(0, 40 * 2**20),
-        name="move",
-    )(pin(order), pin(x), pin(diag, pltpu.HBM))
-
-
-def near_kernel(first, d, x, out):
-    size = out.shape[0]
-
-    for j in range(0, x.shape[1], 256):
-        out[:, j : j + 256] = nn(d[first : first + size], x[:, j : j + 256]).astype(BF)
-
-
-def near_rows(first, size, diag, ordered):
+        specs=[SMEM] + [VMEM] * 7 + [HBM],
+        alias={7: 1},
+    )
+
+
+def near_kernel(first, size, order, d, x, near_in, out, even, odd, row_at, sem):
+    block = even.shape[0] // PITCH
+    load = pltpu.make_async_copy(order, row_at, sem)
+    load.start()
+    waiting = []
+
+    def place_rows(count):
+        for _ in range(min(count, len(waiting))):
+            row, i, h, src = waiting.pop(0)
+            to = row_at[0, row + i] * PITCH
+            out[pl.ds(to + h, 8), :] = src[pl.ds(i * PITCH + h, 8), :]
+
+    steps = x.shape[1] // 256
+    for k, row in enumerate(range(first, first + size, block)):
+        src = (even, odd)[k % 2]
+        for j in range(steps):
+            spread(nn(d[row : row + block], x[:, j * 256 : (j + 1) * 256]), 0, j * 2, src)
+            if k == 0 and j == steps // 2 - 1:
+                load.wait()
+            place_rows(2 * block // steps)
+            if j == steps // 2 - 1 or j == steps - 1:
+                waiting += [(row, i, 8 * (2 * j // steps), src) for i in range(block)]
+    place_rows(len(waiting))
+
+
+def near_rows(first, size, order, diag, ordered, sofar):
     rows, depth = diag.shape
     cols = ordered.shape[1]
-    return pl.pallas_call(
-        functools.partial(near_kernel, first),
-        out_shape=held(size, cols),
-        in_specs=[VMEM] * 2,
-        out_specs=VMEM,
-        compiler_params=params(8 * 2**20),
-        cost_estimate=cost(2 * size * depth * cols, 2**20),
-        name=f"near_{first}",
-    )(pin(diag), pin(ordered))
+    block = min(size, 512)
+    return call(
+        functools.partial(near_kernel, first, size),
+        f"near_{first}",
+        pltpu.VMEM((rows * PITCH, 128), F32),
+        tuple(map(pin, (order, diag, ordered, sofar))),
+        flops=2 * size * depth * cols,
+        limit=4 + block // 64,
+        scratch=[pltpu.VMEM((block * PITCH, 128), F32)] * 2
+        + [pltpu.SMEM(order.shape, jnp.int32), pltpu.SemaphoreType.DMA],
+        specs=[VMEM] * 4,
+        alias={3: 0},
+    )
 
 
 def quad_up_kernel(ranks, u0, u1, u2, u3, inner, mid, p0, p1, p2, p3, leaf, top):
@@ -390,39 +469,39 @@
     )
 
 
-TAIL = 256
-
-
-def tail_kernel(shifts, starts, ranks, basis, sibling, node, *refs):
+TAIL = 512
+
+
+def tail_kernel(shifts, ranks, basis, sibling, node, near, *refs):
     fars = refs[: len(shifts)]
-    nears = refs[len(shifts) : len(shifts) + len(starts)]
     o_hbm, buf, sem = refs[-3:]
     x, z, outer = place()
     cols = fars[0].shape[0]
     rank = ranks[127 + outer * 16 + z * RING + x]
     copies = []
     for i, (shift, far1) in enumerate(zip(shifts, fars)):
-        at = pl.ds(pl.multiple_of(((x - shift) & 3) * cols, cols), cols)
+        part = (x - shift) & 3
+        at = pl.ds(pl.multiple_of(part * cols, cols), cols)
+        tiles = cols // 128
         down = nt(sibling[at, :], node[1]) + nt(far1[...], node[0])
         far = masked(down, rank)
-        for first, near in zip(starts, nears):
-            for r in range(0, near.shape[0], TAIL):
-                row = first + r
-                add = nt(basis[row : row + TAIL], far)
-                buf[i, row : row + TAIL] = (near[r : r + TAIL, at].astype(F32) + add).astype(BF)
-                copy = pltpu.make_async_copy(
-                    buf.at[i, pl.ds(row, TAIL)], o_hbm.at[pl.ds(row, TAIL), at], sem.at[len(copies)]
-                )
-                copy.start()
-                copies.append(copy)
+        for row in range(0, basis.shape[0], TAIL):
+            add = nt(basis[row : row + TAIL], far)
+            value = gathered(row, TAIL, part * tiles, tiles, near) + add
+            buf[i, row : row + TAIL] = value.astype(BF)
+            copy = pltpu.make_async_copy(
+                buf.at[i, pl.ds(row, TAIL)], o_hbm.at[pl.ds(row, TAIL), at], sem.at[len(copies)]
+            )
+            copy.start()
+            copies.append(copy)
     for copy in copies:
         copy.wait()
 
 
-def add_far(shifts, starts, ranks, basis, sibling, node, fars, nears, sofar):
+def add_far(shifts, ranks, basis, sibling, node, near, fars, sofar):
     rows, width = basis.shape
     cols = fars[0].shape[0]
-    args = [ranks] + [pin(a) for a in (basis, sibling, node, *fars, *nears)]
+    args = [ranks] + [pin(a) for a in (basis, sibling, node, near, *fars)]
     specs = [SMEM] + [VMEM] * (len(args) - 1)
     alias = {}
     if sofar is not None:
@@ -430,8 +509,8 @@
         args.append(sofar)
         specs.append(HBM)
     return pl.pallas_call(
-        functools.partial(tail_kernel, shifts, starts),
-        out_shape=sds(rows, nears[0].shape[1]),
+        functools.partial(tail_kernel, shifts),
+        out_shape=sds(rows, cols * RING),
         in_specs=specs,
         out_specs=HBM,
         input_output_aliases=alias,
@@ -439,7 +518,7 @@
             pltpu.VMEM((len(shifts), rows, cols), BF),
             pltpu.SemaphoreType.DMA((len(shifts) * rows // TAIL,)),
         ],
-        compiler_params=params(12 * 2**20),
+        compiler_params=params(14 * 2**20),
         cost_estimate=cost(2 * rows * width * cols, 3 * 2**20),
         name="tail_" + "".join(map(str, shifts)),
     )(*args)
@@ -485,34 +564,36 @@
     inner = inner_nodes[0]
     node = leaf_nodes[0]
 
-    basis, x, coef, *pieces = front(leaf_order, ranks, leaf_basis[0], points, node)
-    pieces = exchange(ring_x, pieces)
-    ordered, diag = move_both(leaf_order, x, diag_blocks[0])
-    *pieces, ordered, diag, coef = lax.optimization_barrier((*pieces, ordered, diag, coef))
+    basis, basis_t, x, c2, piece = front(leaf_order, ranks, leaf_basis[0], points, node)
+    c1, c3, *others = coef_rest(ranks, basis_t, x, node)
+    sent = {2: ring_x(piece, 2), 1: ring_x(others[0], 1), 3: ring_x(others[1], 3)}
+    coefs = (c1, c2, c3)
+    coef, ordered, diag, own, near = move(ranks, leaf_order, basis_t, node, coefs, x, diag_blocks[0])
+    near = near_rows(0, 256, leaf_order, diag, ordered, near)
+    pieces = [own, sent[1], sent[2], sent[3]]
+    *pieces, coef, near = lax.optimization_barrier((*pieces, coef, near))
 
     mid, *parts = quad_up(ranks, pieces, inner)
     coef, *parts = lax.optimization_barrier((coef, *parts))
     parts = exchange(ring_z, parts)
     sibling = swap_inner(coef, 1)
-    starts = (0, 256, 768, 1024)
-    nears = [near_rows(0, 256, diag, ordered)]
-    *parts, nears[0] = lax.optimization_barrier((*parts, nears[0]))
+    near = near_rows(256, 256, leaf_order, diag, ordered, near)
+    *parts, near = lax.optimization_barrier((*parts, near))
     c2, c3, lift = group_up(ranks, parts, inner)
     peer = swap_outer(lift, 1)
     five = five_up(ranks, lift, peer)
     fives = [five] + [swap_outer(five, 2 * s) for s in (1, 2, 3)]
-    nears.append(near_rows(256, 512, diag, ordered))
-    *fives, nears[1] = lax.optimization_barrier((*fives, nears[1]))
+    near = near_rows(512, 256, leaf_order, diag, ordered, near)
+    *fives, near = lax.optimization_barrier((*fives, near))
     parts = top_sweep(ranks, fives, peer, c2, c3, inner, outer_nodes, root_coupling)
     parts = exchange(ring_z, parts)
-    nears.append(near_rows(768, 256, diag, ordered))
-    *parts, nears[2], sibling = lax.optimization_barrier((*parts, nears[2], sibling))
+    near = near_rows(768, 256, leaf_order, diag, ordered, near)
+    *parts, near, sibling = lax.optimization_barrier((*parts, near, sibling))
     fars = quad_down(ranks, parts, mid, inner)
     fars = exchange(ring_x, fars)
-    nears.append(near_rows(1024, 1024, diag, ordered))
-    add = functools.partial(add_far, starts=starts, ranks=ranks, basis=basis, sibling=sibling, node=node)
-    out = add((0, 1, 3), fars=[fars[s] for s in (0, 1, 3)], nears=nears, sofar=None)
-    return add((2,), fars=[fars[2]], nears=nears, sofar=out)
+    near = near_rows(1024, 1024, leaf_order, diag, ordered, near)
+    add = functools.partial(add_far, ranks=ranks, basis=basis, sibling=sibling, node=node, near=near)
+    return add((0, 1, 3, 2), fars=[fars[s] for s in (0, 1, 3, 2)], sofar=None)
 
 
 def solution(mesh):

time: 81.7 us -> 78.9 us (0.966)
  Pallas kernels: 50.6 us -> 47 us
  waiting for transfers between devices: 3.75 us -> 5.47 us
  starting transfers between devices: 26.9 us -> 25.8 us
    pallas_call x7 -> x1, Pallas kernels: 35.5 us -> 5.43 us  [add_far(): pl.pallas_call(functools.partial(tail_kernel, shifts), out_shape=sds(rows...]
    pallas_call x6 -> x13, Pallas kernels: 15.1 us -> 41.6 us  [call(): pl.pallas_call(kernel, out_shape=out_shapes, in_specs=specs or [SMEM] + [...]
    ppermute x4, waiting for transfers between devices: 2.26 us -> 3.8 us  [swap_outer(): lax.ppermute(block, 'outer', [(o, o ^ bits) for o in range(2 * RING)])]
    ppermute x1, starting transfers between devices: 1.06 us -> 0.09 us  [swap_inner(): lax.ppermute(block, 'inner', [(i, i ^ bits) for i in range(RING * RING)])]
  transfers between devices with their start and end apart: 17 -> 17, of which waited for: 4 -> 4; matrix products, arithmetic and copies ran while one was open for 0% -> 0% of each run, Pallas kernels for 45% -> 43%
where the time goes in v3:
time: 78.9 us; the launch traced here: 78.7 us
  Pallas kernels  47 us (60%)
  starting transfers between devices  25.8 us (33%)
  waiting for transfers between devices  5.47 us (7%)
    pallas_call x13, Pallas kernels, call(): pl.pallas_call(kernel, out_shape=out_shapes, in_specs=specs or [SMEM] + [...  41.6 us
    ppermute x6, starting transfers between devices, ring_z(): return lax.ppermute(block, 'inner', route)  10.8 us
    ppermute x6, starting transfers between devices, ring_x(): return lax.ppermute(block, 'inner', route)  10.7 us
    pallas_call x1, Pallas kernels, add_far(): pl.pallas_call(functools.partial(tail_kernel, shifts), out_shape=sds(rows...  5.43 us
    ppermute x4, starting transfers between devices, swap_outer(): lax.ppermute(block, 'outer', [(o, o ^ bits) for o in range(2 * RING)])  4.26 us
    ppermute x4, waiting for transfers between devices, swap_outer(): lax.ppermute(block, 'outer', [(o, o ^ bits) for o in range(2 * RING)])  3.8 us
    ppermute x6, waiting for transfers between devices, ring_z(): return lax.ppermute(block, 'inner', route)  1.65 us
  transfers between devices with their start and end apart: 17, of which 4 were waited for; matrix products, arithmetic and copies ran while one was open for 0% of the time, Pallas kernels for 43%

profile of v3, /device:TPU:0, one launch (start us, length us, event | category | flops | bytes accessed | tf_op | source)
XLA Modules:
  0.0 78.7 jit_solution(2901486719432143981)
XLA Ops:
  0.0 5.9 %front.1 = (bf16[2048,256]{1,0:T(8,128)(2,1)S(1)}, bf16[256,2048]{1,0:T(8,128)(2,1)S(1)}, bf16[2048,2048]{1,0:T(8,128)(2,1)S(1)}, bf16[512,256]{1,0:T(8,128)(2,1)S(1)}, bf16[512,256]{1,0:T(8,128)(2,1)S(1)}) custom-call(s32[1,2048]{1,0:T(1,128)} %order.11, s32[255]{0:T(256)} %ranks.15, bf16[2048,256]{1,0:T(8,128)(2,1)} %bitcast.12, bf16[2048,2048]{1,0:T(8,128)(2,1)} %x_hbm.1, ...), custom_call_target="tpu_custom_call" | custom-call | flops 2147483648 | bytes 1048576 | tf_op jit(solution)/shard_map/front/pallas_call | solution.py:61
  5.9 3.2 %collective-permute-start.1 = (bf16[512,256]{1,0:T(8,128)(2,1)S(1)}, bf16[512,256]{1,0:T(8,128)(2,1)S(1)}, u32[]{:S(2)}, u32[]{:S(2)}) collective-permute-start(bf16[512,256]{1,0:T(8,128)(2,1)S(1)} %get-tuple-element.70), channel_id=1, source_target_pairs={{0,2},{1,3},{2,0},{3,1},{4,6},{5,7},{6,4},{7,5},{8,10},{9,11},{10,... | collective-permute-start | bytes 786440 | tf_op jit(solution)/shard_map/ppermute | solution.py:529
  9.1 2.1 %coef.1 = (bf16[512,256]{1,0:T(8,128)(2,1)S(1)}, bf16[512,256]{1,0:T(8,128)(2,1)S(1)}, bf16[512,256]{1,0:T(8,128)(2,1)S(1)}, bf16[512,256]{1,0:T(8,128)(2,1)S(1)}) custom-call(s32[255]{0:T(256)S(1)} %copy-done.5, bf16[256,2048]{1,0:T(8,128)(2,1)S(1)} %get-tuple-element.63.basis_t, bf16[2048,2048]{1,0:T(8,128)(2,1)S(1)} %get-tuple-element.64.x.x_in, ...), custom_call_target="tpu_custom_call" | custom-call | flops 1073741824 | bytes 1048576 | tf_op jit(solution)/shard_map/coef/pallas_call | solution.py:61
  11.2 0.7 collective-permute-start
  11.9 2.6 %collective-permute-start.2 = (bf16[512,256]{1,0:T(8,128)(2,1)S(1)}, bf16[512,256]{1,0:T(8,128)(2,1)S(1)}, u32[]{:S(2)}, u32[]{:S(2)}) collective-permute-start(bf16[512,256]{1,0:T(8,128)(2,1)S(1)} %get-tuple-element.71), channel_id=1, source_target_pairs={{0,3},{1,0},{2,1},{3,2},{4,7},{5,4},{6,5},{7,6},{8,11},{9,8},{10,9... | collective-permute-start | bytes 786440 | tf_op jit(solution)/shard_map/ppermute | solution.py:529
  14.5 6.8 %move.1 = (bf16[2048,256]{1,0:T(8,128)(2,1)S(1)}, bf16[2048,2048]{1,0:T(8,128)(2,1)S(1)}, bf16[2048,2048]{1,0:T(8,128)(2,1)S(1)}, bf16[512,256]{1,0:T(8,128)(2,1)S(1)}, f32[34816,128]{1,0:T(8,128)S(1)}) custom-call(s32[255]{0:T(256)S(1)} %copy-done.5, s32[1,2048]{1,0:T(1,128)S(1)} %copy-done.3, ...), custom_call_target="tpu_custom_call", output_to_operand_aliasing={{1}: (7, {})} | custom-call | flops 8589934592 | bytes 1048576 | tf_op jit(solution)/shard_map/move/pallas_call | solution.py:61
  21.3 0.0 copy-start
  21.3 2.7 %near_0.1.near_in = f32[34816,128]{1,0:T(8,128)S(1)} custom-call(s32[1,2048]{1,0:T(1,128)S(1)} %copy-done.3, bf16[2048,2048]{1,0:T(8,128)(2,1)S(1)} %get-tuple-element.73.d, bf16[2048,2048]{1,0:T(8,128)(2,1)S(1)} %get-tuple-element.74.x, f32[34816,128]{1,0:T(8,128)S(1)} %get-tuple-element.75.near_in), custom_call_target="tpu_custom_call", output_to_operand_aliasing={{}: (3, {})} | custom-call | flops 2147483648 | bytes 1048576 | tf_op jit(solution)/shard_map/near_0/pallas_call | solution.py:61
  24.0 0.0 collective-permute-done.1.u2
  24.0 0.0 collective-permute-done.u1
  24.0 0.0 collective-permute-done.2.u3
  24.1 1.1 %quad_up.1 = (bf16[2,512,256]{2,1,0:T(8,128)(2,1)S(1)}, bf16[128,256]{1,0:T(8,128)(2,1)S(1)}, bf16[128,256]{1,0:T(8,128)(2,1)S(1)}, bf16[128,256]{1,0:T(8,128)(2,1)S(1)}, bf16[128,256]{1,0:T(8,128)(2,1)S(1)}) custom-call(s32[255]{0:T(256)S(1)} %copy-done.5, bf16[512,256]{1,0:T(8,128)(2,1)S(1)} %get-tuple-element.77.u0, ...), custom_call_target="tpu_custom_call" | custom-call | flops 268435456 | bytes 1048576 | tf_op jit(solution)/shard_map/quad_up/pallas_call | solution.py:61
  25.2 0.1 collective-permute-start.13
  25.3 2.0 %collective-permute-start.3 = (bf16[128,256]{1,0:T(8,128)(2,1)S(1)}, bf16[128,256]{1,0:T(8,128)(2,1)S(1)}, u32[]{:S(2)}, u32[]{:S(2)}) collective-permute-start(bf16[128,256]{1,0:T(8,128)(2,1)S(1)} %get-tuple-element.86), channel_id=1, source_target_pairs={{0,4},{1,5},{2,6},{3,7},{4,8},{5,9},{6,10},{7,11},{8,12},{9,13},{1... | collective-permute-start | bytes 196616 | tf_op jit(solution)/shard_map/ppermute | solution.py:534
  27.2 3.6 %collective-permute-start.4 = (bf16[128,256]{1,0:T(8,128)(2,1)S(1)}, bf16[128,256]{1,0:T(8,128)(2,1)S(1)}, u32[]{:S(2)}, u32[]{:S(2)}) collective-permute-start(bf16[128,256]{1,0:T(8,128)(2,1)S(1)} %get-tuple-element.87), channel_id=1, source_target_pairs={{0,8},{1,9},{2,10},{3,11},{4,12},{5,13},{6,14},{7,15},{8,0},{9,1},... | collective-permute-start | bytes 196616 | tf_op jit(solution)/shard_map/ppermute | solution.py:534
  30.8 1.0 %collective-permute-start.5 = (bf16[128,256]{1,0:T(8,128)(2,1)S(1)}, bf16[128,256]{1,0:T(8,128)(2,1)S(1)}, u32[]{:S(2)}, u32[]{:S(2)}) collective-permute-start(bf16[128,256]{1,0:T(8,128)(2,1)S(1)} %get-tuple-element.88), channel_id=1, source_target_pairs={{0,12},{1,13},{2,14},{3,15},{4,0},{5,1},{6,2},{7,3},{8,4},{9,5},{1... | collective-permute-start | bytes 196616 | tf_op jit(solution)/shard_map/ppermute | solution.py:534
  31.8 2.7 %near_256.1.near_in = f32[34816,128]{1,0:T(8,128)S(1)} custom-call(s32[1,2048]{1,0:T(1,128)S(1)} %copy-done.3, bf16[2048,2048]{1,0:T(8,128)(2,1)S(1)} %get-tuple-element.73.d, bf16[2048,2048]{1,0:T(8,128)(2,1)S(1)} %get-tuple-element.74.x, f32[34816,128]{1,0:T(8,128)S(1)} %near_0.1.near_in), custom_call_target="tpu_custom_call", output_to_operand_aliasing={{}: (3, {})} | custom-call | flops 2147483648 | bytes 1048576 | tf_op jit(solution)/shard_map/near_256/pallas_call | solution.py:61
  34.5 0.0 collective-permute-done.3.q1
  34.5 0.0 collective-permute-done.4.q2
  34.5 0.5 collective-permute-done.5.q3
  35.1 1.1 %group_up.1 = (bf16[4,128,256]{2,1,0:T(8,128)(2,1)S(1)}, bf16[2,128,256]{2,1,0:T(8,128)(2,1)S(1)}, f32[2,128,256]{2,1,0:T(8,128)S(1)}) custom-call(s32[255]{0:T(256)S(1)} %copy-done.5, bf16[128,256]{1,0:T(8,128)(2,1)S(1)} %get-tuple-element.90.q0, bf16[128,256]{1,0:T(8,128)(2,1)S(1)} %collective-permute-done.3.q1, ...), custom_call_target="tpu_custom_call" | custom-call | flops 268435456 | bytes 1048576 | tf_op jit(solution)/shard_map/group_up/pallas_call | solution.py:61
  36.2 0.1 collective-permute-start.6
  36.3 1.5 %collective-permute-done.6.peer.peer4 = f32[2,128,256]{2,1,0:T(8,128)S(1)} collective-permute-done((f32[2,128,256]{2,1,0:T(8,128)S(1)}, f32[2,128,256]{2,1,0:T(8,128)S(1)}, u32[]{:S(2)}, u32[]{:S(2)}) %collective-permute-start.6) | collective-permute-done | bytes 262176 | tf_op jit(solution)/shard_map/ppermute | solution.py:542
  37.8 0.6 five.1.y0
  38.4 0.0 copy-start.2
  38.4 0.0 copy-start.4
  38.4 3.1 %collective-permute-start.9 = (bf16[128,256]{1,0:T(8,128)(2,1)S(1)}, bf16[128,256]{1,0:T(8,128)(2,1)S(1)}, u32[]{:S(2)}, u32[]{:S(2)}) collective-permute-start(bf16[128,256]{1,0:T(8,128)(2,1)S(1)} %five.1.y0), channel_id=1, source_target_pairs={{0,96},{16,112},{32,64},{48,80},{64,32},{80,48},{96,0},{112,16},{1... | collective-permute-start | bytes 196616 | tf_op jit(solution)/shard_map/ppermute | solution.py:542
  41.5 0.6 collective-permute-start.8
  42.1 0.5 collective-permute-start.7
  42.6 2.7 %near_512.1.near_in = f32[34816,128]{1,0:T(8,128)S(1)} custom-call(s32[1,2048]{1,0:T(1,128)S(1)} %copy-done.3, bf16[2048,2048]{1,0:T(8,128)(2,1)S(1)} %get-tuple-element.73.d, bf16[2048,2048]{1,0:T(8,128)(2,1)S(1)} %get-tuple-element.74.x, f32[34816,128]{1,0:T(8,128)S(1)} %near_256.1.near_in), custom_call_target="tpu_custom_call", output_to_operand_aliasing={{}: (3, {})} | custom-call | flops 2147483648 | bytes 1048576 | tf_op jit(solution)/shard_map/near_512/pallas_call | solution.py:61
  45.3 0.0 collective-permute-done.9.y3
  45.3 2.3 %collective-permute-done.8.y2 = bf16[128,256]{1,0:T(8,128)(2,1)S(1)} collective-permute-done((bf16[128,256]{1,0:T(8,128)(2,1)S(1)}, bf16[128,256]{1,0:T(8,128)(2,1)S(1)}, u32[]{:S(2)}, u32[]{:S(2)}) %collective-permute-start.8) | collective-permute-done | bytes 65568 | tf_op jit(solution)/shard_map/ppermute | solution.py:542
  47.5 0.0 collective-permute-done.7.y1
  47.6 2.3 %top.1 = (bf16[128,256]{1,0:T(8,128)(2,1)S(1)}, bf16[128,256]{1,0:T(8,128)(2,1)S(1)}, bf16[128,256]{1,0:T(8,128)(2,1)S(1)}, bf16[128,256]{1,0:T(8,128)(2,1)S(1)}) custom-call(s32[255]{0:T(256)S(1)} %copy-done.5, bf16[128,256]{1,0:T(8,128)(2,1)S(1)} %five.1.y0, bf16[128,256]{1,0:T(8,128)(2,1)S(1)} %collective-permute-done.7.y1, ...), custom_call_target="tpu_custom_call" | custom-call | flops 268435456 | bytes 1048576 | tf_op jit(solution)/shard_map/top/pallas_call | solution.py:61
  49.9 0.5 collective-permute-start.10
  50.4 3.2 %collective-permute-start.11 = (bf16[128,256]{1,0:T(8,128)(2,1)S(1)}, bf16[128,256]{1,0:T(8,128)(2,1)S(1)}, u32[]{:S(2)}, u32[]{:S(2)}) collective-permute-start(bf16[128,256]{1,0:T(8,128)(2,1)S(1)} %get-tuple-element.104), channel_id=1, source_target_pairs={{0,8},{1,9},{2,10},{3,11},{4,12},{5,13},{6,14},{7,15},{8,0},{9,1},... | collective-permute-start | bytes 196616 | tf_op jit(solution)/shard_map/ppermute | solution.py:534
  53.7 0.5 collective-permute-start.12
  54.1 2.7 %near_768.1.near_in = f32[34816,128]{1,0:T(8,128)S(1)} custom-call(s32[1,2048]{1,0:T(1,128)S(1)} %copy-done.3, bf16[2048,2048]{1,0:T(8,128)(2,1)S(1)} %get-tuple-element.73.d, bf16[2048,2048]{1,0:T(8,128)(2,1)S(1)} %get-tuple-element.74.x, f32[34816,128]{1,0:T(8,128)S(1)} %near_512.1.near_in), custom_call_target="tpu_custom_call", output_to_operand_aliasing={{}: (3, {})} | custom-call | flops 2147483648 | bytes 1048576 | tf_op jit(solution)/shard_map/near_768/pallas_call | solution.py:61
  56.8 1.1 %collective-permute-done.12.f3 = bf16[128,256]{1,0:T(8,128)(2,1)S(1)} collective-permute-done((bf16[128,256]{1,0:T(8,128)(2,1)S(1)}, bf16[128,256]{1,0:T(8,128)(2,1)S(1)}, u32[]{:S(2)}, u32[]{:S(2)}) %collective-permute-start.12) | collective-permute-done | bytes 65568 | tf_op jit(solution)/shard_map/ppermute | solution.py:534
  57.9 0.0 collective-permute-done.13.sibling
  57.9 1.1 %quad_down.1 = (bf16[512,256]{1,0:T(8,128)(2,1)S(1)}, bf16[512,256]{1,0:T(8,128)(2,1)S(1)}, bf16[512,256]{1,0:T(8,128)(2,1)S(1)}, bf16[512,256]{1,0:T(8,128)(2,1)S(1)}) custom-call(s32[255]{0:T(256)S(1)} %copy-done.5, bf16[128,256]{1,0:T(8,128)(2,1)S(1)} %get-tuple-element.110.f0, bf16[128,256]{1,0:T(8,128)(2,1)S(1)} %collective-permute-done.10.f1, ...), custom_call_target="tpu_custom_call" | custom-call | flops 268435456 | bytes 1048576 | tf_op jit(solution)/shard_map/quad_down/pallas_call | solution.py:61
  59.1 2.0 %collective-permute-start.14 = (bf16[512,256]{1,0:T(8,128)(2,1)S(1)}, bf16[512,256]{1,0:T(8,128)(2,1)S(1)}, u32[]{:S(2)}, u32[]{:S(2)}) collective-permute-start(bf16[512,256]{1,0:T(8,128)(2,1)S(1)} %get-tuple-element.116), channel_id=1, source_target_pairs={{0,1},{1,2},{2,3},{3,0},{4,5},{5,6},{6,7},{7,4},{8,9},{9,10},{10,1... | collective-permute-start | bytes 786440 | tf_op jit(solution)/shard_map/ppermute | solution.py:529
  61.1 1.3 %collective-permute-start.15 = (bf16[512,256]{1,0:T(8,128)(2,1)S(1)}, bf16[512,256]{1,0:T(8,128)(2,1)S(1)}, u32[]{:S(2)}, u32[]{:S(2)}) collective-permute-start(bf16[512,256]{1,0:T(8,128)(2,1)S(1)} %get-tuple-element.117), channel_id=1, source_target_pairs={{0,3},{1,0},{2,1},{3,2},{4,7},{5,4},{6,5},{7,6},{8,11},{9,8},{10,9... | collective-permute-start | bytes 786440 | tf_op jit(solution)/shard_map/ppermute | solution.py:529
  62.4 0.9 %collective-permute-start.16 = (bf16[512,256]{1,0:T(8,128)(2,1)S(1)}, bf16[512,256]{1,0:T(8,128)(2,1)S(1)}, u32[]{:S(2)}, u32[]{:S(2)}) collective-permute-start(bf16[512,256]{1,0:T(8,128)(2,1)S(1)} %get-tuple-element.118), channel_id=1, source_target_pairs={{0,2},{1,3},{2,0},{3,1},{4,6},{5,7},{6,4},{7,5},{8,10},{9,11},{10,... | collective-permute-start | bytes 786440 | tf_op jit(solution)/shard_map/ppermute | solution.py:529
  63.2 9.9 %near_1024.1.near = f32[34816,128]{1,0:T(8,128)S(1)} custom-call(s32[1,2048]{1,0:T(1,128)S(1)} %copy-done.3, bf16[2048,2048]{1,0:T(8,128)(2,1)S(1)} %get-tuple-element.73.d, bf16[2048,2048]{1,0:T(8,128)(2,1)S(1)} %get-tuple-element.74.x, f32[34816,128]{1,0:T(8,128)S(1)} %near_768.1.near_in), custom_call_target="tpu_custom_call", output_to_operand_aliasing={{}: (3, {})} | custom-call | flops 8589934592 | bytes 1048576 | tf_op jit(solution)/shard_map/near_1024/pallas_call | solution.py:61
  73.1 0.0 collective-permute-done.14.refs_1_
  73.1 0.0 collective-permute-done.15.refs_2_
  73.1 5.4 %tail_0132.1 = bf16[2048,2048]{1,0:T(8,128)(2,1)} custom-call(s32[255]{0:T(256)S(1)} %copy-done.5, bf16[2048,256]{1,0:T(8,128)(2,1)S(1)} %get-tuple-element.62.basis, bf16[2048,256]{1,0:T(8,128)(2,1)S(1)} %collective-permute-done.13.sibling, bf16[2,256,256]{2,1,0:T(8,128)(2,1)S(1)} %bitcast.11, f32[34816,128]{1,0:T(8,128)S(1)} %near_1024.1.near, ...), custom_call_target="tpu_custom_call" | custom-call | flops 536870912 | bytes 3145728 | tf_op jit(solution)/shard_map/tail_0132/pallas_call | solution.py:511
  (12 shorter events, 0.0 us)
Async XLA Ops:
  0.0 9.1 %copy-start.5 = (s32[255]{0:T(256)S(1)}, s32[255]{0:T(256)}, u32[]{:S(2)}) copy-start(s32[255]{0:T(256)} %ranks.15) | copy-start | bytes 3064
  0.0 9.1 %copy-start.1 = (bf16[1,2,256,256]{3,2,1,0:T(8,128)(2,1)S(1)}, bf16[1,2,256,256]{3,2,1,0:T(8,128)(2,1)}, u32[]{:S(2)}) copy-start(bf16[1,2,256,256]{3,2,1,0:T(8,128)(2,1)} %param.13) | copy-start | bytes 786436
  0.0 14.5 %copy-start.3 = (s32[1,2048]{1,0:T(1,128)S(1)}, s32[1,2048]{1,0:T(1,128)}, u32[]{:S(2)}) copy-start(s32[1,2048]{1,0:T(1,128)} %order.11) | copy-start | bytes 24580
  5.9 18.2 %collective-permute-start.1 = (bf16[512,256]{1,0:T(8,128)(2,1)S(1)}, bf16[512,256]{1,0:T(8,128)(2,1)S(1)}, u32[]{:S(2)}, u32[]{:S(2)}) collective-permute-start(bf16[512,256]{1,0:T(8,128)(2,1)S(1)} %get-tuple-element.70), channel_id=1, source_target_pairs={{0,2},{1,3},{2,0},{3,1},{4,6},{5,7},{6,4},{7,5},{8,10},{9,11},{10,... | collective-permute-start | bytes 786440 | tf_op jit(solution)/shard_map/ppermute | solution.py:529
  11.2 12.8 %collective-permute-start = (bf16[512,256]{1,0:T(8,128)(2,1)S(1)}, bf16[512,256]{1,0:T(8,128)(2,1)S(1)}, u32[]{:S(2)}, u32[]{:S(2)}) collective-permute-start(bf16[512,256]{1,0:T(8,128)(2,1)S(1)} %get-tuple-element.69), channel_id=1, source_target_pairs={{0,1},{1,2},{2,3},{3,0},{4,5},{5,6},{6,7},{7,4},{8,9},{9,10},{10,1... | collective-permute-start | bytes 786440 | tf_op jit(solution)/shard_map/ppermute | solution.py:529
  11.9 12.2 %collective-permute-start.2 = (bf16[512,256]{1,0:T(8,128)(2,1)S(1)}, bf16[512,256]{1,0:T(8,128)(2,1)S(1)}, u32[]{:S(2)}, u32[]{:S(2)}) collective-permute-start(bf16[512,256]{1,0:T(8,128)(2,1)S(1)} %get-tuple-element.71), channel_id=1, source_target_pairs={{0,3},{1,0},{2,1},{3,2},{4,7},{5,4},{6,5},{7,6},{8,11},{9,8},{10,9... | collective-permute-start | bytes 786440 | tf_op jit(solution)/shard_map/ppermute | solution.py:529
  21.3 2.7 %copy-start = (bf16[1,15,2,256,256]{4,3,2,1,0:T(8,128)(2,1)S(1)}, bf16[1,15,2,256,256]{4,3,2,1,0:T(8,128)(2,1)}, u32[]{:S(2)}) copy-start(bf16[1,15,2,256,256]{4,3,2,1,0:T(8,128)(2,1)} %param.14) | copy-start | bytes 11796484
  25.2 32.8 %collective-permute-start.13 = (bf16[2048,256]{1,0:T(8,128)(2,1)S(1)}, bf16[2048,256]{1,0:T(8,128)(2,1)S(1)}, u32[]{:S(2)}, u32[]{:S(2)}) collective-permute-start(bf16[2048,256]{1,0:T(8,128)(2,1)S(1)} %get-tuple-element.107), channel_id=1, source_target_pairs={{0,1},{1,0},{2,3},{3,2},{4,5},{5,4},{6,7},{7,6},{8,9},{9,8},{10,11... | collective-permute-start | bytes 3145736 | tf_op jit(solution)/shard_map/ppermute | solution.py:538
  25.3 9.3 %collective-permute-start.3 = (bf16[128,256]{1,0:T(8,128)(2,1)S(1)}, bf16[128,256]{1,0:T(8,128)(2,1)S(1)}, u32[]{:S(2)}, u32[]{:S(2)}) collective-permute-start(bf16[128,256]{1,0:T(8,128)(2,1)S(1)} %get-tuple-element.86), channel_id=1, source_target_pairs={{0,4},{1,5},{2,6},{3,7},{4,8},{5,9},{6,10},{7,11},{8,12},{9,13},{1... | collective-permute-start | bytes 196616 | tf_op jit(solution)/shard_map/ppermute | solution.py:534
  27.2 7.3 %collective-permute-start.4 = (bf16[128,256]{1,0:T(8,128)(2,1)S(1)}, bf16[128,256]{1,0:T(8,128)(2,1)S(1)}, u32[]{:S(2)}, u32[]{:S(2)}) collective-permute-start(bf16[128,256]{1,0:T(8,128)(2,1)S(1)} %get-tuple-element.87), channel_id=1, source_target_pairs={{0,8},{1,9},{2,10},{3,11},{4,12},{5,13},{6,14},{7,15},{8,0},{9,1},... | collective-permute-start | bytes 196616 | tf_op jit(solution)/shard_map/ppermute | solution.py:534
  30.8 4.3 %collective-permute-start.5 = (bf16[128,256]{1,0:T(8,128)(2,1)S(1)}, bf16[128,256]{1,0:T(8,128)(2,1)S(1)}, u32[]{:S(2)}, u32[]{:S(2)}) collective-permute-start(bf16[128,256]{1,0:T(8,128)(2,1)S(1)} %get-tuple-element.88), channel_id=1, source_target_pairs={{0,12},{1,13},{2,14},{3,15},{4,0},{5,1},{6,2},{7,3},{8,4},{9,5},{1... | collective-permute-start | bytes 196616 | tf_op jit(solution)/shard_map/ppermute | solution.py:534
  36.2 1.6 %collective-permute-start.6 = (f32[2,128,256]{2,1,0:T(8,128)S(1)}, f32[2,128,256]{2,1,0:T(8,128)S(1)}, u32[]{:S(2)}, u32[]{:S(2)}) collective-permute-start(f32[2,128,256]{2,1,0:T(8,128)S(1)} %get-tuple-element.94.own), channel_id=1, source_target_pairs={{0,16},{16,0},{32,48},{48,32},{64,80},{80,64},{96,112},{112,96},{1... | collective-permute-start | bytes 786440 | tf_op jit(solution)/shard_map/ppermute | solution.py:542
  38.4 9.2 %copy-start.2 = (bf16[6,2,256,256]{3,2,1,0:T(8,128)(2,1)S(1)}, bf16[6,2,256,256]{3,2,1,0:T(8,128)(2,1)}, u32[]{:S(2)}) copy-start(bf16[6,2,256,256]{3,2,1,0:T(8,128)(2,1)} %outer.1) | copy-start | bytes 4718596
  38.4 9.2 %copy-start.4 = (bf16[256,256]{1,0:T(8,128)(2,1)S(1)}, bf16[256,256]{1,0:T(8,128)(2,1)}, u32[]{:S(2)}) copy-start(bf16[256,256]{1,0:T(8,128)(2,1)} %root.1) | copy-start | bytes 393220
  38.4 6.9 %collective-permute-start.9 = (bf16[128,256]{1,0:T(8,128)(2,1)S(1)}, bf16[128,256]{1,0:T(8,128)(2,1)S(1)}, u32[]{:S(2)}, u32[]{:S(2)}) collective-permute-start(bf16[128,256]{1,0:T(8,128)(2,1)S(1)} %five.1.y0), channel_id=1, source_target_pairs={{0,96},{16,112},{32,64},{48,80},{64,32},{80,48},{96,0},{112,16},{1... | collective-permute-start | bytes 196616 | tf_op jit(solution)/shard_map/ppermute | solution.py:542
  41.5 6.1 %collective-permute-start.8 = (bf16[128,256]{1,0:T(8,128)(2,1)S(1)}, bf16[128,256]{1,0:T(8,128)(2,1)S(1)}, u32[]{:S(2)}, u32[]{:S(2)}) collective-permute-start(bf16[128,256]{1,0:T(8,128)(2,1)S(1)} %five.1.y0), channel_id=1, source_target_pairs={{0,64},{16,80},{32,96},{48,112},{64,0},{80,16},{96,32},{112,48},{1... | collective-permute-start | bytes 196616 | tf_op jit(solution)/shard_map/ppermute | solution.py:542
  42.1 5.4 %collective-permute-start.7 = (bf16[128,256]{1,0:T(8,128)(2,1)S(1)}, bf16[128,256]{1,0:T(8,128)(2,1)S(1)}, u32[]{:S(2)}, u32[]{:S(2)}) collective-permute-start(bf16[128,256]{1,0:T(8,128)(2,1)S(1)} %five.1.y0), channel_id=1, source_target_pairs={{0,32},{16,48},{32,0},{48,16},{64,96},{80,112},{96,64},{112,80},{1... | collective-permute-start | bytes 196616 | tf_op jit(solution)/shard_map/ppermute | solution.py:542
  49.9 6.9 %collective-permute-start.10 = (bf16[128,256]{1,0:T(8,128)(2,1)S(1)}, bf16[128,256]{1,0:T(8,128)(2,1)S(1)}, u32[]{:S(2)}, u32[]{:S(2)}) collective-permute-start(bf16[128,256]{1,0:T(8,128)(2,1)S(1)} %get-tuple-element.103), channel_id=1, source_target_pairs={{0,4},{1,5},{2,6},{3,7},{4,8},{5,9},{6,10},{7,11},{8,12},{9,13},{1... | collective-permute-start | bytes 196616 | tf_op jit(solution)/shard_map/ppermute | solution.py:534
  50.4 6.4 %collective-permute-start.11 = (bf16[128,256]{1,0:T(8,128)(2,1)S(1)}, bf16[128,256]{1,0:T(8,128)(2,1)S(1)}, u32[]{:S(2)}, u32[]{:S(2)}) collective-permute-start(bf16[128,256]{1,0:T(8,128)(2,1)S(1)} %get-tuple-element.104), channel_id=1, source_target_pairs={{0,8},{1,9},{2,10},{3,11},{4,12},{5,13},{6,14},{7,15},{8,0},{9,1},... | collective-permute-start | bytes 196616 | tf_op jit(solution)/shard_map/ppermute | solution.py:534
  53.7 4.3 %collective-permute-start.12 = (bf16[128,256]{1,0:T(8,128)(2,1)S(1)}, bf16[128,256]{1,0:T(8,128)(2,1)S(1)}, u32[]{:S(2)}, u32[]{:S(2)}) collective-permute-start(bf16[128,256]{1,0:T(8,128)(2,1)S(1)} %get-tuple-element.105), channel_id=1, source_target_pairs={{0,12},{1,13},{2,14},{3,15},{4,0},{5,1},{6,2},{7,3},{8,4},{9,5},{1... | collective-permute-start | bytes 196616 | tf_op jit(solution)/shard_map/ppermute | solution.py:534
  59.1 14.0 %collective-permute-start.14 = (bf16[512,256]{1,0:T(8,128)(2,1)S(1)}, bf16[512,256]{1,0:T(8,128)(2,1)S(1)}, u32[]{:S(2)}, u32[]{:S(2)}) collective-permute-start(bf16[512,256]{1,0:T(8,128)(2,1)S(1)} %get-tuple-element.116), channel_id=1, source_target_pairs={{0,1},{1,2},{2,3},{3,0},{4,5},{5,6},{6,7},{7,4},{8,9},{9,10},{10,1... | collective-permute-start | bytes 786440 | tf_op jit(solution)/shard_map/ppermute | solution.py:529
  61.1 12.0 %collective-permute-start.15 = (bf16[512,256]{1,0:T(8,128)(2,1)S(1)}, bf16[512,256]{1,0:T(8,128)(2,1)S(1)}, u32[]{:S(2)}, u32[]{:S(2)}) collective-permute-start(bf16[512,256]{1,0:T(8,128)(2,1)S(1)} %get-tuple-element.117), channel_id=1, source_target_pairs={{0,3},{1,0},{2,1},{3,2},{4,7},{5,4},{6,5},{7,6},{8,11},{9,8},{10,9... | collective-permute-start | bytes 786440 | tf_op jit(solution)/shard_map/ppermute | solution.py:529
  62.4 10.8 %collective-permute-start.16 = (bf16[512,256]{1,0:T(8,128)(2,1)S(1)}, bf16[512,256]{1,0:T(8,128)(2,1)S(1)}, u32[]{:S(2)}, u32[]{:S(2)}) collective-permute-start(bf16[512,256]{1,0:T(8,128)(2,1)S(1)} %get-tuple-element.118), channel_id=1, source_target_pairs={{0,2},{1,3},{2,0},{3,1},{4,6},{5,7},{6,4},{7,5},{8,10},{9,11},{10,... | collective-permute-start | bytes 786440 | tf_op jit(solution)/shard_map/ppermute | solution.py:529

commit v4 on v3

--- a/solution.py
+++ b/solution.py
@@ -21,9 +21,13 @@
     return lax.dot_general(a, b, (((1,), (1,)), ((), ())), preferred_element_type=F32)
 
 
-def masked(value, rank):
+def masked(value, limit):
     lane = lax.broadcasted_iota(jnp.int32, value.shape, 1)
-    return jnp.where(lane < rank, value, 0.0).astype(BF)
+    return jnp.where(lane < limit, value, 0.0).astype(BF)
+
+
+def limit_of(table, heap_id):
+    return table[pl.ds(heap_id, 1), :]
 
 
 def params(limit):
@@ -46,7 +50,6 @@
     return pltpu.with_memory_space_constraint(x, space)
 
 
-SMEM = pl.BlockSpec(memory_space=pltpu.SMEM)
 VMEM = pl.BlockSpec(memory_space=pltpu.VMEM)
 HBM = pl.BlockSpec(memory_space=pltpu.HBM)
 
@@ -61,7 +64,7 @@
     return pl.pallas_call(
         kernel,
         out_shape=out_shapes,
-        in_specs=specs or [SMEM] + [VMEM] * (len(args) - 1),
+        in_specs=specs or [VMEM] * len(args),
         out_specs=(VMEM,) * len(out_shapes) if many else VMEM,
         input_output_aliases=alias,
         scratch_shapes=list(scratch),
@@ -109,20 +112,19 @@
     return nn(basis_t[...], x[:, pl.ds(start, cols)])
 
 
-def coef_finish(product, ranks, transfer, coef, piece):
-    ring, z, outer = place()
-    c = masked(product.T, ranks[127 + outer * 16 + z * RING + ring])
+def coef_finish(product, limit, transfer, coef, piece):
+    c = masked(product.T, limit[0:1])
     coef[...] = c
     piece[...] = nn(c, transfer[...]).astype(BF)
 
 
 def front_kernel(
     order_hbm, ranks_hbm, basis_hbm, x_hbm, node_hbm,
-    out, out_t, x, coef, piece,
+    out, out_t, x, coef, piece, limit,
     order, ranks, basis, transfer, src, dst, sem,
 ):
     cols = piece.shape[0]
-    ring = place()[0]
+    ring, z, outer = place()
 
     def fetch(k):
         start = pl.multiple_of(lax.rem(ring + (2, 1, 3, 0)[k], RING) * cols, cols)
@@ -141,9 +143,10 @@
         load.wait()
     for k in range(RING):
         fetch(k).start()
+    limit[...] = jnp.full(limit.shape, ranks[127 + outer * 16 + z * RING + ring], jnp.int32)
     shuffle_basis(order, basis, out, out_t, src, dst)
     fetch(0).wait()
-    coef_finish(coef_product(2, out_t, x), ranks, transfer, coef, piece)
+    coef_finish(coef_product(2, out_t, x), limit, transfer, coef, piece)
     for k in range(1, RING):
         fetch(k).wait()
 
@@ -160,6 +163,7 @@
             held(rows, cols),
             held(cols // RING, width),
             held(cols // RING, width),
+            pltpu.VMEM((8, width), jnp.int32),
         ),
         [pin(a, pltpu.HBM) for a in (order, ranks, basis, points, nodes)],
         flops=2**31,
@@ -177,19 +181,19 @@
     )
 
 
-def coef_kernel(ranks, basis_t, x, node, c1, c3, p1, p3):
+def coef_kernel(limit, basis_t, x, node, c1, c3, p1, p3):
     product1 = coef_product(1, basis_t, x)
     product3 = coef_product(3, basis_t, x)
-    coef_finish(product1, ranks, node.at[0], c1, p1)
-    coef_finish(product3, ranks, node.at[0], c3, p3)
-
-
-def coef_rest(ranks, basis_t, x, node):
+    coef_finish(product1, limit, node.at[0], c1, p1)
+    coef_finish(product3, limit, node.at[0], c3, p3)
+
+
+def coef_rest(limit, basis_t, x, node):
     return call(
         coef_kernel,
         "coef",
         (held(x.shape[1] // RING, basis_t.shape[0]),) * 4,
-        (ranks, *map(pin, (basis_t, x, node))),
+        tuple(map(pin, (limit, basis_t, x, node))),
         flops=2**30,
     )
 
@@ -244,9 +248,9 @@
 
 
 def move_kernel(
-    ranks, order, basis_t, node, c1, c2, c3, x_in, diag_hbm,
-    coef, x, diag, piece, src,
-    even, odd, scaled, row_at, sem,
+    limit, order, basis_t, node, c1, c2, c3, x_in, diag_hbm, ranks_hbm,
+    coef, x, diag, piece, src, table,
+    even, odd, scaled, row_at, ranks, sem,
 ):
     size = diag.shape[0] // 4
     loads = []
@@ -257,22 +261,27 @@
     scaled[...] = order[...] * PITCH
     load = pltpu.make_async_copy(scaled, row_at, sem.at[4])
     load.start()
+    load_ranks = pltpu.make_async_copy(ranks_hbm, ranks, sem.at[5])
+    load_ranks.start()
     cols = piece.shape[0]
     ring = place()[0]
 
     def rows_of(shift):
         return coef.at[pl.ds(pl.multiple_of(((ring + shift) & 3) * cols, cols), cols)]
 
-    coef_finish(coef_product(0, basis_t, x), ranks, node.at[0], rows_of(0), piece)
+    coef_finish(coef_product(0, basis_t, x), limit, node.at[0], rows_of(0), piece)
     for shift, ref in ((1, c1), (2, c2), (3, c3)):
         rows_of(shift)[...] = ref[...]
+    load_ranks.wait()
+    for node_id in range(ranks.shape[0]):
+        table[node_id : node_id + 1] = jnp.full((1, table.shape[1]), ranks[node_id], jnp.int32)
     load.wait()
     move_rows(row_at, x, src, (even, odd))
     for load in loads:
         load.wait()
 
 
-def move(ranks, order, basis_t, node, coefs, x, diag):
+def move(limit, ranks, order, basis_t, node, coefs, x, diag):
     rows, cols = x.shape
     width = basis_t.shape[0]
     return call(
@@ -284,8 +293,13 @@
             held(rows, cols),
             held(cols // RING, width),
             pltpu.VMEM((rows * PITCH, 128), F32),
+            pltpu.VMEM((ranks.shape[0] + 1, width), jnp.int32),
         ),
-        (ranks, *map(pin, (order, basis_t, node, *coefs, x)), pin(diag, pltpu.HBM)),
+        (
+            *map(pin, (limit, order, basis_t, node, *coefs, x)),
+            pin(diag, pltpu.HBM),
+            pin(ranks, pltpu.HBM),
+        ),
         flops=2**33,
         limit=6,
         scratch=[
@@ -293,9 +307,10 @@
             pltpu.VMEM((GROUP * PITCH, 128), F32),
             pltpu.VMEM(order.shape, jnp.int32),
             pltpu.SMEM(order.shape, jnp.int32),
-            pltpu.SemaphoreType.DMA((5,)),
+            pltpu.SMEM(ranks.shape, jnp.int32),
+            pltpu.SemaphoreType.DMA((6,)),
         ],
-        specs=[SMEM] + [VMEM] * 7 + [HBM],
+        specs=[VMEM] * 8 + [HBM] * 2,
         alias={7: 1},
     )
 
@@ -304,38 +319,29 @@
     block = even.shape[0] // PITCH
     load = pltpu.make_async_copy(order, row_at, sem)
     load.start()
-    waiting = []
-
-    def place_rows(count):
-        for _ in range(min(count, len(waiting))):
-            row, i, h, src = waiting.pop(0)
-            to = row_at[0, row + i] * PITCH
-            out[pl.ds(to + h, 8), :] = src[pl.ds(i * PITCH + h, 8), :]
-
-    steps = x.shape[1] // 256
     for k, row in enumerate(range(first, first + size, block)):
         src = (even, odd)[k % 2]
-        for j in range(steps):
-            spread(nn(d[row : row + block], x[:, j * 256 : (j + 1) * 256]), 0, j * 2, src)
-            if k == 0 and j == steps // 2 - 1:
-                load.wait()
-            place_rows(2 * block // steps)
-            if j == steps // 2 - 1 or j == steps - 1:
-                waiting += [(row, i, 8 * (2 * j // steps), src) for i in range(block)]
-    place_rows(len(waiting))
+        for j in range(0, x.shape[1], 256):
+            spread(nn(d[row : row + block], x[:, j : j + 256]), 0, j // 128, src)
+        if k == 0:
+            load.wait()
+        for i in range(block):
+            to = row_at[0, row + i] * PITCH
+            for h in (0, 8):
+                out[pl.ds(to + h, 8), :] = src[pl.ds(i * PITCH + h, 8), :]
 
 
 def near_rows(first, size, order, diag, ordered, sofar):
     rows, depth = diag.shape
     cols = ordered.shape[1]
-    block = min(size, 512)
+    block = size if size <= 512 else size // 2
     return call(
         functools.partial(near_kernel, first, size),
         f"near_{first}",
         pltpu.VMEM((rows * PITCH, 128), F32),
         tuple(map(pin, (order, diag, ordered, sofar))),
         flops=2 * size * depth * cols,
-        limit=4 + block // 64,
+        limit=6 + block // 64,
         scratch=[pltpu.VMEM((block * PITCH, 128), F32)] * 2
         + [pltpu.SMEM(order.shape, jnp.int32), pltpu.SemaphoreType.DMA],
         specs=[VMEM] * 4,
@@ -343,7 +349,7 @@
     )
 
 
-def quad_up_kernel(ranks, u0, u1, u2, u3, inner, mid, p0, p1, p2, p3, leaf, top):
+def quad_up_kernel(table, u0, u1, u2, u3, inner, mid, p0, p1, p2, p3, leaf, top):
     x, z, outer = place()
     quad = outer * RING + z
     size = p0.shape[0]
@@ -351,38 +357,38 @@
         leaf[(x - s) & 3] = ref[...]
     for k in range(2):
         up = leaf[2 * k].astype(F32) + leaf[2 * k + 1].astype(F32)
-        mid[k] = masked(up, ranks[63 + 2 * quad + k])
+        mid[k] = masked(up, limit_of(table, 63 + 2 * quad + k))
     up = nn(mid[0], inner[2 * z, 0]) + nn(mid[1], inner[2 * z + 1, 0])
-    top[...] = masked(up, ranks[31 + quad])
+    top[...] = masked(up, limit_of(table, 31 + quad))
     for t, ref in enumerate((p0, p1, p2, p3)):
         ref[...] = top[pl.ds(pl.multiple_of(((z + t) & 3) * size, size), size), :]
 
 
-def quad_up(ranks, pieces, inner):
+def quad_up(table, pieces, inner):
     cols, width = pieces[0].shape
     return call(
         quad_up_kernel,
         "quad_up",
         (held(2, cols, width),) + (held(cols // RING, width),) * 4,
-        (ranks, *map(pin, pieces), pin(inner)),
+        (pin(table), *map(pin, pieces), pin(inner)),
         scratch=[pltpu.VMEM((4, cols, width), BF), pltpu.VMEM((cols, width), BF)],
     )
 
 
-def group_up_kernel(ranks, q0, q1, q2, q3, inner, out2, out3, lift):
+def group_up_kernel(table, q0, q1, q2, q3, inner, out2, out3, lift):
     x, z, group = place()
     for t, ref in enumerate((q0, q1, q2, q3)):
         out2[(z - t) & 3] = ref[...]
     for k in range(2):
         up = nn(out2[2 * k], inner[8 + 2 * k, 0]) + nn(out2[2 * k + 1], inner[9 + 2 * k, 0])
-        out3[k] = masked(up, ranks[15 + 2 * group + k])
+        out3[k] = masked(up, limit_of(table, 15 + 2 * group + k))
     up = nn(out3[0], inner[12, 0]) + nn(out3[1], inner[13, 0])
-    four = masked(up, ranks[7 + group])
+    four = masked(up, limit_of(table, 7 + group))
     lift[0] = four.astype(F32)
     lift[1] = nn(four, inner[14, 0])
 
 
-def group_up(ranks, pieces, inner):
+def group_up(table, pieces, inner):
     part, width = pieces[0].shape
     return call(
         group_up_kernel,
@@ -392,20 +398,20 @@
             held(2, part, width),
             pltpu.VMEM((2, part, width), F32),
         ),
-        (ranks, *map(pin, pieces), pin(inner)),
-    )
-
-
-def five_kernel(ranks, own, peer, out):
-    out[...] = masked(own[1] + peer[1], ranks[3 + (place()[2] >> 1)])
-
-
-def five_up(ranks, own, peer):
-    return call(five_kernel, "five", held(*own.shape[1:]), (ranks, pin(own), pin(peer)))
+        (pin(table), *map(pin, pieces), pin(inner)),
+    )
+
+
+def five_kernel(table, own, peer, out):
+    out[...] = masked(own[1] + peer[1], limit_of(table, 3 + (place()[2] >> 1)))
+
+
+def five_up(table, own, peer):
+    return call(five_kernel, "five", held(*own.shape[1:]), (pin(table), pin(own), pin(peer)))
 
 
 def top_kernel(
-    ranks, y0, y1, y2, y3, peer4, c2, c3, inner, outer, root, p0, p1, p2, p3, five, far2
+    table, y0, y1, y2, y3, peer4, c2, c3, inner, outer, root, p0, p1, p2, p3, five, far2
 ):
     x, z, group = place()
     y = group >> 1
@@ -415,36 +421,36 @@
     six = []
     for k in range(2):
         up = nn(five[2 * k], outer[2 * k, 0]) + nn(five[2 * k + 1], outer[2 * k + 1, 0])
-        six.append(masked(up, ranks[1 + k]))
+        six.append(masked(up, limit_of(table, 1 + k)))
     up = nn(six[0], outer[4, 0]) + nn(six[1], outer[5, 0])
-    seven = masked(up, ranks[0])
-    far = masked(nt(seven, root[...]), ranks[0])
+    seven = masked(up, limit_of(table, 0))
+    far = masked(nt(seven, root[...]), limit_of(table, 0))
     sib = jnp.where(half == 0, six[1].astype(F32), six[0].astype(F32)).astype(BF)
-    far = masked(nt(sib, outer[4 + half, 1]) + nt(far, outer[4 + half, 0]), ranks[1 + half])
-    far = masked(nt(five[y ^ 1], outer[y, 1]) + nt(far, outer[y, 0]), ranks[3 + y])
-    far = masked(nt(peer4[0].astype(BF), inner[14, 1]) + nt(far, inner[14, 0]), ranks[7 + group])
+    far = masked(nt(sib, outer[4 + half, 1]) + nt(far, outer[4 + half, 0]), limit_of(table, 1 + half))
+    far = masked(nt(five[y ^ 1], outer[y, 1]) + nt(far, outer[y, 0]), limit_of(table, 3 + y))
+    far = masked(nt(peer4[0].astype(BF), inner[14, 1]) + nt(far, inner[14, 0]), limit_of(table, 7 + group))
     for k in range(2):
         down = nt(c3[1 - k], inner[12 + k, 1]) + nt(far, inner[12 + k, 0])
-        far3 = masked(down, ranks[15 + 2 * group + k])
+        far3 = masked(down, limit_of(table, 15 + 2 * group + k))
         for i in (2 * k, 2 * k + 1):
             down = nt(c2[i ^ 1], inner[8 + i, 1]) + nt(far3, inner[8 + i, 0])
-            far2[i] = masked(down, ranks[31 + 4 * group + i])
+            far2[i] = masked(down, limit_of(table, 31 + 4 * group + i))
     for t, ref in enumerate((p0, p1, p2, p3)):
         ref[...] = far2[(z + t) & 3]
 
 
-def top_sweep(ranks, fives, peer4, c2, c3, inner, outer, root):
+def top_sweep(table, fives, peer4, c2, c3, inner, outer, root):
     part, width = fives[0].shape
     return call(
         top_kernel,
         "top",
         (held(part, width),) * 4,
-        (ranks, *map(pin, (*fives, peer4, c2, c3, inner, outer, root))),
+        (pin(table), *map(pin, (*fives, peer4, c2, c3, inner, outer, root))),
         scratch=[pltpu.VMEM((4, part, width), BF)] * 2,
     )
 
 
-def quad_down_kernel(ranks, f0, f1, f2, f3, mid, inner, p0, p1, p2, p3, far2, far1):
+def quad_down_kernel(table, f0, f1, f2, f3, mid, inner, p0, p1, p2, p3, far2, far1):
     x, z, outer = place()
     quad = outer * RING + z
     size = f0.shape[0]
@@ -452,19 +458,19 @@
         far2[pl.ds(pl.multiple_of(((z - t) & 3) * size, size), size), :] = ref[...]
     for k in range(2):
         down = nt(mid[1 - k], inner[2 * z + k, 1]) + nt(far2[...], inner[2 * z + k, 0])
-        far1[k] = masked(down, ranks[63 + 2 * quad + k])
+        far1[k] = masked(down, limit_of(table, 63 + 2 * quad + k))
     for s, ref in enumerate((p0, p1, p2, p3)):
         ref[...] = far1[((x + s) & 3) >> 1]
 
 
-def quad_down(ranks, fars, mid, inner):
+def quad_down(table, fars, mid, inner):
     part, width = fars[0].shape
     cols = part * RING
     return call(
         quad_down_kernel,
         "quad_down",
         (held(cols, width),) * 4,
-        (ranks, *map(pin, (*fars, mid, inner))),
+        (pin(table), *map(pin, (*fars, mid, inner))),
         scratch=[pltpu.VMEM((cols, width), BF), pltpu.VMEM((2, cols, width), BF)],
     )
 
@@ -472,19 +478,19 @@
 TAIL = 512
 
 
-def tail_kernel(shifts, ranks, basis, sibling, node, near, *refs):
+def tail_kernel(shifts, table, basis, sibling, node, near, *refs):
     fars = refs[: len(shifts)]
     o_hbm, buf, sem = refs[-3:]
     x, z, outer = place()
     cols = fars[0].shape[0]
-    rank = ranks[127 + outer * 16 + z * RING + x]
+    limit = limit_of(table, 127 + outer * 16 + z * RING + x)
     copies = []
     for i, (shift, far1) in enumerate(zip(shifts, fars)):
         part = (x - shift) & 3
         at = pl.ds(pl.multiple_of(part * cols, cols), cols)
         tiles = cols // 128
         down = nt(sibling[at, :], node[1]) + nt(far1[...], node[0])
-        far = masked(down, rank)
+        far = masked(down, limit)
         for row in range(0, basis.shape[0], TAIL):
             add = nt(basis[row : row + TAIL], far)
             value = gathered(row, TAIL, part * tiles, tiles, near) + add
@@ -498,11 +504,11 @@
         copy.wait()
 
 
-def add_far(shifts, ranks, basis, sibling, node, near, fars, sofar):
+def add_far(shifts, table, basis, sibling, node, near, fars, sofar):
     rows, width = basis.shape
     cols = fars[0].shape[0]
-    args = [ranks] + [pin(a) for a in (basis, sibling, node, near, *fars)]
-    specs = [SMEM] + [VMEM] * (len(args) - 1)
+    args = [pin(a) for a in (table, basis, sibling, node, near, *fars)]
+    specs = [VMEM] * len(args)
     alias = {}
     if sofar is not None:
         alias = {len(args): 0}
@@ -560,39 +566,42 @@
     root_coupling,
     node_ranks,
 ):
-    ranks = node_ranks
     inner = inner_nodes[0]
     node = leaf_nodes[0]
 
-    basis, basis_t, x, c2, piece = front(leaf_order, ranks, leaf_basis[0], points, node)
-    c1, c3, *others = coef_rest(ranks, basis_t, x, node)
+    basis, basis_t, x, c2, piece, limit = front(leaf_order, node_ranks, leaf_basis[0], points, node)
+    c1, c3, *others = coef_rest(limit, basis_t, x, node)
     sent = {2: ring_x(piece, 2), 1: ring_x(others[0], 1), 3: ring_x(others[1], 3)}
     coefs = (c1, c2, c3)
-    coef, ordered, diag, own, near = move(ranks, leaf_order, basis_t, node, coefs, x, diag_blocks[0])
+    coef, ordered, diag, own, near, table = move(
+        limit, node_ranks, leaf_order, basis_t, node, coefs, x, diag_blocks[0]
+    )
     near = near_rows(0, 256, leaf_order, diag, ordered, near)
     pieces = [own, sent[1], sent[2], sent[3]]
     *pieces, coef, near = lax.optimization_barrier((*pieces, coef, near))
 
-    mid, *parts = quad_up(ranks, pieces, inner)
+    mid, *parts = quad_up(table, pieces, inner)
     coef, *parts = lax.optimization_barrier((coef, *parts))
     parts = exchange(ring_z, parts)
     sibling = swap_inner(coef, 1)
     near = near_rows(256, 256, leaf_order, diag, ordered, near)
     *parts, near = lax.optimization_barrier((*parts, near))
-    c2, c3, lift = group_up(ranks, parts, inner)
+    c2, c3, lift = group_up(table, parts, inner)
     peer = swap_outer(lift, 1)
-    five = five_up(ranks, lift, peer)
+    near = near_rows(512, 128, leaf_order, diag, ordered, near)
+    peer, near = lax.optimization_barrier((peer, near))
+    five = five_up(table, lift, peer)
     fives = [five] + [swap_outer(five, 2 * s) for s in (1, 2, 3)]
-    near = near_rows(512, 256, leaf_order, diag, ordered, near)
+    near = near_rows(640, 256, leaf_order, diag, ordered, near)
     *fives, near = lax.optimization_barrier((*fives, near))
-    parts = top_sweep(ranks, fives, peer, c2, c3, inner, outer_nodes, root_coupling)
+    parts = top_sweep(table, fives, peer, c2, c3, inner, outer_nodes, root_coupling)
     parts = exchange(ring_z, parts)
-    near = near_rows(768, 256, leaf_order, diag, ordered, near)
+    near = near_rows(896, 256, leaf_order, diag, ordered, near)
     *parts, near, sibling = lax.optimization_barrier((*parts, near, sibling))
-    fars = quad_down(ranks, parts, mid, inner)
+    fars = quad_down(table, parts, mid, inner)
     fars = exchange(ring_x, fars)
-    near = near_rows(1024, 1024, leaf_order, diag, ordered, near)
-    add = functools.partial(add_far, ranks=ranks, basis=basis, sibling=sibling, node=node, near=near)
+    near = near_rows(1152, 896, leaf_order, diag, ordered, near)
+    add = functools.partial(add_far, table=table, basis=basis, sibling=sibling, node=node, near=near)
     return add((0, 1, 3, 2), fars=[fars[s] for s in (0, 1, 3, 2)], sofar=None)
 
 

time: 78.9 us -> 73.6 us (0.933)
  Pallas kernels: 47 us -> 42.6 us
  waiting for transfers between devices: 5.47 us -> 4.51 us
    pallas_call x13 -> x14, Pallas kernels: 41.6 us -> 37.7 us  [call(): pl.pallas_call(kernel, out_shape=out_shapes, in_specs=specs or [VMEM] * l...]
    ppermute x4, waiting for transfers between devices: 3.8 us -> 2.69 us  [swap_outer(): lax.ppermute(block, 'outer', [(o, o ^ bits) for o in range(2 * RING)])]
  transfers between devices with their start and end apart: 17 -> 17, of which waited for: 4 -> 4; matrix products, arithmetic and copies ran while one was open for 0% -> 0% of each run, Pallas kernels for 43% -> 42%
where the time goes in v4:
time: 73.6 us; the launch traced here: 73.4 us
  Pallas kernels  42.6 us (58%)
  starting transfers between devices  25.8 us (35%)
  waiting for transfers between devices  4.51 us (6%)
    pallas_call x14, Pallas kernels, call(): pl.pallas_call(kernel, out_shape=out_shapes, in_specs=specs or [VMEM] * l...  37.7 us
    ppermute x6, starting transfers between devices, ring_z(): return lax.ppermute(block, 'inner', route)  10.8 us
    ppermute x6, starting transfers between devices, ring_x(): return lax.ppermute(block, 'inner', route)  10.7 us
    pallas_call x1, Pallas kernels, add_far(): pl.pallas_call(functools.partial(tail_kernel, shifts), out_shape=sds(rows...  4.89 us
    ppermute x4, starting transfers between devices, swap_outer(): lax.ppermute(block, 'outer', [(o, o ^ bits) for o in range(2 * RING)])  4.31 us
    ppermute x4, waiting for transfers between devices, swap_outer(): lax.ppermute(block, 'outer', [(o, o ^ bits) for o in range(2 * RING)])  2.69 us
    ppermute x6, waiting for transfers between devices, ring_z(): return lax.ppermute(block, 'inner', route)  1.8 us
  transfers between devices with their start and end apart: 17, of which 4 were waited for; matrix products, arithmetic and copies ran while one was open for 0% of the time, Pallas kernels for 42%

profile of v4, /device:TPU:0, one launch (start us, length us, event | category | flops | bytes accessed | tf_op | source)
XLA Modules:
  0.0 73.4 jit_solution(16980335870460929256)
XLA Ops:
  0.0 5.9 %front.1 = (bf16[2048,256]{1,0:T(8,128)(2,1)S(1)}, bf16[256,2048]{1,0:T(8,128)(2,1)S(1)}, bf16[2048,2048]{1,0:T(8,128)(2,1)S(1)}, bf16[512,256]{1,0:T(8,128)(2,1...) custom-call(s32[1,2048]{1,0:T(1,128)} %order.13, s32[255]{0:T(256)} %ranks_hbm.3, bf16[2048,256]{1,0:T(8,128)(2,1)} %bitcast.12, ...), custom_call_target="tpu_custom_call" | custom-call | flops 2147483648 | bytes 1048576 | tf_op jit(solution)/shard_map/front/pallas_call | solution.py:64
  5.9 3.2 %collective-permute-start.1 = (bf16[512,256]{1,0:T(8,128)(2,1)S(1)}, bf16[512,256]{1,0:T(8,128)(2,1)S(1)}, u32[]{:S(2)}, u32[]{:S(2)}) collective-permute-start(bf16[512,256]{1,0:T(8,128)(2,1)S(1)} %get-tuple-element.76), channel_id=1, source_target_pairs={{0,2},{1,3},{2,0},{3,1},{4,6},{5,7},{6,4},{7,5},{8,10},{9,11},{10,... | collective-permute-start | bytes 786440 | tf_op jit(solution)/shard_map/ppermute | solution.py:535
  9.1 1.6 %coef.1 = (bf16[512,256]{1,0:T(8,128)(2,1)S(1)}, bf16[512,256]{1,0:T(8,128)(2,1)S(1)}, bf16[512,256]{1,0:T(8,128)(2,1)S(1)}, bf16[512,256]{1,0:T(8,128)(2,1)S(1)}) custom-call(s32[8,256]{1,0:T(8,128)S(1)} %get-tuple-element.66.limit, bf16[256,2048]{1,0:T(8,128)(2,1)S(1)} %get-tuple-element.67.basis_t, bf16[2048,2048]{1,0:T(8,128)(2,1)S(1)} %get-tuple-element.68.x.x_in, ...), custom_call_target="tpu_custom_call" | custom-call | flops 1073741824 | bytes 1048576 | tf_op jit(solution)/shard_map/coef/pallas_call | solution.py:64
  10.6 0.7 collective-permute-start
  11.3 2.6 %collective-permute-start.2 = (bf16[512,256]{1,0:T(8,128)(2,1)S(1)}, bf16[512,256]{1,0:T(8,128)(2,1)S(1)}, u32[]{:S(2)}, u32[]{:S(2)}) collective-permute-start(bf16[512,256]{1,0:T(8,128)(2,1)S(1)} %get-tuple-element.77), channel_id=1, source_target_pairs={{0,3},{1,0},{2,1},{3,2},{4,7},{5,4},{6,5},{7,6},{8,11},{9,8},{10,9... | collective-permute-start | bytes 786440 | tf_op jit(solution)/shard_map/ppermute | solution.py:535
  13.9 6.7 %move.1 = (bf16[2048,256]{1,0:T(8,128)(2,1)S(1)}, bf16[2048,2048]{1,0:T(8,128)(2,1)S(1)}, bf16[2048,2048]{1,0:T(8,128)(2,1)S(1)}, bf16[512,256]{1,0:T(8,128)(2,1...) custom-call(s32[8,256]{1,0:T(8,128)S(1)} %get-tuple-element.66.limit, ...), custom_call_target="tpu_custom_call", output_to_operand_aliasing={{1}: (7, {})} | custom-call | flops 8589934592 | bytes 1048576 | tf_op jit(solution)/shard_map/move/pallas_call | solution.py:64
  20.6 0.0 copy-start
  20.6 2.6 %near_0.1.near_in = f32[34816,128]{1,0:T(8,128)S(1)} custom-call(s32[1,2048]{1,0:T(1,128)S(1)} %copy-done.3, bf16[2048,2048]{1,0:T(8,128)(2,1)S(1)} %get-tuple-element.79.d, bf16[2048,2048]{1,0:T(8,128)(2,1)S(1)} %get-tuple-element.80.x, f32[34816,128]{1,0:T(8,128)S(1)} %get-tuple-element.81.near_in), custom_call_target="tpu_custom_call", output_to_operand_aliasing={{}: (3, {})} | custom-call | flops 2147483648 | bytes 1048576 | tf_op jit(solution)/shard_map/near_0/pallas_call | solution.py:64
  23.3 0.0 collective-permute-done.1.u2
  23.3 0.0 collective-permute-done.u1
  23.3 0.0 collective-permute-done.2.u3
  23.3 0.5 quad_up.1
  23.8 0.1 collective-permute-start.13
  23.9 2.0 %collective-permute-start.3 = (bf16[128,256]{1,0:T(8,128)(2,1)S(1)}, bf16[128,256]{1,0:T(8,128)(2,1)S(1)}, u32[]{:S(2)}, u32[]{:S(2)}) collective-permute-start(bf16[128,256]{1,0:T(8,128)(2,1)S(1)} %get-tuple-element.92), channel_id=1, source_target_pairs={{0,4},{1,5},{2,6},{3,7},{4,8},{5,9},{6,10},{7,11},{8,12},{9,13},{1... | collective-permute-start | bytes 196616 | tf_op jit(solution)/shard_map/ppermute | solution.py:540
  25.9 3.6 %collective-permute-start.4 = (bf16[128,256]{1,0:T(8,128)(2,1)S(1)}, bf16[128,256]{1,0:T(8,128)(2,1)S(1)}, u32[]{:S(2)}, u32[]{:S(2)}) collective-permute-start(bf16[128,256]{1,0:T(8,128)(2,1)S(1)} %get-tuple-element.93), channel_id=1, source_target_pairs={{0,8},{1,9},{2,10},{3,11},{4,12},{5,13},{6,14},{7,15},{8,0},{9,1},... | collective-permute-start | bytes 196616 | tf_op jit(solution)/shard_map/ppermute | solution.py:540
  29.5 1.0 %collective-permute-start.5 = (bf16[128,256]{1,0:T(8,128)(2,1)S(1)}, bf16[128,256]{1,0:T(8,128)(2,1)S(1)}, u32[]{:S(2)}, u32[]{:S(2)}) collective-permute-start(bf16[128,256]{1,0:T(8,128)(2,1)S(1)} %get-tuple-element.94), channel_id=1, source_target_pairs={{0,12},{1,13},{2,14},{3,15},{4,0},{5,1},{6,2},{7,3},{8,4},{9,5},{1... | collective-permute-start | bytes 196616 | tf_op jit(solution)/shard_map/ppermute | solution.py:540
  30.5 2.6 %near_256.1.near_in = f32[34816,128]{1,0:T(8,128)S(1)} custom-call(s32[1,2048]{1,0:T(1,128)S(1)} %copy-done.3, bf16[2048,2048]{1,0:T(8,128)(2,1)S(1)} %get-tuple-element.79.d, bf16[2048,2048]{1,0:T(8,128)(2,1)S(1)} %get-tuple-element.80.x, f32[34816,128]{1,0:T(8,128)S(1)} %near_0.1.near_in), custom_call_target="tpu_custom_call", output_to_operand_aliasing={{}: (3, {})} | custom-call | flops 2147483648 | bytes 1048576 | tf_op jit(solution)/shard_map/near_256/pallas_call | solution.py:64
  33.1 0.0 collective-permute-done.3.q1
  33.1 0.0 collective-permute-done.4.q2
  33.1 0.6 collective-permute-done.5.q3
  33.8 0.5 group_up.1
  34.3 0.1 collective-permute-start.6
  34.4 1.4 %near_512.1.near_in = f32[34816,128]{1,0:T(8,128)S(1)} custom-call(s32[1,2048]{1,0:T(1,128)S(1)} %copy-done.3, bf16[2048,2048]{1,0:T(8,128)(2,1)S(1)} %get-tuple-element.79.d, bf16[2048,2048]{1,0:T(8,128)(2,1)S(1)} %get-tuple-element.80.x, f32[34816,128]{1,0:T(8,128)S(1)} %near_256.1.near_in), custom_call_target="tpu_custom_call", output_to_operand_aliasing={{}: (3, {})} | custom-call | flops 1073741824 | bytes 1048576 | tf_op jit(solution)/shard_map/near_512/pallas_call | solution.py:64
  35.8 0.1 collective-permute-done.6.peer.peer4
  36.0 0.0 copy-start.2
  36.0 0.0 copy-start.4
  36.0 3.1 %collective-permute-start.9 = (bf16[128,256]{1,0:T(8,128)(2,1)S(1)}, bf16[128,256]{1,0:T(8,128)(2,1)S(1)}, u32[]{:S(2)}, u32[]{:S(2)}) collective-permute-start(bf16[128,256]{1,0:T(8,128)(2,1)S(1)} %five.1.y0), channel_id=1, source_target_pairs={{0,96},{16,112},{32,64},{48,80},{64,32},{80,48},{96,0},{112,16},{1... | collective-permute-start | bytes 196616 | tf_op jit(solution)/shard_map/ppermute | solution.py:548
  39.1 0.6 collective-permute-start.8
  39.7 0.5 collective-permute-start.7
  40.2 2.6 %near_640.1.near_in = f32[34816,128]{1,0:T(8,128)S(1)} custom-call(s32[1,2048]{1,0:T(1,128)S(1)} %copy-done.3, bf16[2048,2048]{1,0:T(8,128)(2,1)S(1)} %get-tuple-element.79.d, bf16[2048,2048]{1,0:T(8,128)(2,1)S(1)} %get-tuple-element.80.x, f32[34816,128]{1,0:T(8,128)S(1)} %near_512.1.near_in), custom_call_target="tpu_custom_call", output_to_operand_aliasing={{}: (3, {})} | custom-call | flops 2147483648 | bytes 1048576 | tf_op jit(solution)/shard_map/near_640/pallas_call | solution.py:64
  42.8 2.6 %collective-permute-done.8.y2 = bf16[128,256]{1,0:T(8,128)(2,1)S(1)} collective-permute-done((bf16[128,256]{1,0:T(8,128)(2,1)S(1)}, bf16[128,256]{1,0:T(8,128)(2,1)S(1)}, u32[]{:S(2)}, u32[]{:S(2)}) %collective-permute-start.8) | collective-permute-done | bytes 65568 | tf_op jit(solution)/shard_map/ppermute | solution.py:548
  45.4 1.8 %top.1 = (bf16[128,256]{1,0:T(8,128)(2,1)S(1)}, bf16[128,256]{1,0:T(8,128)(2,1)S(1)}, bf16[128,256]{1,0:T(8,128)(2,1)S(1)}, bf16[128,256]{1,0:T(8,128)(2,1)S(1)}) custom-call(s32[256,256]{1,0:T(8,128)S(1)} %get-tuple-element.72.table, bf16[128,256]{1,0:T(8,128)(2,1)S(1)} %five.1.y0, bf16[128,256]{1,0:T(8,128)(2,1)S(1)} %collective-permute-done.7.y1, ...), custom_call_target="tpu_custom_call" | custom-call | flops 268435456 | bytes 1048576 | tf_op jit(solution)/shard_map/top/pallas_call | solution.py:64
  47.2 0.5 collective-permute-start.10
  47.7 3.3 %collective-permute-start.11 = (bf16[128,256]{1,0:T(8,128)(2,1)S(1)}, bf16[128,256]{1,0:T(8,128)(2,1)S(1)}, u32[]{:S(2)}, u32[]{:S(2)}) collective-permute-start(bf16[128,256]{1,0:T(8,128)(2,1)S(1)} %get-tuple-element.112), channel_id=1, source_target_pairs={{0,8},{1,9},{2,10},{3,11},{4,12},{5,13},{6,14},{7,15},{8,0},{9,1},... | collective-permute-start | bytes 196616 | tf_op jit(solution)/shard_map/ppermute | solution.py:540
  51.0 0.5 collective-permute-start.12
  51.4 2.6 %near_896.1.near_in = f32[34816,128]{1,0:T(8,128)S(1)} custom-call(s32[1,2048]{1,0:T(1,128)S(1)} %copy-done.3, bf16[2048,2048]{1,0:T(8,128)(2,1)S(1)} %get-tuple-element.79.d, bf16[2048,2048]{1,0:T(8,128)(2,1)S(1)} %get-tuple-element.80.x, f32[34816,128]{1,0:T(8,128)S(1)} %near_640.1.near_in), custom_call_target="tpu_custom_call", output_to_operand_aliasing={{}: (3, {})} | custom-call | flops 2147483648 | bytes 1048576 | tf_op jit(solution)/shard_map/near_896/pallas_call | solution.py:64
  54.1 0.0 collective-permute-done.10.f1
  54.1 0.0 collective-permute-done.11.f2
  54.1 1.2 %collective-permute-done.12.f3 = bf16[128,256]{1,0:T(8,128)(2,1)S(1)} collective-permute-done((bf16[128,256]{1,0:T(8,128)(2,1)S(1)}, bf16[128,256]{1,0:T(8,128)(2,1)S(1)}, u32[]{:S(2)}, u32[]{:S(2)}) %collective-permute-start.12) | collective-permute-done | bytes 65568 | tf_op jit(solution)/shard_map/ppermute | solution.py:540
  55.2 0.0 collective-permute-done.13.sibling
  55.2 0.6 quad_down.1
  55.8 2.0 %collective-permute-start.14 = (bf16[512,256]{1,0:T(8,128)(2,1)S(1)}, bf16[512,256]{1,0:T(8,128)(2,1)S(1)}, u32[]{:S(2)}, u32[]{:S(2)}) collective-permute-start(bf16[512,256]{1,0:T(8,128)(2,1)S(1)} %get-tuple-element.124), channel_id=1, source_target_pairs={{0,1},{1,2},{2,3},{3,0},{4,5},{5,6},{6,7},{7,4},{8,9},{9,10},{10,1... | collective-permute-start | bytes 786440 | tf_op jit(solution)/shard_map/ppermute | solution.py:535
  57.9 1.3 %collective-permute-start.15 = (bf16[512,256]{1,0:T(8,128)(2,1)S(1)}, bf16[512,256]{1,0:T(8,128)(2,1)S(1)}, u32[]{:S(2)}, u32[]{:S(2)}) collective-permute-start(bf16[512,256]{1,0:T(8,128)(2,1)S(1)} %get-tuple-element.125), channel_id=1, source_target_pairs={{0,3},{1,0},{2,1},{3,2},{4,7},{5,4},{6,5},{7,6},{8,11},{9,8},{10,9... | collective-permute-start | bytes 786440 | tf_op jit(solution)/shard_map/ppermute | solution.py:535
  59.1 0.9 %collective-permute-start.16 = (bf16[512,256]{1,0:T(8,128)(2,1)S(1)}, bf16[512,256]{1,0:T(8,128)(2,1)S(1)}, u32[]{:S(2)}, u32[]{:S(2)}) collective-permute-start(bf16[512,256]{1,0:T(8,128)(2,1)S(1)} %get-tuple-element.126), channel_id=1, source_target_pairs={{0,2},{1,3},{2,0},{3,1},{4,6},{5,7},{6,4},{7,5},{8,10},{9,11},{10,... | collective-permute-start | bytes 786440 | tf_op jit(solution)/shard_map/ppermute | solution.py:535
  60.0 8.3 %near_1152.1.near = f32[34816,128]{1,0:T(8,128)S(1)} custom-call(s32[1,2048]{1,0:T(1,128)S(1)} %copy-done.3, bf16[2048,2048]{1,0:T(8,128)(2,1)S(1)} %get-tuple-element.79.d, bf16[2048,2048]{1,0:T(8,128)(2,1)S(1)} %get-tuple-element.80.x, f32[34816,128]{1,0:T(8,128)S(1)} %near_896.1.near_in), custom_call_target="tpu_custom_call", output_to_operand_aliasing={{}: (3, {})} | custom-call | flops 7516192768 | bytes 1048576 | tf_op jit(solution)/shard_map/near_1152/pallas_call | solution.py:64
  68.3 0.0 collective-permute-done.15.refs_2_
  68.4 0.0 collective-permute-done.16.refs_3_
  68.4 4.9 %tail_0132.1 = bf16[2048,2048]{1,0:T(8,128)(2,1)} custom-call(s32[256,256]{1,0:T(8,128)S(1)} %get-tuple-element.72.table, bf16[2048,256]{1,0:T(8,128)(2,1)S(1)} %get-tuple-element.73.basis, bf16[2048,256]{1,0:T(8,128)(2,1)S(1)} %collective-permute-done.13.sibling, bf16[2,256,256]{2,1,0:T(8,128)(2,1)S(1)} %bitcast.11, f32[34816,128]{1,0:T(8,128)S(1)} %near_1152.1.near, ...), custom_call_target="tpu_custom_call" | custom-call | flops 536870912 | bytes 3145728 | tf_op jit(solution)/shard_map/tail_0132/pallas_call | solution.py:517
  (11 shorter events, 0.0 us)
Async XLA Ops:
  0.0 9.1 %copy-start.1 = (bf16[1,2,256,256]{3,2,1,0:T(8,128)(2,1)S(1)}, bf16[1,2,256,256]{3,2,1,0:T(8,128)(2,1)}, u32[]{:S(2)}) copy-start(bf16[1,2,256,256]{3,2,1,0:T(8,128)(2,1)} %param.13) | copy-start | bytes 786436
  0.0 13.9 %copy-start.3 = (s32[1,2048]{1,0:T(1,128)S(1)}, s32[1,2048]{1,0:T(1,128)}, u32[]{:S(2)}) copy-start(s32[1,2048]{1,0:T(1,128)} %order.13) | copy-start | bytes 24580
  5.9 17.4 %collective-permute-start.1 = (bf16[512,256]{1,0:T(8,128)(2,1)S(1)}, bf16[512,256]{1,0:T(8,128)(2,1)S(1)}, u32[]{:S(2)}, u32[]{:S(2)}) collective-permute-start(bf16[512,256]{1,0:T(8,128)(2,1)S(1)} %get-tuple-element.76), channel_id=1, source_target_pairs={{0,2},{1,3},{2,0},{3,1},{4,6},{5,7},{6,4},{7,5},{8,10},{9,11},{10,... | collective-permute-start | bytes 786440 | tf_op jit(solution)/shard_map/ppermute | solution.py:535
  10.6 12.6 %collective-permute-start = (bf16[512,256]{1,0:T(8,128)(2,1)S(1)}, bf16[512,256]{1,0:T(8,128)(2,1)S(1)}, u32[]{:S(2)}, u32[]{:S(2)}) collective-permute-start(bf16[512,256]{1,0:T(8,128)(2,1)S(1)} %get-tuple-element.75), channel_id=1, source_target_pairs={{0,1},{1,2},{2,3},{3,0},{4,5},{5,6},{6,7},{7,4},{8,9},{9,10},{10,1... | collective-permute-start | bytes 786440 | tf_op jit(solution)/shard_map/ppermute | solution.py:535
  11.3 12.0 %collective-permute-start.2 = (bf16[512,256]{1,0:T(8,128)(2,1)S(1)}, bf16[512,256]{1,0:T(8,128)(2,1)S(1)}, u32[]{:S(2)}, u32[]{:S(2)}) collective-permute-start(bf16[512,256]{1,0:T(8,128)(2,1)S(1)} %get-tuple-element.77), channel_id=1, source_target_pairs={{0,3},{1,0},{2,1},{3,2},{4,7},{5,4},{6,5},{7,6},{8,11},{9,8},{10,9... | collective-permute-start | bytes 786440 | tf_op jit(solution)/shard_map/ppermute | solution.py:535
  20.6 2.7 %copy-start = (bf16[1,15,2,256,256]{4,3,2,1,0:T(8,128)(2,1)S(1)}, bf16[1,15,2,256,256]{4,3,2,1,0:T(8,128)(2,1)}, u32[]{:S(2)}) copy-start(bf16[1,15,2,256,256]{4,3,2,1,0:T(8,128)(2,1)} %param.14) | copy-start | bytes 11796484
  23.8 31.4 %collective-permute-start.13 = (bf16[2048,256]{1,0:T(8,128)(2,1)S(1)}, bf16[2048,256]{1,0:T(8,128)(2,1)S(1)}, u32[]{:S(2)}, u32[]{:S(2)}) collective-permute-start(bf16[2048,256]{1,0:T(8,128)(2,1)S(1)} %get-tuple-element.115), channel_id=1, source_target_pairs={{0,1},{1,0},{2,3},{3,2},{4,5},{5,4},{6,7},{7,6},{8,9},{9,8},{10,11... | collective-permute-start | bytes 3145736 | tf_op jit(solution)/shard_map/ppermute | solution.py:544
  23.9 9.2 %collective-permute-start.3 = (bf16[128,256]{1,0:T(8,128)(2,1)S(1)}, bf16[128,256]{1,0:T(8,128)(2,1)S(1)}, u32[]{:S(2)}, u32[]{:S(2)}) collective-permute-start(bf16[128,256]{1,0:T(8,128)(2,1)S(1)} %get-tuple-element.92), channel_id=1, source_target_pairs={{0,4},{1,5},{2,6},{3,7},{4,8},{5,9},{6,10},{7,11},{8,12},{9,13},{1... | collective-permute-start | bytes 196616 | tf_op jit(solution)/shard_map/ppermute | solution.py:540
  25.9 7.2 %collective-permute-start.4 = (bf16[128,256]{1,0:T(8,128)(2,1)S(1)}, bf16[128,256]{1,0:T(8,128)(2,1)S(1)}, u32[]{:S(2)}, u32[]{:S(2)}) collective-permute-start(bf16[128,256]{1,0:T(8,128)(2,1)S(1)} %get-tuple-element.93), channel_id=1, source_target_pairs={{0,8},{1,9},{2,10},{3,11},{4,12},{5,13},{6,14},{7,15},{8,0},{9,1},... | collective-permute-start | bytes 196616 | tf_op jit(solution)/shard_map/ppermute | solution.py:540
  29.5 4.3 %collective-permute-start.5 = (bf16[128,256]{1,0:T(8,128)(2,1)S(1)}, bf16[128,256]{1,0:T(8,128)(2,1)S(1)}, u32[]{:S(2)}, u32[]{:S(2)}) collective-permute-start(bf16[128,256]{1,0:T(8,128)(2,1)S(1)} %get-tuple-element.94), channel_id=1, source_target_pairs={{0,12},{1,13},{2,14},{3,15},{4,0},{5,1},{6,2},{7,3},{8,4},{9,5},{1... | collective-permute-start | bytes 196616 | tf_op jit(solution)/shard_map/ppermute | solution.py:540
  34.3 1.6 %collective-permute-start.6 = (f32[2,128,256]{2,1,0:T(8,128)S(1)}, f32[2,128,256]{2,1,0:T(8,128)S(1)}, u32[]{:S(2)}, u32[]{:S(2)}) collective-permute-start(f32[2,128,256]{2,1,0:T(8,128)S(1)} %get-tuple-element.100.own), channel_id=1, source_target_pairs={{0,16},{16,0},{32,48},{48,32},{64,80},{80,64},{96,112},{112,96},{1... | collective-permute-start | bytes 786440 | tf_op jit(solution)/shard_map/ppermute | solution.py:548
  36.0 9.5 %copy-start.2 = (bf16[6,2,256,256]{3,2,1,0:T(8,128)(2,1)S(1)}, bf16[6,2,256,256]{3,2,1,0:T(8,128)(2,1)}, u32[]{:S(2)}) copy-start(bf16[6,2,256,256]{3,2,1,0:T(8,128)(2,1)} %outer.1) | copy-start | bytes 4718596
  36.0 9.5 %copy-start.4 = (bf16[256,256]{1,0:T(8,128)(2,1)S(1)}, bf16[256,256]{1,0:T(8,128)(2,1)}, u32[]{:S(2)}) copy-start(bf16[256,256]{1,0:T(8,128)(2,1)} %root.1) | copy-start | bytes 393220
  36.0 6.8 %collective-permute-start.9 = (bf16[128,256]{1,0:T(8,128)(2,1)S(1)}, bf16[128,256]{1,0:T(8,128)(2,1)S(1)}, u32[]{:S(2)}, u32[]{:S(2)}) collective-permute-start(bf16[128,256]{1,0:T(8,128)(2,1)S(1)} %five.1.y0), channel_id=1, source_target_pairs={{0,96},{16,112},{32,64},{48,80},{64,32},{80,48},{96,0},{112,16},{1... | collective-permute-start | bytes 196616 | tf_op jit(solution)/shard_map/ppermute | solution.py:548
  39.1 6.4 %collective-permute-start.8 = (bf16[128,256]{1,0:T(8,128)(2,1)S(1)}, bf16[128,256]{1,0:T(8,128)(2,1)S(1)}, u32[]{:S(2)}, u32[]{:S(2)}) collective-permute-start(bf16[128,256]{1,0:T(8,128)(2,1)S(1)} %five.1.y0), channel_id=1, source_target_pairs={{0,64},{16,80},{32,96},{48,112},{64,0},{80,16},{96,32},{112,48},{1... | collective-permute-start | bytes 196616 | tf_op jit(solution)/shard_map/ppermute | solution.py:548
  39.7 5.7 %collective-permute-start.7 = (bf16[128,256]{1,0:T(8,128)(2,1)S(1)}, bf16[128,256]{1,0:T(8,128)(2,1)S(1)}, u32[]{:S(2)}, u32[]{:S(2)}) collective-permute-start(bf16[128,256]{1,0:T(8,128)(2,1)S(1)} %five.1.y0), channel_id=1, source_target_pairs={{0,32},{16,48},{32,0},{48,16},{64,96},{80,112},{96,64},{112,80},{1... | collective-permute-start | bytes 196616 | tf_op jit(solution)/shard_map/ppermute | solution.py:548
  47.2 6.8 %collective-permute-start.10 = (bf16[128,256]{1,0:T(8,128)(2,1)S(1)}, bf16[128,256]{1,0:T(8,128)(2,1)S(1)}, u32[]{:S(2)}, u32[]{:S(2)}) collective-permute-start(bf16[128,256]{1,0:T(8,128)(2,1)S(1)} %get-tuple-element.111), channel_id=1, source_target_pairs={{0,4},{1,5},{2,6},{3,7},{4,8},{5,9},{6,10},{7,11},{8,12},{9,13},{1... | collective-permute-start | bytes 196616 | tf_op jit(solution)/shard_map/ppermute | solution.py:540
  47.7 6.4 %collective-permute-start.11 = (bf16[128,256]{1,0:T(8,128)(2,1)S(1)}, bf16[128,256]{1,0:T(8,128)(2,1)S(1)}, u32[]{:S(2)}, u32[]{:S(2)}) collective-permute-start(bf16[128,256]{1,0:T(8,128)(2,1)S(1)} %get-tuple-element.112), channel_id=1, source_target_pairs={{0,8},{1,9},{2,10},{3,11},{4,12},{5,13},{6,14},{7,15},{8,0},{9,1},... | collective-permute-start | bytes 196616 | tf_op jit(solution)/shard_map/ppermute | solution.py:540
  51.0 4.3 %collective-permute-start.12 = (bf16[128,256]{1,0:T(8,128)(2,1)S(1)}, bf16[128,256]{1,0:T(8,128)(2,1)S(1)}, u32[]{:S(2)}, u32[]{:S(2)}) collective-permute-start(bf16[128,256]{1,0:T(8,128)(2,1)S(1)} %get-tuple-element.113), channel_id=1, source_target_pairs={{0,12},{1,13},{2,14},{3,15},{4,0},{5,1},{6,2},{7,3},{8,4},{9,5},{1... | collective-permute-start | bytes 196616 | tf_op jit(solution)/shard_map/ppermute | solution.py:540
  55.8 12.5 %collective-permute-start.14 = (bf16[512,256]{1,0:T(8,128)(2,1)S(1)}, bf16[512,256]{1,0:T(8,128)(2,1)S(1)}, u32[]{:S(2)}, u32[]{:S(2)}) collective-permute-start(bf16[512,256]{1,0:T(8,128)(2,1)S(1)} %get-tuple-element.124), channel_id=1, source_target_pairs={{0,1},{1,2},{2,3},{3,0},{4,5},{5,6},{6,7},{7,4},{8,9},{9,10},{10,1... | collective-permute-start | bytes 786440 | tf_op jit(solution)/shard_map/ppermute | solution.py:535
  57.9 10.5 %collective-permute-start.15 = (bf16[512,256]{1,0:T(8,128)(2,1)S(1)}, bf16[512,256]{1,0:T(8,128)(2,1)S(1)}, u32[]{:S(2)}, u32[]{:S(2)}) collective-permute-start(bf16[512,256]{1,0:T(8,128)(2,1)S(1)} %get-tuple-element.125), channel_id=1, source_target_pairs={{0,3},{1,0},{2,1},{3,2},{4,7},{5,4},{6,5},{7,6},{8,11},{9,8},{10,9... | collective-permute-start | bytes 786440 | tf_op jit(solution)/shard_map/ppermute | solution.py:535
  59.1 9.2 %collective-permute-start.16 = (bf16[512,256]{1,0:T(8,128)(2,1)S(1)}, bf16[512,256]{1,0:T(8,128)(2,1)S(1)}, u32[]{:S(2)}, u32[]{:S(2)}) collective-permute-start(bf16[512,256]{1,0:T(8,128)(2,1)S(1)} %get-tuple-element.126), channel_id=1, source_target_pairs={{0,2},{1,3},{2,0},{3,1},{4,6},{5,7},{6,4},{7,5},{8,10},{9,11},{10,... | collective-permute-start | bytes 786440 | tf_op jit(solution)/shard_map/ppermute | solution.py:535

commit v5 on v4

--- a/solution.py
+++ b/solution.py
@@ -78,16 +78,6 @@
     rows = basis.shape[0]
 
     @pl.loop(0, rows // 64)
-    def _(b):
-        for r in range(4):
-            for t in range(2):
-                start = pl.multiple_of(b * 64 + r * 16, 16)
-                x = basis[pl.ds(start, 16), t * 128 : (t + 1) * 128].astype(F32)
-                base = (b * 64 + r * 16) * 3 + t
-                src[pl.ds(base, 8, stride=3), :] = x[:8]
-                src[pl.ds(base + 24, 8, stride=3), :] = x[8:]
-
-    @pl.loop(0, rows // 64)
     def _(i):
         for j in range(64):
             to = order[0, i * 64 + j] * 3
@@ -106,6 +96,18 @@
             out_t[t * 128 : (t + 1) * 128, pl.ds(start, 256)] = x.T.astype(BF)
 
 
+def spread_basis(first, rows, basis, src):
+    @pl.loop(first // 64, (first + rows) // 64)
+    def _(b):
+        for r in range(4):
+            for t in range(2):
+                start = pl.multiple_of(b * 64 + r * 16, 16)
+                x = basis[pl.ds(start, 16), t * 128 : (t + 1) * 128].astype(F32)
+                base = (b * 64 + r * 16) * 3 + t
+                src[pl.ds(base, 8, stride=3), :] = x[:8]
+                src[pl.ds(base + 24, 8, stride=3), :] = x[8:]
+
+
 def coef_product(shift, basis_t, x):
     cols = x.shape[1] // RING
     start = pl.multiple_of(((place()[0] + shift) & 3) * cols, cols)
@@ -120,8 +122,8 @@
 
 def front_kernel(
     order_hbm, ranks_hbm, basis_hbm, x_hbm, node_hbm,
-    out, out_t, x, coef, piece, limit,
-    order, ranks, basis, transfer, src, dst, sem,
+    out, out_t, x, coef, piece, limit, transfer,
+    order, ranks, basis, src, dst, sem,
 ):
     cols = piece.shape[0]
     ring, z, outer = place()
@@ -131,18 +133,26 @@
         part = pl.ds(start, cols)
         return pltpu.make_async_copy(x_hbm.at[:, part], x.at[:, part], sem.at[k])
 
+    size = basis.shape[0] // 4
+    parts = []
+    for k in range(4):
+        part = pl.ds(k * size, size)
+        parts.append(pltpu.make_async_copy(basis_hbm.at[part], basis.at[part], sem.at[7 + k]))
+        parts[k].start()
     loads = [
-        pltpu.make_async_copy(basis_hbm, basis, sem.at[4]),
-        pltpu.make_async_copy(order_hbm, order, sem.at[5]),
-        pltpu.make_async_copy(ranks_hbm, ranks, sem.at[6]),
-        pltpu.make_async_copy(node_hbm.at[0], transfer, sem.at[7]),
+        pltpu.make_async_copy(order_hbm, order, sem.at[4]),
+        pltpu.make_async_copy(ranks_hbm, ranks, sem.at[5]),
+        pltpu.make_async_copy(node_hbm.at[0], transfer, sem.at[6]),
     ]
     for load in loads:
         load.start()
+    for k in range(RING):
+        fetch(k).start()
+    for k in range(4):
+        parts[k].wait()
+        spread_basis(k * size, size, basis, src)
     for load in loads:
         load.wait()
-    for k in range(RING):
-        fetch(k).start()
     limit[...] = jnp.full(limit.shape, ranks[127 + outer * 16 + z * RING + ring], jnp.int32)
     shuffle_basis(order, basis, out, out_t, src, dst)
     fetch(0).wait()
@@ -164,6 +174,7 @@
             held(cols // RING, width),
             held(cols // RING, width),
             pltpu.VMEM((8, width), jnp.int32),
+            held(width, width),
         ),
         [pin(a, pltpu.HBM) for a in (order, ranks, basis, points, nodes)],
         flops=2**31,
@@ -172,28 +183,27 @@
             pltpu.SMEM(order.shape, jnp.int32),
             pltpu.SMEM(ranks.shape, jnp.int32),
             pltpu.VMEM((rows, width), BF),
-            pltpu.VMEM((width, width), BF),
             pltpu.VMEM((rows * 3, 128), F32),
             pltpu.VMEM((rows * 3, 128), F32),
-            pltpu.SemaphoreType.DMA((8,)),
+            pltpu.SemaphoreType.DMA((11,)),
         ],
         specs=[HBM] * 5,
     )
 
 
-def coef_kernel(limit, basis_t, x, node, c1, c3, p1, p3):
+def coef_kernel(limit, basis_t, x, transfer, c1, c3, p1, p3):
     product1 = coef_product(1, basis_t, x)
     product3 = coef_product(3, basis_t, x)
-    coef_finish(product1, limit, node.at[0], c1, p1)
-    coef_finish(product3, limit, node.at[0], c3, p3)
-
-
-def coef_rest(limit, basis_t, x, node):
+    coef_finish(product1, limit, transfer, c1, p1)
+    coef_finish(product3, limit, transfer, c3, p3)
+
+
+def coef_rest(limit, basis_t, x, transfer):
     return call(
         coef_kernel,
         "coef",
         (held(x.shape[1] // RING, basis_t.shape[0]),) * 4,
-        tuple(map(pin, (limit, basis_t, x, node))),
+        tuple(map(pin, (limit, basis_t, x, transfer))),
         flops=2**30,
     )
 
@@ -248,9 +258,9 @@
 
 
 def move_kernel(
-    limit, order, basis_t, node, c1, c2, c3, x_in, diag_hbm, ranks_hbm,
-    coef, x, diag, piece, src, table,
-    even, odd, scaled, row_at, ranks, sem,
+    limit, order, basis_t, transfer, c1, c2, c3, x_in, diag_hbm, ranks_hbm,
+    coef, x, diag, piece, src, table, scaled,
+    even, odd, row_at, ranks, sem,
 ):
     size = diag.shape[0] // 4
     loads = []
@@ -269,19 +279,24 @@
     def rows_of(shift):
         return coef.at[pl.ds(pl.multiple_of(((ring + shift) & 3) * cols, cols), cols)]
 
-    coef_finish(coef_product(0, basis_t, x), limit, node.at[0], rows_of(0), piece)
+    coef_finish(coef_product(0, basis_t, x), limit, transfer, rows_of(0), piece)
     for shift, ref in ((1, c1), (2, c2), (3, c3)):
         rows_of(shift)[...] = ref[...]
     load_ranks.wait()
-    for node_id in range(ranks.shape[0]):
-        table[node_id : node_id + 1] = jnp.full((1, table.shape[1]), ranks[node_id], jnp.int32)
+    z, outer = place()[1:]
+    quad = outer * RING + z
+    used = [0, 1, 2, 3 + (outer >> 1), 7 + outer, 15 + 2 * outer, 16 + 2 * outer]
+    used += [31 + RING * outer + k for k in range(RING)]
+    used += [63 + 2 * quad, 64 + 2 * quad, 127 + RING * quad + ring]
+    for node_id in used:
+        table[pl.ds(node_id, 1), :] = jnp.full((1, table.shape[1]), ranks[node_id], jnp.int32)
     load.wait()
     move_rows(row_at, x, src, (even, odd))
     for load in loads:
         load.wait()
 
 
-def move(limit, ranks, order, basis_t, node, coefs, x, diag):
+def move(limit, ranks, order, basis_t, transfer, coefs, x, diag):
     rows, cols = x.shape
     width = basis_t.shape[0]
     return call(
@@ -294,9 +309,10 @@
             held(cols // RING, width),
             pltpu.VMEM((rows * PITCH, 128), F32),
             pltpu.VMEM((ranks.shape[0] + 1, width), jnp.int32),
+            pltpu.VMEM(order.shape, jnp.int32),
         ),
         (
-            *map(pin, (limit, order, basis_t, node, *coefs, x)),
+            *map(pin, (limit, order, basis_t, transfer, *coefs, x)),
             pin(diag, pltpu.HBM),
             pin(ranks, pltpu.HBM),
         ),
@@ -305,7 +321,6 @@
         scratch=[
             pltpu.VMEM((GROUP * PITCH, 128), F32),
             pltpu.VMEM((GROUP * PITCH, 128), F32),
-            pltpu.VMEM(order.shape, jnp.int32),
             pltpu.SMEM(order.shape, jnp.int32),
             pltpu.SMEM(ranks.shape, jnp.int32),
             pltpu.SemaphoreType.DMA((6,)),
@@ -326,7 +341,7 @@
         if k == 0:
             load.wait()
         for i in range(block):
-            to = row_at[0, row + i] * PITCH
+            to = row_at[0, row + i]
             for h in (0, 8):
                 out[pl.ds(to + h, 8), :] = src[pl.ds(i * PITCH + h, 8), :]
 
@@ -475,7 +490,7 @@
     )
 
 
-TAIL = 512
+TAIL = 256
 
 
 def tail_kernel(shifts, table, basis, sibling, node, near, *refs):
@@ -569,14 +584,16 @@
     inner = inner_nodes[0]
     node = leaf_nodes[0]
 
-    basis, basis_t, x, c2, piece, limit = front(leaf_order, node_ranks, leaf_basis[0], points, node)
-    c1, c3, *others = coef_rest(limit, basis_t, x, node)
+    basis, basis_t, x, c2, piece, limit, transfer = front(
+        leaf_order, node_ranks, leaf_basis[0], points, node
+    )
+    c1, c3, *others = coef_rest(limit, basis_t, x, transfer)
     sent = {2: ring_x(piece, 2), 1: ring_x(others[0], 1), 3: ring_x(others[1], 3)}
     coefs = (c1, c2, c3)
-    coef, ordered, diag, own, near, table = move(
-        limit, node_ranks, leaf_order, basis_t, node, coefs, x, diag_blocks[0]
-    )
-    near = near_rows(0, 256, leaf_order, diag, ordered, near)
+    coef, ordered, diag, own, near, table, row_at = move(
+        limit, node_ranks, leaf_order, basis_t, transfer, coefs, x, diag_blocks[0]
+    )
+    near = near_rows(0, 256, row_at, diag, ordered, near)
     pieces = [own, sent[1], sent[2], sent[3]]
     *pieces, coef, near = lax.optimization_barrier((*pieces, coef, near))
 
@@ -584,23 +601,23 @@
     coef, *parts = lax.optimization_barrier((coef, *parts))
     parts = exchange(ring_z, parts)
     sibling = swap_inner(coef, 1)
-    near = near_rows(256, 256, leaf_order, diag, ordered, near)
+    near = near_rows(256, 256, row_at, diag, ordered, near)
     *parts, near = lax.optimization_barrier((*parts, near))
     c2, c3, lift = group_up(table, parts, inner)
     peer = swap_outer(lift, 1)
-    near = near_rows(512, 128, leaf_order, diag, ordered, near)
+    near = near_rows(512, 128, row_at, diag, ordered, near)
     peer, near = lax.optimization_barrier((peer, near))
     five = five_up(table, lift, peer)
     fives = [five] + [swap_outer(five, 2 * s) for s in (1, 2, 3)]
-    near = near_rows(640, 256, leaf_order, diag, ordered, near)
+    near = near_rows(640, 256, row_at, diag, ordered, near)
     *fives, near = lax.optimization_barrier((*fives, near))
     parts = top_sweep(table, fives, peer, c2, c3, inner, outer_nodes, root_coupling)
     parts = exchange(ring_z, parts)
-    near = near_rows(896, 256, leaf_order, diag, ordered, near)
+    near = near_rows(896, 256, row_at, diag, ordered, near)
     *parts, near, sibling = lax.optimization_barrier((*parts, near, sibling))
     fars = quad_down(table, parts, mid, inner)
     fars = exchange(ring_x, fars)
-    near = near_rows(1152, 896, leaf_order, diag, ordered, near)
+    near = near_rows(1152, 896, row_at, diag, ordered, near)
     add = functools.partial(add_far, table=table, basis=basis, sibling=sibling, node=node, near=near)
     return add((0, 1, 3, 2), fars=[fars[s] for s in (0, 1, 3, 2)], sofar=None)
 

time: 73.6 us -> 73.1 us (level)
  Pallas kernels: 42.6 us -> 41.8 us
    pallas_call x14, Pallas kernels: 37.7 us -> 36.8 us  [call(): pl.pallas_call(kernel, out_shape=out_shapes, in_specs=specs or [VMEM] * l...]
  transfers between devices with their start and end apart: 17 -> 17, of which waited for: 4 -> 5; matrix products, arithmetic and copies ran while one was open for 0% -> 0% of each run, Pallas kernels for 42% -> 41%
where the time goes in v5:
time: 73.1 us; the launch traced here: 73 us
  Pallas kernels  41.8 us (57%)
  starting transfers between devices  25.8 us (35%)
  waiting for transfers between devices  4.97 us (7%)
    pallas_call x14, Pallas kernels, call(): pl.pallas_call(kernel, out_shape=out_shapes, in_specs=specs or [VMEM] * l...  36.8 us
    ppermute x6, starting transfers between devices, ring_z(): return lax.ppermute(block, 'inner', route)  10.8 us
    ppermute x6, starting transfers between devices, ring_x(): return lax.ppermute(block, 'inner', route)  10.7 us
    pallas_call x1, Pallas kernels, add_far(): pl.pallas_call(functools.partial(tail_kernel, shifts), out_shape=sds(rows...  4.95 us
    ppermute x4, starting transfers between devices, swap_outer(): lax.ppermute(block, 'outer', [(o, o ^ bits) for o in range(2 * RING)])  4.26 us
    ppermute x4, waiting for transfers between devices, swap_outer(): lax.ppermute(block, 'outer', [(o, o ^ bits) for o in range(2 * RING)])  2.85 us
    ppermute x6, waiting for transfers between devices, ring_z(): return lax.ppermute(block, 'inner', route)  2.03 us
  transfers between devices with their start and end apart: 17, of which 5 were waited for; matrix products, arithmetic and copies ran while one was open for 0% of the time, Pallas kernels for 41%

profile of v5, /device:TPU:0, one launch (start us, length us, event | category | flops | bytes accessed | tf_op | source)
XLA Modules:
  0.0 73.0 jit_solution(14867459166439323408)
XLA Ops:
  0.0 5.6 %front.1 = (bf16[2048,256]{1,0:T(8,128)(2,1)S(1)}, bf16[256,2048]{1,0:T(8,128)(2,1)S(1)}, bf16[2048,2048]{1,0:T(8,128)(2,1)S(1)}, bf16[512,256]{1,0:T(8,128)(2,1...) custom-call(s32[1,2048]{1,0:T(1,128)} %order.1, s32[255]{0:T(256)} %ranks_hbm.3, ...), custom_call_target="tpu_custom_call" | custom-call | flops 2147483648 | bytes 1048576 | tf_op jit(solution)/shard_map/front/pallas_call | solution.py:64
  5.6 3.2 %collective-permute-start.1 = (bf16[512,256]{1,0:T(8,128)(2,1)S(1)}, bf16[512,256]{1,0:T(8,128)(2,1)S(1)}, u32[]{:S(2)}, u32[]{:S(2)}) collective-permute-start(bf16[512,256]{1,0:T(8,128)(2,1)S(1)} %get-tuple-element.79), channel_id=1, source_target_pairs={{0,2},{1,3},{2,0},{3,1},{4,6},{5,7},{6,4},{7,5},{8,10},{9,11},{10,... | collective-permute-start | bytes 786440 | tf_op jit(solution)/shard_map/ppermute | solution.py:550
  8.8 1.6 %coef.1 = (bf16[512,256]{1,0:T(8,128)(2,1)S(1)}, bf16[512,256]{1,0:T(8,128)(2,1)S(1)}, bf16[512,256]{1,0:T(8,128)(2,1)S(1)}, bf16[512,256]{1,0:T(8,128)(2,1)S(1)}) custom-call(s32[8,256]{1,0:T(8,128)S(1)} %get-tuple-element.68.limit, bf16[256,2048]{1,0:T(8,128)(2,1)S(1)} %get-tuple-element.69.basis_t, bf16[2048,2048]{1,0:T(8,128)(2,1)S(1)} %get-tuple-element.71.x.x_in, ...), custom_call_target="tpu_custom_call" | custom-call | flops 1073741824 | bytes 1048576 | tf_op jit(solution)/shard_map/coef/pallas_call | solution.py:64
  10.4 0.6 collective-permute-start
  11.0 2.7 %collective-permute-start.2 = (bf16[512,256]{1,0:T(8,128)(2,1)S(1)}, bf16[512,256]{1,0:T(8,128)(2,1)S(1)}, u32[]{:S(2)}, u32[]{:S(2)}) collective-permute-start(bf16[512,256]{1,0:T(8,128)(2,1)S(1)} %get-tuple-element.80), channel_id=1, source_target_pairs={{0,3},{1,0},{2,1},{3,2},{4,7},{5,4},{6,5},{7,6},{8,11},{9,8},{10,9... | collective-permute-start | bytes 786440 | tf_op jit(solution)/shard_map/ppermute | solution.py:550
  13.7 6.7 %move.1 = (bf16[2048,256]{1,0:T(8,128)(2,1)S(1)}, bf16[2048,2048]{1,0:T(8,128)(2,1)S(1)}, bf16[2048,2048]{1,0:T(8,128)(2,1)S(1)}, bf16[512,256]{1,0:T(8,128)(2,1...) custom-call(s32[8,256]{1,0:T(8,128)S(1)} %get-tuple-element.68.limit, ...), custom_call_target="tpu_custom_call", output_to_operand_aliasing={{1}: (7, {})} | custom-call | flops 8589934592 | bytes 1048576 | tf_op jit(solution)/shard_map/move/pallas_call | solution.py:64
  20.4 0.0 copy-start
  20.4 2.5 %near_0.1.near_in = f32[34816,128]{1,0:T(8,128)S(1)} custom-call(s32[1,2048]{1,0:T(1,128)S(1)} %get-tuple-element.82.order, bf16[2048,2048]{1,0:T(8,128)(2,1)S(1)} %get-tuple-element.83.d, bf16[2048,2048]{1,0:T(8,128)(2,1)S(1)} %get-tuple-element.84.x, f32[34816,128]{1,0:T(8,128)S(1)} %get-tuple-element.85.near_in), custom_call_target="tpu_custom_call", output_to_operand_aliasing={{}: (3, {})} | custom-call | flops 2147483648 | bytes 1048576 | tf_op jit(solution)/shard_map/near_0/pallas_call | solution.py:64
  22.9 0.0 collective-permute-done.1.u2
  22.9 0.0 collective-permute-done.u1
  22.9 0.0 collective-permute-done.2.u3
  23.0 0.5 quad_up.1
  23.5 0.1 collective-permute-start.13
  23.6 2.0 %collective-permute-start.3 = (bf16[128,256]{1,0:T(8,128)(2,1)S(1)}, bf16[128,256]{1,0:T(8,128)(2,1)S(1)}, u32[]{:S(2)}, u32[]{:S(2)}) collective-permute-start(bf16[128,256]{1,0:T(8,128)(2,1)S(1)} %get-tuple-element.96), channel_id=1, source_target_pairs={{0,4},{1,5},{2,6},{3,7},{4,8},{5,9},{6,10},{7,11},{8,12},{9,13},{1... | collective-permute-start | bytes 196616 | tf_op jit(solution)/shard_map/ppermute | solution.py:555
  25.6 3.6 %collective-permute-start.4 = (bf16[128,256]{1,0:T(8,128)(2,1)S(1)}, bf16[128,256]{1,0:T(8,128)(2,1)S(1)}, u32[]{:S(2)}, u32[]{:S(2)}) collective-permute-start(bf16[128,256]{1,0:T(8,128)(2,1)S(1)} %get-tuple-element.97), channel_id=1, source_target_pairs={{0,8},{1,9},{2,10},{3,11},{4,12},{5,13},{6,14},{7,15},{8,0},{9,1},... | collective-permute-start | bytes 196616 | tf_op jit(solution)/shard_map/ppermute | solution.py:555
  29.2 1.0 %collective-permute-start.5 = (bf16[128,256]{1,0:T(8,128)(2,1)S(1)}, bf16[128,256]{1,0:T(8,128)(2,1)S(1)}, u32[]{:S(2)}, u32[]{:S(2)}) collective-permute-start(bf16[128,256]{1,0:T(8,128)(2,1)S(1)} %get-tuple-element.98), channel_id=1, source_target_pairs={{0,12},{1,13},{2,14},{3,15},{4,0},{5,1},{6,2},{7,3},{8,4},{9,5},{1... | collective-permute-start | bytes 196616 | tf_op jit(solution)/shard_map/ppermute | solution.py:555
  30.2 2.5 %near_256.1.near_in = f32[34816,128]{1,0:T(8,128)S(1)} custom-call(s32[1,2048]{1,0:T(1,128)S(1)} %get-tuple-element.82.order, bf16[2048,2048]{1,0:T(8,128)(2,1)S(1)} %get-tuple-element.83.d, bf16[2048,2048]{1,0:T(8,128)(2,1)S(1)} %get-tuple-element.84.x, f32[34816,128]{1,0:T(8,128)S(1)} %near_0.1.near_in), custom_call_target="tpu_custom_call", output_to_operand_aliasing={{}: (3, {})} | custom-call | flops 2147483648 | bytes 1048576 | tf_op jit(solution)/shard_map/near_256/pallas_call | solution.py:64
  32.7 0.0 collective-permute-done.3.q1
  32.7 0.0 collective-permute-done.4.q2
  32.7 0.7 %collective-permute-done.5.q3 = bf16[128,256]{1,0:T(8,128)(2,1)S(1)} collective-permute-done((bf16[128,256]{1,0:T(8,128)(2,1)S(1)}, bf16[128,256]{1,0:T(8,128)(2,1)S(1)}, u32[]{:S(2)}, u32[]{:S(2)}) %collective-permute-start.5) | collective-permute-done | bytes 65568 | tf_op jit(solution)/shard_map/ppermute | solution.py:555
  33.4 0.5 group_up.1
  34.0 0.1 collective-permute-start.6
  34.1 1.4 %near_512.1.near_in = f32[34816,128]{1,0:T(8,128)S(1)} custom-call(s32[1,2048]{1,0:T(1,128)S(1)} %get-tuple-element.82.order, bf16[2048,2048]{1,0:T(8,128)(2,1)S(1)} %get-tuple-element.83.d, bf16[2048,2048]{1,0:T(8,128)(2,1)S(1)} %get-tuple-element.84.x, f32[34816,128]{1,0:T(8,128)S(1)} %near_256.1.near_in), custom_call_target="tpu_custom_call", output_to_operand_aliasing={{}: (3, {})} | custom-call | flops 1073741824 | bytes 1048576 | tf_op jit(solution)/shard_map/near_512/pallas_call | solution.py:64
  35.4 0.2 collective-permute-done.6.peer.peer4
  35.6 0.0 copy-start.1
  35.7 0.0 copy-start.3
  35.7 3.1 %collective-permute-start.9 = (bf16[128,256]{1,0:T(8,128)(2,1)S(1)}, bf16[128,256]{1,0:T(8,128)(2,1)S(1)}, u32[]{:S(2)}, u32[]{:S(2)}) collective-permute-start(bf16[128,256]{1,0:T(8,128)(2,1)S(1)} %five.1.y0), channel_id=1, source_target_pairs={{0,96},{16,112},{32,64},{48,80},{64,32},{80,48},{96,0},{112,16},{1... | collective-permute-start | bytes 196616 | tf_op jit(solution)/shard_map/ppermute | solution.py:563
  38.8 0.6 collective-permute-start.8
  39.4 0.4 collective-permute-start.7
  39.8 2.5 %near_640.1.near_in = f32[34816,128]{1,0:T(8,128)S(1)} custom-call(s32[1,2048]{1,0:T(1,128)S(1)} %get-tuple-element.82.order, bf16[2048,2048]{1,0:T(8,128)(2,1)S(1)} %get-tuple-element.83.d, bf16[2048,2048]{1,0:T(8,128)(2,1)S(1)} %get-tuple-element.84.x, f32[34816,128]{1,0:T(8,128)S(1)} %near_512.1.near_in), custom_call_target="tpu_custom_call", output_to_operand_aliasing={{}: (3, {})} | custom-call | flops 2147483648 | bytes 1048576 | tf_op jit(solution)/shard_map/near_640/pallas_call | solution.py:64
  42.3 0.0 collective-permute-done.9.y3
  42.3 2.7 %collective-permute-done.8.y2 = bf16[128,256]{1,0:T(8,128)(2,1)S(1)} collective-permute-done((bf16[128,256]{1,0:T(8,128)(2,1)S(1)}, bf16[128,256]{1,0:T(8,128)(2,1)S(1)}, u32[]{:S(2)}, u32[]{:S(2)}) %collective-permute-start.8) | collective-permute-done | bytes 65568 | tf_op jit(solution)/shard_map/ppermute | solution.py:563
  45.0 0.0 collective-permute-done.7.y1
  45.0 1.8 %top.1 = (bf16[128,256]{1,0:T(8,128)(2,1)S(1)}, bf16[128,256]{1,0:T(8,128)(2,1)S(1)}, bf16[128,256]{1,0:T(8,128)(2,1)S(1)}, bf16[128,256]{1,0:T(8,128)(2,1)S(1)}) custom-call(s32[256,256]{1,0:T(8,128)S(1)} %get-tuple-element.75.table, bf16[128,256]{1,0:T(8,128)(2,1)S(1)} %five.1.y0, bf16[128,256]{1,0:T(8,128)(2,1)S(1)} %collective-permute-done.7.y1, ...), custom_call_target="tpu_custom_call" | custom-call | flops 268435456 | bytes 1048576 | tf_op jit(solution)/shard_map/top/pallas_call | solution.py:64
  46.8 0.3 collective-permute-start.10
  47.2 3.4 %collective-permute-start.11 = (bf16[128,256]{1,0:T(8,128)(2,1)S(1)}, bf16[128,256]{1,0:T(8,128)(2,1)S(1)}, u32[]{:S(2)}, u32[]{:S(2)}) collective-permute-start(bf16[128,256]{1,0:T(8,128)(2,1)S(1)} %get-tuple-element.116), channel_id=1, source_target_pairs={{0,8},{1,9},{2,10},{3,11},{4,12},{5,13},{6,14},{7,15},{8,0},{9,1},... | collective-permute-start | bytes 196616 | tf_op jit(solution)/shard_map/ppermute | solution.py:555
  50.6 0.5 collective-permute-start.12
  51.1 2.5 %near_896.1.near_in = f32[34816,128]{1,0:T(8,128)S(1)} custom-call(s32[1,2048]{1,0:T(1,128)S(1)} %get-tuple-element.82.order, bf16[2048,2048]{1,0:T(8,128)(2,1)S(1)} %get-tuple-element.83.d, bf16[2048,2048]{1,0:T(8,128)(2,1)S(1)} %get-tuple-element.84.x, f32[34816,128]{1,0:T(8,128)S(1)} %near_640.1.near_in), custom_call_target="tpu_custom_call", output_to_operand_aliasing={{}: (3, {})} | custom-call | flops 2147483648 | bytes 1048576 | tf_op jit(solution)/shard_map/near_896/pallas_call | solution.py:64
  53.6 0.0 collective-permute-done.11.f2
  53.6 1.3 %collective-permute-done.12.f3 = bf16[128,256]{1,0:T(8,128)(2,1)S(1)} collective-permute-done((bf16[128,256]{1,0:T(8,128)(2,1)S(1)}, bf16[128,256]{1,0:T(8,128)(2,1)S(1)}, u32[]{:S(2)}, u32[]{:S(2)}) %collective-permute-start.12) | collective-permute-done | bytes 65568 | tf_op jit(solution)/shard_map/ppermute | solution.py:555
  54.9 0.6 quad_down.1
  55.4 2.0 %collective-permute-start.14 = (bf16[512,256]{1,0:T(8,128)(2,1)S(1)}, bf16[512,256]{1,0:T(8,128)(2,1)S(1)}, u32[]{:S(2)}, u32[]{:S(2)}) collective-permute-start(bf16[512,256]{1,0:T(8,128)(2,1)S(1)} %get-tuple-element.128), channel_id=1, source_target_pairs={{0,1},{1,2},{2,3},{3,0},{4,5},{5,6},{6,7},{7,4},{8,9},{9,10},{10,1... | collective-permute-start | bytes 786440 | tf_op jit(solution)/shard_map/ppermute | solution.py:550
  57.5 1.3 %collective-permute-start.15 = (bf16[512,256]{1,0:T(8,128)(2,1)S(1)}, bf16[512,256]{1,0:T(8,128)(2,1)S(1)}, u32[]{:S(2)}, u32[]{:S(2)}) collective-permute-start(bf16[512,256]{1,0:T(8,128)(2,1)S(1)} %get-tuple-element.129), channel_id=1, source_target_pairs={{0,3},{1,0},{2,1},{3,2},{4,7},{5,4},{6,5},{7,6},{8,11},{9,8},{10,9... | collective-permute-start | bytes 786440 | tf_op jit(solution)/shard_map/ppermute | solution.py:550
  58.8 0.9 %collective-permute-start.16 = (bf16[512,256]{1,0:T(8,128)(2,1)S(1)}, bf16[512,256]{1,0:T(8,128)(2,1)S(1)}, u32[]{:S(2)}, u32[]{:S(2)}) collective-permute-start(bf16[512,256]{1,0:T(8,128)(2,1)S(1)} %get-tuple-element.130), channel_id=1, source_target_pairs={{0,2},{1,3},{2,0},{3,1},{4,6},{5,7},{6,4},{7,5},{8,10},{9,11},{10,... | collective-permute-start | bytes 786440 | tf_op jit(solution)/shard_map/ppermute | solution.py:550
  59.7 8.1 %near_1152.1.near = f32[34816,128]{1,0:T(8,128)S(1)} custom-call(s32[1,2048]{1,0:T(1,128)S(1)} %get-tuple-element.82.order, bf16[2048,2048]{1,0:T(8,128)(2,1)S(1)} %get-tuple-element.83.d, bf16[2048,2048]{1,0:T(8,128)(2,1)S(1)} %get-tuple-element.84.x, f32[34816,128]{1,0:T(8,128)S(1)} %near_896.1.near_in), custom_call_target="tpu_custom_call", output_to_operand_aliasing={{}: (3, {})} | custom-call | flops 7516192768 | bytes 1048576 | tf_op jit(solution)/shard_map/near_1152/pallas_call | solution.py:64
  67.8 0.1 collective-permute-done.14.refs_1_
  67.9 0.0 collective-permute-done.15.refs_2_
  67.9 4.9 %tail_0132.1 = bf16[2048,2048]{1,0:T(8,128)(2,1)} custom-call(s32[256,256]{1,0:T(8,128)S(1)} %get-tuple-element.75.table, bf16[2048,256]{1,0:T(8,128)(2,1)S(1)} %get-tuple-element.76.basis, bf16[2048,256]{1,0:T(8,128)(2,1)S(1)} %collective-permute-done.13.sibling, bf16[2,256,256]{2,1,0:T(8,128)(2,1)S(1)} %bitcast.9, f32[34816,128]{1,0:T(8,128)S(1)} %near_1152.1.near, ...), custom_call_target="tpu_custom_call" | custom-call | flops 536870912 | bytes 3145728 | tf_op jit(solution)/shard_map/tail_0132/pallas_call | solution.py:532
  (11 shorter events, 0.1 us)
Async XLA Ops:
  0.0 13.7 %copy-start.4 = (s32[1,2048]{1,0:T(1,128)S(1)}, s32[1,2048]{1,0:T(1,128)}, u32[]{:S(2)}) copy-start(s32[1,2048]{1,0:T(1,128)} %order.1) | copy-start | bytes 24580
  5.6 17.3 %collective-permute-start.1 = (bf16[512,256]{1,0:T(8,128)(2,1)S(1)}, bf16[512,256]{1,0:T(8,128)(2,1)S(1)}, u32[]{:S(2)}, u32[]{:S(2)}) collective-permute-start(bf16[512,256]{1,0:T(8,128)(2,1)S(1)} %get-tuple-element.79), channel_id=1, source_target_pairs={{0,2},{1,3},{2,0},{3,1},{4,6},{5,7},{6,4},{7,5},{8,10},{9,11},{10,... | collective-permute-start | bytes 786440 | tf_op jit(solution)/shard_map/ppermute | solution.py:550
  10.4 12.6 %collective-permute-start = (bf16[512,256]{1,0:T(8,128)(2,1)S(1)}, bf16[512,256]{1,0:T(8,128)(2,1)S(1)}, u32[]{:S(2)}, u32[]{:S(2)}) collective-permute-start(bf16[512,256]{1,0:T(8,128)(2,1)S(1)} %get-tuple-element.78), channel_id=1, source_target_pairs={{0,1},{1,2},{2,3},{3,0},{4,5},{5,6},{6,7},{7,4},{8,9},{9,10},{10,1... | collective-permute-start | bytes 786440 | tf_op jit(solution)/shard_map/ppermute | solution.py:550
  11.0 11.9 %collective-permute-start.2 = (bf16[512,256]{1,0:T(8,128)(2,1)S(1)}, bf16[512,256]{1,0:T(8,128)(2,1)S(1)}, u32[]{:S(2)}, u32[]{:S(2)}) collective-permute-start(bf16[512,256]{1,0:T(8,128)(2,1)S(1)} %get-tuple-element.80), channel_id=1, source_target_pairs={{0,3},{1,0},{2,1},{3,2},{4,7},{5,4},{6,5},{7,6},{8,11},{9,8},{10,9... | collective-permute-start | bytes 786440 | tf_op jit(solution)/shard_map/ppermute | solution.py:550
  20.4 2.5 %copy-start = (bf16[1,15,2,256,256]{4,3,2,1,0:T(8,128)(2,1)S(1)}, bf16[1,15,2,256,256]{4,3,2,1,0:T(8,128)(2,1)}, u32[]{:S(2)}) copy-start(bf16[1,15,2,256,256]{4,3,2,1,0:T(8,128)(2,1)} %param.14) | copy-start | bytes 11796484
  23.5 31.3 %collective-permute-start.13 = (bf16[2048,256]{1,0:T(8,128)(2,1)S(1)}, bf16[2048,256]{1,0:T(8,128)(2,1)S(1)}, u32[]{:S(2)}, u32[]{:S(2)}) collective-permute-start(bf16[2048,256]{1,0:T(8,128)(2,1)S(1)} %get-tuple-element.119), channel_id=1, source_target_pairs={{0,1},{1,0},{2,3},{3,2},{4,5},{5,4},{6,7},{7,6},{8,9},{9,8},{10,11... | collective-permute-start | bytes 3145736 | tf_op jit(solution)/shard_map/ppermute | solution.py:559
  23.6 9.1 %collective-permute-start.3 = (bf16[128,256]{1,0:T(8,128)(2,1)S(1)}, bf16[128,256]{1,0:T(8,128)(2,1)S(1)}, u32[]{:S(2)}, u32[]{:S(2)}) collective-permute-start(bf16[128,256]{1,0:T(8,128)(2,1)S(1)} %get-tuple-element.96), channel_id=1, source_target_pairs={{0,4},{1,5},{2,6},{3,7},{4,8},{5,9},{6,10},{7,11},{8,12},{9,13},{1... | collective-permute-start | bytes 196616 | tf_op jit(solution)/shard_map/ppermute | solution.py:555
  25.6 7.1 %collective-permute-start.4 = (bf16[128,256]{1,0:T(8,128)(2,1)S(1)}, bf16[128,256]{1,0:T(8,128)(2,1)S(1)}, u32[]{:S(2)}, u32[]{:S(2)}) collective-permute-start(bf16[128,256]{1,0:T(8,128)(2,1)S(1)} %get-tuple-element.97), channel_id=1, source_target_pairs={{0,8},{1,9},{2,10},{3,11},{4,12},{5,13},{6,14},{7,15},{8,0},{9,1},... | collective-permute-start | bytes 196616 | tf_op jit(solution)/shard_map/ppermute | solution.py:555
  29.2 4.3 %collective-permute-start.5 = (bf16[128,256]{1,0:T(8,128)(2,1)S(1)}, bf16[128,256]{1,0:T(8,128)(2,1)S(1)}, u32[]{:S(2)}, u32[]{:S(2)}) collective-permute-start(bf16[128,256]{1,0:T(8,128)(2,1)S(1)} %get-tuple-element.98), channel_id=1, source_target_pairs={{0,12},{1,13},{2,14},{3,15},{4,0},{5,1},{6,2},{7,3},{8,4},{9,5},{1... | collective-permute-start | bytes 196616 | tf_op jit(solution)/shard_map/ppermute | solution.py:555
  34.0 1.6 %collective-permute-start.6 = (f32[2,128,256]{2,1,0:T(8,128)S(1)}, f32[2,128,256]{2,1,0:T(8,128)S(1)}, u32[]{:S(2)}, u32[]{:S(2)}) collective-permute-start(f32[2,128,256]{2,1,0:T(8,128)S(1)} %get-tuple-element.104.own), channel_id=1, source_target_pairs={{0,16},{16,0},{32,48},{48,32},{64,80},{80,64},{96,112},{112,96},{1... | collective-permute-start | bytes 786440 | tf_op jit(solution)/shard_map/ppermute | solution.py:563
  35.6 9.4 %copy-start.1 = (bf16[6,2,256,256]{3,2,1,0:T(8,128)(2,1)S(1)}, bf16[6,2,256,256]{3,2,1,0:T(8,128)(2,1)}, u32[]{:S(2)}) copy-start(bf16[6,2,256,256]{3,2,1,0:T(8,128)(2,1)} %outer.1) | copy-start | bytes 4718596
  35.7 9.4 %copy-start.3 = (bf16[256,256]{1,0:T(8,128)(2,1)S(1)}, bf16[256,256]{1,0:T(8,128)(2,1)}, u32[]{:S(2)}) copy-start(bf16[256,256]{1,0:T(8,128)(2,1)} %root.1) | copy-start | bytes 393220
  35.7 6.7 %collective-permute-start.9 = (bf16[128,256]{1,0:T(8,128)(2,1)S(1)}, bf16[128,256]{1,0:T(8,128)(2,1)S(1)}, u32[]{:S(2)}, u32[]{:S(2)}) collective-permute-start(bf16[128,256]{1,0:T(8,128)(2,1)S(1)} %five.1.y0), channel_id=1, source_target_pairs={{0,96},{16,112},{32,64},{48,80},{64,32},{80,48},{96,0},{112,16},{1... | collective-permute-start | bytes 196616 | tf_op jit(solution)/shard_map/ppermute | solution.py:563
  38.8 6.3 %collective-permute-start.8 = (bf16[128,256]{1,0:T(8,128)(2,1)S(1)}, bf16[128,256]{1,0:T(8,128)(2,1)S(1)}, u32[]{:S(2)}, u32[]{:S(2)}) collective-permute-start(bf16[128,256]{1,0:T(8,128)(2,1)S(1)} %five.1.y0), channel_id=1, source_target_pairs={{0,64},{16,80},{32,96},{48,112},{64,0},{80,16},{96,32},{112,48},{1... | collective-permute-start | bytes 196616 | tf_op jit(solution)/shard_map/ppermute | solution.py:563
  39.4 5.6 %collective-permute-start.7 = (bf16[128,256]{1,0:T(8,128)(2,1)S(1)}, bf16[128,256]{1,0:T(8,128)(2,1)S(1)}, u32[]{:S(2)}, u32[]{:S(2)}) collective-permute-start(bf16[128,256]{1,0:T(8,128)(2,1)S(1)} %five.1.y0), channel_id=1, source_target_pairs={{0,32},{16,48},{32,0},{48,16},{64,96},{80,112},{96,64},{112,80},{1... | collective-permute-start | bytes 196616 | tf_op jit(solution)/shard_map/ppermute | solution.py:563
  46.8 6.7 %collective-permute-start.10 = (bf16[128,256]{1,0:T(8,128)(2,1)S(1)}, bf16[128,256]{1,0:T(8,128)(2,1)S(1)}, u32[]{:S(2)}, u32[]{:S(2)}) collective-permute-start(bf16[128,256]{1,0:T(8,128)(2,1)S(1)} %get-tuple-element.115), channel_id=1, source_target_pairs={{0,4},{1,5},{2,6},{3,7},{4,8},{5,9},{6,10},{7,11},{8,12},{9,13},{1... | collective-permute-start | bytes 196616 | tf_op jit(solution)/shard_map/ppermute | solution.py:555
  47.2 6.4 %collective-permute-start.11 = (bf16[128,256]{1,0:T(8,128)(2,1)S(1)}, bf16[128,256]{1,0:T(8,128)(2,1)S(1)}, u32[]{:S(2)}, u32[]{:S(2)}) collective-permute-start(bf16[128,256]{1,0:T(8,128)(2,1)S(1)} %get-tuple-element.116), channel_id=1, source_target_pairs={{0,8},{1,9},{2,10},{3,11},{4,12},{5,13},{6,14},{7,15},{8,0},{9,1},... | collective-permute-start | bytes 196616 | tf_op jit(solution)/shard_map/ppermute | solution.py:555
  50.6 4.3 %collective-permute-start.12 = (bf16[128,256]{1,0:T(8,128)(2,1)S(1)}, bf16[128,256]{1,0:T(8,128)(2,1)S(1)}, u32[]{:S(2)}, u32[]{:S(2)}) collective-permute-start(bf16[128,256]{1,0:T(8,128)(2,1)S(1)} %get-tuple-element.117), channel_id=1, source_target_pairs={{0,12},{1,13},{2,14},{3,15},{4,0},{5,1},{6,2},{7,3},{8,4},{9,5},{1... | collective-permute-start | bytes 196616 | tf_op jit(solution)/shard_map/ppermute | solution.py:555
  55.4 12.4 %collective-permute-start.14 = (bf16[512,256]{1,0:T(8,128)(2,1)S(1)}, bf16[512,256]{1,0:T(8,128)(2,1)S(1)}, u32[]{:S(2)}, u32[]{:S(2)}) collective-permute-start(bf16[512,256]{1,0:T(8,128)(2,1)S(1)} %get-tuple-element.128), channel_id=1, source_target_pairs={{0,1},{1,2},{2,3},{3,0},{4,5},{5,6},{6,7},{7,4},{8,9},{9,10},{10,1... | collective-permute-start | bytes 786440 | tf_op jit(solution)/shard_map/ppermute | solution.py:550
  57.5 10.4 %collective-permute-start.15 = (bf16[512,256]{1,0:T(8,128)(2,1)S(1)}, bf16[512,256]{1,0:T(8,128)(2,1)S(1)}, u32[]{:S(2)}, u32[]{:S(2)}) collective-permute-start(bf16[512,256]{1,0:T(8,128)(2,1)S(1)} %get-tuple-element.129), channel_id=1, source_target_pairs={{0,3},{1,0},{2,1},{3,2},{4,7},{5,4},{6,5},{7,6},{8,11},{9,8},{10,9... | collective-permute-start | bytes 786440 | tf_op jit(solution)/shard_map/ppermute | solution.py:550
  58.8 9.1 %copy-start.2 = (bf16[1,2,256,256]{3,2,1,0:T(8,128)(2,1)S(1)}, bf16[1,2,256,256]{3,2,1,0:T(8,128)(2,1)}, u32[]{:S(2)}) copy-start(bf16[1,2,256,256]{3,2,1,0:T(8,128)(2,1)} %param.13) | copy-start | bytes 786436
  58.8 9.1 %collective-permute-start.16 = (bf16[512,256]{1,0:T(8,128)(2,1)S(1)}, bf16[512,256]{1,0:T(8,128)(2,1)S(1)}, u32[]{:S(2)}, u32[]{:S(2)}) collective-permute-start(bf16[512,256]{1,0:T(8,128)(2,1)S(1)} %get-tuple-element.130), channel_id=1, source_target_pairs={{0,2},{1,3},{2,0},{3,1},{4,6},{5,7},{6,4},{7,5},{8,10},{9,11},{10,... | collective-permute-start | bytes 786440 | tf_op jit(solution)/shard_map/ppermute | solution.py:550

commit v6 on v5

--- a/solution.py
+++ b/solution.py
@@ -209,7 +209,7 @@
 
 
 PITCH = 17
-GROUP = 64
+GROUP = 128
 
 
 def spread(value, first_row, first_tile, to):
@@ -234,13 +234,13 @@
     rows = x.shape[0]
     tiles = x.shape[1] // 128
 
-    @pl.loop(0, rows // 32)
+    @pl.loop(0, rows // 64)
     def _(b):
-        for r in range(0, 32, 16):
-            start = pl.multiple_of(b * 32 + r, 16)
+        for r in range(0, 64, 16):
+            start = pl.multiple_of(b * 64 + r, 16)
             for t in range(tiles):
                 v = x[pl.ds(start, 16), t * 128 : (t + 1) * 128].astype(F32)
-                spread(v, b * 32 + r, t, src)
+                spread(v, b * 64 + r, t, src)
 
     @pl.loop(0, rows // (2 * GROUP))
     def _(i):
@@ -490,7 +490,7 @@
     )
 
 
-TAIL = 256
+TAIL = 512
 
 
 def tail_kernel(shifts, table, basis, sibling, node, near, *refs):

time: 73.1 us -> 73 us (level)
  transfers between devices with their start and end apart: 17 -> 17, of which waited for: 5 -> 4; matrix products, arithmetic and copies ran while one was open for 0% -> 0% of each run, Pallas kernels for 41% -> 41%
where the time goes in v6:
time: 73 us; the launch traced here: 72.9 us
  Pallas kernels  41.4 us (57%)
  starting transfers between devices  26.2 us (36%)
  waiting for transfers between devices  4.86 us (7%)
    pallas_call x14, Pallas kernels, call(): pl.pallas_call(kernel, out_shape=out_shapes, in_specs=specs or [VMEM] * l...  36.5 us
    ppermute x6, starting transfers between devices, ring_x(): return lax.ppermute(block, 'inner', route)  11 us
    ppermute x6, starting transfers between devices, ring_z(): return lax.ppermute(block, 'inner', route)  10.8 us
    pallas_call x1, Pallas kernels, add_far(): pl.pallas_call(functools.partial(tail_kernel, shifts), out_shape=sds(rows...  4.91 us
    ppermute x4, starting transfers between devices, swap_outer(): lax.ppermute(block, 'outer', [(o, o ^ bits) for o in range(2 * RING)])  4.31 us
    ppermute x4, waiting for transfers between devices, swap_outer(): lax.ppermute(block, 'outer', [(o, o ^ bits) for o in range(2 * RING)])  2.8 us
    ppermute x6, waiting for transfers between devices, ring_z(): return lax.ppermute(block, 'inner', route)  2.03 us
  transfers between devices with their start and end apart: 17, of which 4 were waited for; matrix products, arithmetic and copies ran while one was open for 0% of the time, Pallas kernels for 41%

profile of v6, /device:TPU:0, one launch (start us, length us, event | category | flops | bytes accessed | tf_op | source)
XLA Modules:
  0.0 72.9 jit_solution(14157793017356375099)
XLA Ops:
  0.0 5.6 %front.1 = (bf16[2048,256]{1,0:T(8,128)(2,1)S(1)}, bf16[256,2048]{1,0:T(8,128)(2,1)S(1)}, bf16[2048,2048]{1,0:T(8,128)(2,1)S(1)}, bf16[512,256]{1,0:T(8,128)(2,1...) custom-call(s32[1,2048]{1,0:T(1,128)} %order.1, s32[255]{0:T(256)} %ranks_hbm.3, ...), custom_call_target="tpu_custom_call" | custom-call | flops 2147483648 | bytes 1048576 | tf_op jit(solution)/shard_map/front/pallas_call | solution.py:64
  5.6 3.2 %collective-permute-start.1 = (bf16[512,256]{1,0:T(8,128)(2,1)S(1)}, bf16[512,256]{1,0:T(8,128)(2,1)S(1)}, u32[]{:S(2)}, u32[]{:S(2)}) collective-permute-start(bf16[512,256]{1,0:T(8,128)(2,1)S(1)} %get-tuple-element.79), channel_id=1, source_target_pairs={{0,2},{1,3},{2,0},{3,1},{4,6},{5,7},{6,4},{7,5},{8,10},{9,11},{10,... | collective-permute-start | bytes 786440 | tf_op jit(solution)/shard_map/ppermute | solution.py:550
  8.8 1.6 %coef.1 = (bf16[512,256]{1,0:T(8,128)(2,1)S(1)}, bf16[512,256]{1,0:T(8,128)(2,1)S(1)}, bf16[512,256]{1,0:T(8,128)(2,1)S(1)}, bf16[512,256]{1,0:T(8,128)(2,1)S(1)}) custom-call(s32[8,256]{1,0:T(8,128)S(1)} %get-tuple-element.68.limit, bf16[256,2048]{1,0:T(8,128)(2,1)S(1)} %get-tuple-element.69.basis_t, bf16[2048,2048]{1,0:T(8,128)(2,1)S(1)} %get-tuple-element.71.x.x_in, ...), custom_call_target="tpu_custom_call" | custom-call | flops 1073741824 | bytes 1048576 | tf_op jit(solution)/shard_map/coef/pallas_call | solution.py:64
  10.4 0.6 collective-permute-start
  11.0 2.7 %collective-permute-start.2 = (bf16[512,256]{1,0:T(8,128)(2,1)S(1)}, bf16[512,256]{1,0:T(8,128)(2,1)S(1)}, u32[]{:S(2)}, u32[]{:S(2)}) collective-permute-start(bf16[512,256]{1,0:T(8,128)(2,1)S(1)} %get-tuple-element.80), channel_id=1, source_target_pairs={{0,3},{1,0},{2,1},{3,2},{4,7},{5,4},{6,5},{7,6},{8,11},{9,8},{10,9... | collective-permute-start | bytes 786440 | tf_op jit(solution)/shard_map/ppermute | solution.py:550
  13.7 6.4 %move.1 = (bf16[2048,256]{1,0:T(8,128)(2,1)S(1)}, bf16[2048,2048]{1,0:T(8,128)(2,1)S(1)}, bf16[2048,2048]{1,0:T(8,128)(2,1)S(1)}, bf16[512,256]{1,0:T(8,128)(2,1...) custom-call(s32[8,256]{1,0:T(8,128)S(1)} %get-tuple-element.68.limit, ...), custom_call_target="tpu_custom_call", output_to_operand_aliasing={{1}: (7, {})} | custom-call | flops 8589934592 | bytes 1048576 | tf_op jit(solution)/shard_map/move/pallas_call | solution.py:64
  20.1 0.0 copy-start
  20.1 2.5 %near_0.1.near_in = f32[34816,128]{1,0:T(8,128)S(1)} custom-call(s32[1,2048]{1,0:T(1,128)S(1)} %get-tuple-element.82.order, bf16[2048,2048]{1,0:T(8,128)(2,1)S(1)} %get-tuple-element.83.d, bf16[2048,2048]{1,0:T(8,128)(2,1)S(1)} %get-tuple-element.84.x, f32[34816,128]{1,0:T(8,128)S(1)} %get-tuple-element.85.near_in), custom_call_target="tpu_custom_call", output_to_operand_aliasing={{}: (3, {})} | custom-call | flops 2147483648 | bytes 1048576 | tf_op jit(solution)/shard_map/near_0/pallas_call | solution.py:64
  22.6 0.0 collective-permute-done.1.u2
  22.6 0.0 collective-permute-done.u1
  22.6 0.0 collective-permute-done.2.u3
  22.7 0.5 quad_up.1
  23.2 0.1 collective-permute-start.13
  23.3 2.0 %collective-permute-start.3 = (bf16[128,256]{1,0:T(8,128)(2,1)S(1)}, bf16[128,256]{1,0:T(8,128)(2,1)S(1)}, u32[]{:S(2)}, u32[]{:S(2)}) collective-permute-start(bf16[128,256]{1,0:T(8,128)(2,1)S(1)} %get-tuple-element.96), channel_id=1, source_target_pairs={{0,4},{1,5},{2,6},{3,7},{4,8},{5,9},{6,10},{7,11},{8,12},{9,13},{1... | collective-permute-start | bytes 196616 | tf_op jit(solution)/shard_map/ppermute | solution.py:555
  25.3 3.6 %collective-permute-start.4 = (bf16[128,256]{1,0:T(8,128)(2,1)S(1)}, bf16[128,256]{1,0:T(8,128)(2,1)S(1)}, u32[]{:S(2)}, u32[]{:S(2)}) collective-permute-start(bf16[128,256]{1,0:T(8,128)(2,1)S(1)} %get-tuple-element.97), channel_id=1, source_target_pairs={{0,8},{1,9},{2,10},{3,11},{4,12},{5,13},{6,14},{7,15},{8,0},{9,1},... | collective-permute-start | bytes 196616 | tf_op jit(solution)/shard_map/ppermute | solution.py:555
  28.9 1.0 %collective-permute-start.5 = (bf16[128,256]{1,0:T(8,128)(2,1)S(1)}, bf16[128,256]{1,0:T(8,128)(2,1)S(1)}, u32[]{:S(2)}, u32[]{:S(2)}) collective-permute-start(bf16[128,256]{1,0:T(8,128)(2,1)S(1)} %get-tuple-element.98), channel_id=1, source_target_pairs={{0,12},{1,13},{2,14},{3,15},{4,0},{5,1},{6,2},{7,3},{8,4},{9,5},{1... | collective-permute-start | bytes 196616 | tf_op jit(solution)/shard_map/ppermute | solution.py:555
  29.9 2.5 %near_256.1.near_in = f32[34816,128]{1,0:T(8,128)S(1)} custom-call(s32[1,2048]{1,0:T(1,128)S(1)} %get-tuple-element.82.order, bf16[2048,2048]{1,0:T(8,128)(2,1)S(1)} %get-tuple-element.83.d, bf16[2048,2048]{1,0:T(8,128)(2,1)S(1)} %get-tuple-element.84.x, f32[34816,128]{1,0:T(8,128)S(1)} %near_0.1.near_in), custom_call_target="tpu_custom_call", output_to_operand_aliasing={{}: (3, {})} | custom-call | flops 2147483648 | bytes 1048576 | tf_op jit(solution)/shard_map/near_256/pallas_call | solution.py:64
  32.4 0.0 collective-permute-done.3.q1
  32.4 0.0 collective-permute-done.4.q2
  32.4 0.7 %collective-permute-done.5.q3 = bf16[128,256]{1,0:T(8,128)(2,1)S(1)} collective-permute-done((bf16[128,256]{1,0:T(8,128)(2,1)S(1)}, bf16[128,256]{1,0:T(8,128)(2,1)S(1)}, u32[]{:S(2)}, u32[]{:S(2)}) %collective-permute-start.5) | collective-permute-done | bytes 65568 | tf_op jit(solution)/shard_map/ppermute | solution.py:555
  33.1 0.5 group_up.1
  33.7 0.1 collective-permute-start.6
  33.8 1.4 %near_512.1.near_in = f32[34816,128]{1,0:T(8,128)S(1)} custom-call(s32[1,2048]{1,0:T(1,128)S(1)} %get-tuple-element.82.order, bf16[2048,2048]{1,0:T(8,128)(2,1)S(1)} %get-tuple-element.83.d, bf16[2048,2048]{1,0:T(8,128)(2,1)S(1)} %get-tuple-element.84.x, f32[34816,128]{1,0:T(8,128)S(1)} %near_256.1.near_in), custom_call_target="tpu_custom_call", output_to_operand_aliasing={{}: (3, {})} | custom-call | flops 1073741824 | bytes 1048576 | tf_op jit(solution)/shard_map/near_512/pallas_call | solution.py:64
  35.1 0.2 collective-permute-done.6.peer.peer4
  35.3 0.0 copy-start.1
  35.3 0.0 copy-start.3
  35.4 3.1 %collective-permute-start.9 = (bf16[128,256]{1,0:T(8,128)(2,1)S(1)}, bf16[128,256]{1,0:T(8,128)(2,1)S(1)}, u32[]{:S(2)}, u32[]{:S(2)}) collective-permute-start(bf16[128,256]{1,0:T(8,128)(2,1)S(1)} %five.1.y0), channel_id=1, source_target_pairs={{0,96},{16,112},{32,64},{48,80},{64,32},{80,48},{96,0},{112,16},{1... | collective-permute-start | bytes 196616 | tf_op jit(solution)/shard_map/ppermute | solution.py:563
  38.4 0.6 collective-permute-start.8
  39.1 0.5 collective-permute-start.7
  39.6 2.5 %near_640.1.near_in = f32[34816,128]{1,0:T(8,128)S(1)} custom-call(s32[1,2048]{1,0:T(1,128)S(1)} %get-tuple-element.82.order, bf16[2048,2048]{1,0:T(8,128)(2,1)S(1)} %get-tuple-element.83.d, bf16[2048,2048]{1,0:T(8,128)(2,1)S(1)} %get-tuple-element.84.x, f32[34816,128]{1,0:T(8,128)S(1)} %near_512.1.near_in), custom_call_target="tpu_custom_call", output_to_operand_aliasing={{}: (3, {})} | custom-call | flops 2147483648 | bytes 1048576 | tf_op jit(solution)/shard_map/near_640/pallas_call | solution.py:64
  42.1 2.6 %collective-permute-done.8.y2 = bf16[128,256]{1,0:T(8,128)(2,1)S(1)} collective-permute-done((bf16[128,256]{1,0:T(8,128)(2,1)S(1)}, bf16[128,256]{1,0:T(8,128)(2,1)S(1)}, u32[]{:S(2)}, u32[]{:S(2)}) %collective-permute-start.8) | collective-permute-done | bytes 65568 | tf_op jit(solution)/shard_map/ppermute | solution.py:563
  44.7 0.0 collective-permute-done.7.y1
  44.7 1.8 %top.1 = (bf16[128,256]{1,0:T(8,128)(2,1)S(1)}, bf16[128,256]{1,0:T(8,128)(2,1)S(1)}, bf16[128,256]{1,0:T(8,128)(2,1)S(1)}, bf16[128,256]{1,0:T(8,128)(2,1)S(1)}) custom-call(s32[256,256]{1,0:T(8,128)S(1)} %get-tuple-element.75.table, bf16[128,256]{1,0:T(8,128)(2,1)S(1)} %five.1.y0, bf16[128,256]{1,0:T(8,128)(2,1)S(1)} %collective-permute-done.7.y1, ...), custom_call_target="tpu_custom_call" | custom-call | flops 268435456 | bytes 1048576 | tf_op jit(solution)/shard_map/top/pallas_call | solution.py:64
  46.5 0.3 collective-permute-start.10
  46.9 3.4 %collective-permute-start.11 = (bf16[128,256]{1,0:T(8,128)(2,1)S(1)}, bf16[128,256]{1,0:T(8,128)(2,1)S(1)}, u32[]{:S(2)}, u32[]{:S(2)}) collective-permute-start(bf16[128,256]{1,0:T(8,128)(2,1)S(1)} %get-tuple-element.116), channel_id=1, source_target_pairs={{0,8},{1,9},{2,10},{3,11},{4,12},{5,13},{6,14},{7,15},{8,0},{9,1},... | collective-permute-start | bytes 196616 | tf_op jit(solution)/shard_map/ppermute | solution.py:555
  50.3 0.5 collective-permute-start.12
  50.8 2.5 %near_896.1.near_in = f32[34816,128]{1,0:T(8,128)S(1)} custom-call(s32[1,2048]{1,0:T(1,128)S(1)} %get-tuple-element.82.order, bf16[2048,2048]{1,0:T(8,128)(2,1)S(1)} %get-tuple-element.83.d, bf16[2048,2048]{1,0:T(8,128)(2,1)S(1)} %get-tuple-element.84.x, f32[34816,128]{1,0:T(8,128)S(1)} %near_640.1.near_in), custom_call_target="tpu_custom_call", output_to_operand_aliasing={{}: (3, {})} | custom-call | flops 2147483648 | bytes 1048576 | tf_op jit(solution)/shard_map/near_896/pallas_call | solution.py:64
  53.2 0.0 collective-permute-done.10.f1
  53.3 1.3 %collective-permute-done.12.f3 = bf16[128,256]{1,0:T(8,128)(2,1)S(1)} collective-permute-done((bf16[128,256]{1,0:T(8,128)(2,1)S(1)}, bf16[128,256]{1,0:T(8,128)(2,1)S(1)}, u32[]{:S(2)}, u32[]{:S(2)}) %collective-permute-start.12) | collective-permute-done | bytes 65568 | tf_op jit(solution)/shard_map/ppermute | solution.py:555
  54.5 0.0 collective-permute-done.13.sibling
  54.5 0.6 quad_down.1
  55.1 2.0 %collective-permute-start.14 = (bf16[512,256]{1,0:T(8,128)(2,1)S(1)}, bf16[512,256]{1,0:T(8,128)(2,1)S(1)}, u32[]{:S(2)}, u32[]{:S(2)}) collective-permute-start(bf16[512,256]{1,0:T(8,128)(2,1)S(1)} %get-tuple-element.128), channel_id=1, source_target_pairs={{0,1},{1,2},{2,3},{3,0},{4,5},{5,6},{6,7},{7,4},{8,9},{9,10},{10,1... | collective-permute-start | bytes 786440 | tf_op jit(solution)/shard_map/ppermute | solution.py:550
  57.2 1.3 %collective-permute-start.15 = (bf16[512,256]{1,0:T(8,128)(2,1)S(1)}, bf16[512,256]{1,0:T(8,128)(2,1)S(1)}, u32[]{:S(2)}, u32[]{:S(2)}) collective-permute-start(bf16[512,256]{1,0:T(8,128)(2,1)S(1)} %get-tuple-element.129), channel_id=1, source_target_pairs={{0,3},{1,0},{2,1},{3,2},{4,7},{5,4},{6,5},{7,6},{8,11},{9,8},{10,9... | collective-permute-start | bytes 786440 | tf_op jit(solution)/shard_map/ppermute | solution.py:550
  58.4 1.2 %collective-permute-start.16 = (bf16[512,256]{1,0:T(8,128)(2,1)S(1)}, bf16[512,256]{1,0:T(8,128)(2,1)S(1)}, u32[]{:S(2)}, u32[]{:S(2)}) collective-permute-start(bf16[512,256]{1,0:T(8,128)(2,1)S(1)} %get-tuple-element.130), channel_id=1, source_target_pairs={{0,2},{1,3},{2,0},{3,1},{4,6},{5,7},{6,4},{7,5},{8,10},{9,11},{10,... | collective-permute-start | bytes 786440 | tf_op jit(solution)/shard_map/ppermute | solution.py:550
  59.7 8.1 %near_1152.1.near = f32[34816,128]{1,0:T(8,128)S(1)} custom-call(s32[1,2048]{1,0:T(1,128)S(1)} %get-tuple-element.82.order, bf16[2048,2048]{1,0:T(8,128)(2,1)S(1)} %get-tuple-element.83.d, bf16[2048,2048]{1,0:T(8,128)(2,1)S(1)} %get-tuple-element.84.x, f32[34816,128]{1,0:T(8,128)S(1)} %near_896.1.near_in), custom_call_target="tpu_custom_call", output_to_operand_aliasing={{}: (3, {})} | custom-call | flops 7516192768 | bytes 1048576 | tf_op jit(solution)/shard_map/near_1152/pallas_call | solution.py:64
  67.8 0.0 collective-permute-done.14.refs_1_
  67.8 0.0 collective-permute-done.15.refs_2_
  67.8 4.9 %tail_0132.1 = bf16[2048,2048]{1,0:T(8,128)(2,1)} custom-call(s32[256,256]{1,0:T(8,128)S(1)} %get-tuple-element.75.table, bf16[2048,256]{1,0:T(8,128)(2,1)S(1)} %get-tuple-element.76.basis, bf16[2048,256]{1,0:T(8,128)(2,1)S(1)} %collective-permute-done.13.sibling, bf16[2,256,256]{2,1,0:T(8,128)(2,1)S(1)} %bitcast.9, f32[34816,128]{1,0:T(8,128)S(1)} %near_1152.1.near, ...), custom_call_target="tpu_custom_call" | custom-call | flops 536870912 | bytes 3145728 | tf_op jit(solution)/shard_map/tail_0132/pallas_call | solution.py:532
  (11 shorter events, 0.1 us)
Async XLA Ops:
  0.0 13.7 %copy-start.4 = (s32[1,2048]{1,0:T(1,128)S(1)}, s32[1,2048]{1,0:T(1,128)}, u32[]{:S(2)}) copy-start(s32[1,2048]{1,0:T(1,128)} %order.1) | copy-start | bytes 24580
  5.6 17.0 %collective-permute-start.1 = (bf16[512,256]{1,0:T(8,128)(2,1)S(1)}, bf16[512,256]{1,0:T(8,128)(2,1)S(1)}, u32[]{:S(2)}, u32[]{:S(2)}) collective-permute-start(bf16[512,256]{1,0:T(8,128)(2,1)S(1)} %get-tuple-element.79), channel_id=1, source_target_pairs={{0,2},{1,3},{2,0},{3,1},{4,6},{5,7},{6,4},{7,5},{8,10},{9,11},{10,... | collective-permute-start | bytes 786440 | tf_op jit(solution)/shard_map/ppermute | solution.py:550
  10.4 12.3 %collective-permute-start = (bf16[512,256]{1,0:T(8,128)(2,1)S(1)}, bf16[512,256]{1,0:T(8,128)(2,1)S(1)}, u32[]{:S(2)}, u32[]{:S(2)}) collective-permute-start(bf16[512,256]{1,0:T(8,128)(2,1)S(1)} %get-tuple-element.78), channel_id=1, source_target_pairs={{0,1},{1,2},{2,3},{3,0},{4,5},{5,6},{6,7},{7,4},{8,9},{9,10},{10,1... | collective-permute-start | bytes 786440 | tf_op jit(solution)/shard_map/ppermute | solution.py:550
  11.0 11.6 %collective-permute-start.2 = (bf16[512,256]{1,0:T(8,128)(2,1)S(1)}, bf16[512,256]{1,0:T(8,128)(2,1)S(1)}, u32[]{:S(2)}, u32[]{:S(2)}) collective-permute-start(bf16[512,256]{1,0:T(8,128)(2,1)S(1)} %get-tuple-element.80), channel_id=1, source_target_pairs={{0,3},{1,0},{2,1},{3,2},{4,7},{5,4},{6,5},{7,6},{8,11},{9,8},{10,9... | collective-permute-start | bytes 786440 | tf_op jit(solution)/shard_map/ppermute | solution.py:550
  20.1 2.5 %copy-start = (bf16[1,15,2,256,256]{4,3,2,1,0:T(8,128)(2,1)S(1)}, bf16[1,15,2,256,256]{4,3,2,1,0:T(8,128)(2,1)}, u32[]{:S(2)}) copy-start(bf16[1,15,2,256,256]{4,3,2,1,0:T(8,128)(2,1)} %param.14) | copy-start | bytes 11796484
  23.2 31.3 %collective-permute-start.13 = (bf16[2048,256]{1,0:T(8,128)(2,1)S(1)}, bf16[2048,256]{1,0:T(8,128)(2,1)S(1)}, u32[]{:S(2)}, u32[]{:S(2)}) collective-permute-start(bf16[2048,256]{1,0:T(8,128)(2,1)S(1)} %get-tuple-element.119), channel_id=1, source_target_pairs={{0,1},{1,0},{2,3},{3,2},{4,5},{5,4},{6,7},{7,6},{8,9},{9,8},{10,11... | collective-permute-start | bytes 3145736 | tf_op jit(solution)/shard_map/ppermute | solution.py:559
  23.3 9.1 %collective-permute-start.3 = (bf16[128,256]{1,0:T(8,128)(2,1)S(1)}, bf16[128,256]{1,0:T(8,128)(2,1)S(1)}, u32[]{:S(2)}, u32[]{:S(2)}) collective-permute-start(bf16[128,256]{1,0:T(8,128)(2,1)S(1)} %get-tuple-element.96), channel_id=1, source_target_pairs={{0,4},{1,5},{2,6},{3,7},{4,8},{5,9},{6,10},{7,11},{8,12},{9,13},{1... | collective-permute-start | bytes 196616 | tf_op jit(solution)/shard_map/ppermute | solution.py:555
  25.3 7.1 %collective-permute-start.4 = (bf16[128,256]{1,0:T(8,128)(2,1)S(1)}, bf16[128,256]{1,0:T(8,128)(2,1)S(1)}, u32[]{:S(2)}, u32[]{:S(2)}) collective-permute-start(bf16[128,256]{1,0:T(8,128)(2,1)S(1)} %get-tuple-element.97), channel_id=1, source_target_pairs={{0,8},{1,9},{2,10},{3,11},{4,12},{5,13},{6,14},{7,15},{8,0},{9,1},... | collective-permute-start | bytes 196616 | tf_op jit(solution)/shard_map/ppermute | solution.py:555
  28.9 4.3 %collective-permute-start.5 = (bf16[128,256]{1,0:T(8,128)(2,1)S(1)}, bf16[128,256]{1,0:T(8,128)(2,1)S(1)}, u32[]{:S(2)}, u32[]{:S(2)}) collective-permute-start(bf16[128,256]{1,0:T(8,128)(2,1)S(1)} %get-tuple-element.98), channel_id=1, source_target_pairs={{0,12},{1,13},{2,14},{3,15},{4,0},{5,1},{6,2},{7,3},{8,4},{9,5},{1... | collective-permute-start | bytes 196616 | tf_op jit(solution)/shard_map/ppermute | solution.py:555
  33.7 1.6 %collective-permute-start.6 = (f32[2,128,256]{2,1,0:T(8,128)S(1)}, f32[2,128,256]{2,1,0:T(8,128)S(1)}, u32[]{:S(2)}, u32[]{:S(2)}) collective-permute-start(f32[2,128,256]{2,1,0:T(8,128)S(1)} %get-tuple-element.104.own), channel_id=1, source_target_pairs={{0,16},{16,0},{32,48},{48,32},{64,80},{80,64},{96,112},{112,96},{1... | collective-permute-start | bytes 786440 | tf_op jit(solution)/shard_map/ppermute | solution.py:563
  35.3 9.4 %copy-start.1 = (bf16[6,2,256,256]{3,2,1,0:T(8,128)(2,1)S(1)}, bf16[6,2,256,256]{3,2,1,0:T(8,128)(2,1)}, u32[]{:S(2)}) copy-start(bf16[6,2,256,256]{3,2,1,0:T(8,128)(2,1)} %outer.1) | copy-start | bytes 4718596
  35.3 9.4 %copy-start.3 = (bf16[256,256]{1,0:T(8,128)(2,1)S(1)}, bf16[256,256]{1,0:T(8,128)(2,1)}, u32[]{:S(2)}) copy-start(bf16[256,256]{1,0:T(8,128)(2,1)} %root.1) | copy-start | bytes 393220
  35.4 6.7 %collective-permute-start.9 = (bf16[128,256]{1,0:T(8,128)(2,1)S(1)}, bf16[128,256]{1,0:T(8,128)(2,1)S(1)}, u32[]{:S(2)}, u32[]{:S(2)}) collective-permute-start(bf16[128,256]{1,0:T(8,128)(2,1)S(1)} %five.1.y0), channel_id=1, source_target_pairs={{0,96},{16,112},{32,64},{48,80},{64,32},{80,48},{96,0},{112,16},{1... | collective-permute-start | bytes 196616 | tf_op jit(solution)/shard_map/ppermute | solution.py:563
  38.4 6.3 %collective-permute-start.8 = (bf16[128,256]{1,0:T(8,128)(2,1)S(1)}, bf16[128,256]{1,0:T(8,128)(2,1)S(1)}, u32[]{:S(2)}, u32[]{:S(2)}) collective-permute-start(bf16[128,256]{1,0:T(8,128)(2,1)S(1)} %five.1.y0), channel_id=1, source_target_pairs={{0,64},{16,80},{32,96},{48,112},{64,0},{80,16},{96,32},{112,48},{1... | collective-permute-start | bytes 196616 | tf_op jit(solution)/shard_map/ppermute | solution.py:563
  39.1 5.6 %collective-permute-start.7 = (bf16[128,256]{1,0:T(8,128)(2,1)S(1)}, bf16[128,256]{1,0:T(8,128)(2,1)S(1)}, u32[]{:S(2)}, u32[]{:S(2)}) collective-permute-start(bf16[128,256]{1,0:T(8,128)(2,1)S(1)} %five.1.y0), channel_id=1, source_target_pairs={{0,32},{16,48},{32,0},{48,16},{64,96},{80,112},{96,64},{112,80},{1... | collective-permute-start | bytes 196616 | tf_op jit(solution)/shard_map/ppermute | solution.py:563
  46.5 6.7 %collective-permute-start.10 = (bf16[128,256]{1,0:T(8,128)(2,1)S(1)}, bf16[128,256]{1,0:T(8,128)(2,1)S(1)}, u32[]{:S(2)}, u32[]{:S(2)}) collective-permute-start(bf16[128,256]{1,0:T(8,128)(2,1)S(1)} %get-tuple-element.115), channel_id=1, source_target_pairs={{0,4},{1,5},{2,6},{3,7},{4,8},{5,9},{6,10},{7,11},{8,12},{9,13},{1... | collective-permute-start | bytes 196616 | tf_op jit(solution)/shard_map/ppermute | solution.py:555
  46.9 6.4 %collective-permute-start.11 = (bf16[128,256]{1,0:T(8,128)(2,1)S(1)}, bf16[128,256]{1,0:T(8,128)(2,1)S(1)}, u32[]{:S(2)}, u32[]{:S(2)}) collective-permute-start(bf16[128,256]{1,0:T(8,128)(2,1)S(1)} %get-tuple-element.116), channel_id=1, source_target_pairs={{0,8},{1,9},{2,10},{3,11},{4,12},{5,13},{6,14},{7,15},{8,0},{9,1},... | collective-permute-start | bytes 196616 | tf_op jit(solution)/shard_map/ppermute | solution.py:555
  50.3 4.3 %collective-permute-start.12 = (bf16[128,256]{1,0:T(8,128)(2,1)S(1)}, bf16[128,256]{1,0:T(8,128)(2,1)S(1)}, u32[]{:S(2)}, u32[]{:S(2)}) collective-permute-start(bf16[128,256]{1,0:T(8,128)(2,1)S(1)} %get-tuple-element.117), channel_id=1, source_target_pairs={{0,12},{1,13},{2,14},{3,15},{4,0},{5,1},{6,2},{7,3},{8,4},{9,5},{1... | collective-permute-start | bytes 196616 | tf_op jit(solution)/shard_map/ppermute | solution.py:555
  55.1 12.7 %collective-permute-start.14 = (bf16[512,256]{1,0:T(8,128)(2,1)S(1)}, bf16[512,256]{1,0:T(8,128)(2,1)S(1)}, u32[]{:S(2)}, u32[]{:S(2)}) collective-permute-start(bf16[512,256]{1,0:T(8,128)(2,1)S(1)} %get-tuple-element.128), channel_id=1, source_target_pairs={{0,1},{1,2},{2,3},{3,0},{4,5},{5,6},{6,7},{7,4},{8,9},{9,10},{10,1... | collective-permute-start | bytes 786440 | tf_op jit(solution)/shard_map/ppermute | solution.py:550
  57.2 10.7 %collective-permute-start.15 = (bf16[512,256]{1,0:T(8,128)(2,1)S(1)}, bf16[512,256]{1,0:T(8,128)(2,1)S(1)}, u32[]{:S(2)}, u32[]{:S(2)}) collective-permute-start(bf16[512,256]{1,0:T(8,128)(2,1)S(1)} %get-tuple-element.129), channel_id=1, source_target_pairs={{0,3},{1,0},{2,1},{3,2},{4,7},{5,4},{6,5},{7,6},{8,11},{9,8},{10,9... | collective-permute-start | bytes 786440 | tf_op jit(solution)/shard_map/ppermute | solution.py:550
  58.4 9.4 %copy-start.2 = (bf16[1,2,256,256]{3,2,1,0:T(8,128)(2,1)S(1)}, bf16[1,2,256,256]{3,2,1,0:T(8,128)(2,1)}, u32[]{:S(2)}) copy-start(bf16[1,2,256,256]{3,2,1,0:T(8,128)(2,1)} %param.13) | copy-start | bytes 786436
  58.4 9.4 %collective-permute-start.16 = (bf16[512,256]{1,0:T(8,128)(2,1)S(1)}, bf16[512,256]{1,0:T(8,128)(2,1)S(1)}, u32[]{:S(2)}, u32[]{:S(2)}) collective-permute-start(bf16[512,256]{1,0:T(8,128)(2,1)S(1)} %get-tuple-element.130), channel_id=1, source_target_pairs={{0,2},{1,3},{2,0},{3,1},{4,6},{5,7},{6,4},{7,5},{8,10},{9,11},{10,... | collective-permute-start | bytes 786440 | tf_op jit(solution)/shard_map/ppermute | solution.py:550
